TPU v7x, 32 devices: a whole 2x2x4 slice. The times are simulated.
32 devices in a mesh: sub: 8 (over z, x), inner: 4 (over y, core).
Axes of the slice: x: 2, y: 2, z: 4, core: 2. Of those that a mesh axis runs over, the one named last changes fastest.
Arguments:
- operator_tiles: float32 [128, 27, 64, 64], P(('sub', 'inner')), may hold values from -0.15625 to 0.15625
- operator_cols: int32 [128, 27], P(('sub', 'inner')), may hold values from 0 to 11, as said below
- operator_count: int32 [128], P(('sub', 'inner')), may hold values from 13 to 27
- prolong_tiles: float32 [128, 3, 64, 64], P(('sub', 'inner')), may hold values from -0.75 to 0.75
- prolong_cols: int32 [128, 3], P(('sub', 'inner')), may hold values from 0 to 31, as said below
- prolong_count: int32 [128], P(('sub', 'inner')), may hold values from 1 to 3
- fetch_rows: int32 [64, 1], P(('sub', 'inner')), may hold values from 0 to 3, as said below
Outputs:
- coarse_matrix: float32 [32, 12, 64, 64], P('sub')
Inputs may be any that keep to these rules, and one draw needn't show every extreme that they name: `operator_cols`: each entry is a local block row (below 4) or a ghost slot; slot 4 + j + p is position p of the upward list of inner device j of the group below, slot 4 + (4 + j) + p position p of the downward list of inner device j of the group above; only existing groups are named. Entry 0 of each row is the row itself. `fetch_rows`: row 2 d lists the distinct local rows that device d sends to the group below, starting with row 0; row 2 d + 1 those it sends to the group above, starting with row 3. `prolong_cols`: A block row of group s names distinct coarse blocks of its own group, s * 4 to (s + 1) * 4 - 1.
All inputs are finite; a program needn't handle non-finite values.
Results may differ from a plain program's by a relative error of at most 0.0003.
Values sent between devices are 32-bit elements; how exact they have to be, the bound alone decides.
No kernel may reach another device: no remote copies, remote signals or barrier semaphores. Data moves between devices by JAX's collectives and lax.ppermute only.
A program may use at most 64 MiB of HBM per device.

v0:
```python
import jax
import jax.numpy as jnp
from jax import lax
from jax.sharding import PartitionSpec as P

CG = 4


def with_halo(cells, sides, width):
    for axis, dim in sides:
        count = lax.axis_size(axis)
        ends = count - 1
        head = lax.slice_in_dim(cells, 0, width, axis=dim)
        tail = lax.slice_in_dim(cells, cells.shape[dim] - width, cells.shape[dim], axis=dim)
        cells = jnp.concatenate(
            [
                lax.ppermute(tail, axis, [(i, (i + 1) % count) for i in range(ends)]),
                cells,
                lax.ppermute(head, axis, [((i + 1) % count, i) for i in range(ends)]),
            ],
            axis=dim,
        )
    return cells


def per_device(
    operator_tiles,
    operator_cols,
    operator_count,
    prolong_tiles,
    prolong_cols,
    prolong_count,
    fetch_rows,
):
    row_count = operator_tiles.shape[0]
    entry_count = operator_tiles.shape[1]
    tile_count = prolong_tiles.shape[1]
    tile_size = operator_tiles.shape[2]
    sub_index = lax.axis_index("sub")
    tile_keep = (jnp.arange(tile_count, dtype=jnp.int32)[None, :] < prolong_count[:, None]).astype(
        jnp.float32
    )
    local_cols = prolong_cols - sub_index * CG
    placed = (local_cols[:, :, None] == jnp.arange(CG, dtype=jnp.int32)[None, None, :]).astype(
        jnp.float32
    )
    placed = placed * tile_keep[:, :, None]
    dense_rows = jnp.einsum(
        "img,imbc->igbc", placed, prolong_tiles, precision=lax.Precision.HIGHEST
    )
    outgoing = dense_rows[fetch_rows]
    grouped = lax.all_gather(outgoing, "inner", axis=1, tiled=True)
    rimmed = with_halo(grouped, (("sub", 0),), 1)
    ghosts = jnp.concatenate([rimmed[0], rimmed[3]], axis=0)
    extended = jnp.concatenate([dense_rows, ghosts], axis=0)
    ghost_count = ghosts.shape[0]
    half_ghost = ghost_count // 2
    slot_total = row_count + ghost_count
    live_mask = (
        jnp.arange(entry_count, dtype=jnp.int32)[None, :] < operator_count[:, None]
    ).astype(jnp.float32)
    slot_hits = (
        operator_cols[:, :, None] == jnp.arange(slot_total, dtype=jnp.int32)[None, None, :]
    ).astype(jnp.float32)
    slot_hits = slot_hits * live_mask[:, :, None]
    dense_operator = jnp.einsum(
        "iks,ikbc->isbc", slot_hits, operator_tiles, precision=lax.Precision.HIGHEST
    )
    below_part = jnp.einsum(
        "isbc,sgcd->igbd",
        dense_operator[:, row_count : row_count + half_ghost],
        extended[row_count : row_count + half_ghost],
        precision=lax.Precision.HIGHEST,
    )
    local_part = jnp.einsum(
        "isbc,sgcd->igbd",
        dense_operator[:, :row_count],
        extended[:row_count],
        precision=lax.Precision.HIGHEST,
    )
    above_part = jnp.einsum(
        "isbc,sgcd->igbd",
        dense_operator[:, row_count + half_ghost :],
        extended[row_count + half_ghost :],
        precision=lax.Precision.HIGHEST,
    )
    applied = jnp.stack([below_part, local_part, above_part], axis=1)
    partial_value = jnp.einsum(
        "igcb,iqhcd->gqhbd", dense_rows, applied, precision=lax.Precision.HIGHEST
    )
    shared = lax.psum_scatter(partial_value, "inner", scatter_dimension=3, tiled=True)
    gathered = lax.all_gather(shared, "inner", axis=3, tiled=True)
    return gathered.reshape(CG, 3 * CG, tile_size, tile_size)


def solution(mesh):
    placed = (
        P(("sub", "inner"), None, None, None),
        P(("sub", "inner"), None),
        P(("sub", "inner")),
        P(("sub", "inner"), None, None, None),
        P(("sub", "inner"), None),
        P(("sub", "inner")),
        P(("sub", "inner"), None),
    )
    return jax.shard_map(
        per_device,
        mesh=mesh,
        in_specs=placed,
        out_specs=P("sub", None, None, None),
        check_vma=False,
    )
```

profile of v0, /device:TPU:3, one launch (start us, length us, event | category | flops | bytes accessed | tf_op | source)
XLA Modules:
  0.0 129.8 jit_solution(13036377619152348000)
XLA Ops:
  6.5 0.0 all-reduce.3.cloned.1.call-start
  6.5 0.9 fusion.30
  7.4 0.9 fusion.32
  8.3 0.7 broadcast_subtract_fusion
  9.0 2.9 %fusion.18 = f32[4,4,64,64]{3,1,2,0:T(4,128)} fusion(f32[4,3,64,64]{3,2,1,0:T(8,128)} %param.10, f32[4,3]{1,0:T(4,128)S(1)} %fusion.30, s32[4,3]{1,0:T(4,128)S(1)} %broadcast_subtract_fusion), kind=kOutput, calls=%fused_computation.23 | convolution fusion | flops 2359392 | bytes 458848 | tf_op jit(solution)/shard_map/img,imbc->igbc/dot_general | solution.py:48
  11.9 2.4 %gather_fusion = f32[2,4,64,64]{3,1,2,0:T(4,128)} fusion(f32[4,4,64,64]{3,1,2,0:T(4,128)} %fusion.18, s32[1024]{0:T(1024)S(1)} %pad_clamp_fusion), kind=kCustom, calls=%fused_computation | custom fusion | bytes 262152 | tf_op jit(solution)/shard_map/gather | solution.py:51
  14.3 1.0 copy.29
  15.3 10.6 %all-gather = f32[2,16,64,64]{3,2,0,1:T(8,128)S(1)} all-gather(f32[2,4,64,64]{3,2,0,1:T(8,128)S(1)} %copy.29), channel_id=2, replica_groups=mesh['sub'=8,'inner'=4] {'inner'}, dimensions={1}, use_global_device_ids=true | all-gather | bytes 655360 | tf_op jit(solution)/shard_map/all_gather | solution.py:52
  25.9 1.1 fusion.37
  27.0 2.0 %copy.37 = f32[1,4,4,64,64]{3,4,1,2,0:T(8,128)} copy(f32[1,4,4,64,64]{4,3,2,1,0:T(8,128)} %bitcast.79) | data formatting | bytes 524288 | tf_op jit(solution)/shard_map/slice | solution.py:13
  29.0 2.2 %collective-permute-start.1 = (f32[1,4,4,64,64]{3,4,1,2,0:T(8,128)}, f32[1,4,4,64,64]{3,4,1,2,0:T(8,128)}, u32[]{:S(2)}, u32[]{:S(2)}) collective-permute-start(f32[1,4,4,64,64]{3,4,1,2,0:T(8,128)} %copy.37), channel_id=1, source_target_pairs={{4,0},{8,4},{12,8},{16,12},{20,16},{24,20},{28,24},{5,1},{9,5},{13... | collective-permute-start | bytes 786440 | tf_op jit(solution)/shard_map/ppermute | solution.py:19
  31.2 2.0 %copy.31 = f32[1,4,4,64,64]{3,4,1,2,0:T(8,128)} copy(f32[1,4,4,64,64]{4,3,2,1,0:T(8,128)} %bitcast.78) | data formatting | bytes 524288 | tf_op jit(solution)/shard_map/slice | solution.py:14
  33.2 4.2 %collective-permute-start = (f32[1,4,4,64,64]{3,4,1,2,0:T(8,128)}, f32[1,4,4,64,64]{3,4,1,2,0:T(8,128)S(1)}, u32[]{:S(2)}, u32[]{:S(2)}) collective-permute-start(f32[1,4,4,64,64]{3,4,1,2,0:T(8,128)} %copy.31), channel_id=1, source_target_pairs={{0,4},{4,8},{8,12},{12,16},{16,20},{20,24},{24,28},{1,5},{5,9},{9,... | collective-permute-start | bytes 786440 | tf_op jit(solution)/shard_map/ppermute | solution.py:17
  37.4 0.1 fusion.31
  37.5 4.0 %fusion = f32[4,12,64,64]{3,1,2,0:T(8,128)S(1)} fusion(f32[4,27,64,64]{3,2,1,0:T(8,128)S(1)} %copy-done, f32[4,27]{1,0:T(4,128)S(1)} %fusion.31, s32[4,27]{1,0:T(4,128)S(1)} %copy-done.2), kind=kOutput, calls=%fused_computation.1 | convolution fusion | flops 63703584 | bytes 2556768 | tf_op jit(solution)/shard_map/iks,ikbc->isbc/dot_general | solution.py:66
  41.5 0.0 copy-start.1
  41.5 0.3 fusion.36
  41.8 0.8 copy-done.1
  42.6 1.9 %convolution_bitcast_fusion.1 = f32[4,1,4,64,64]{3,4,0,2,1:T(8,128)S(1)} fusion(f32[4,4,64,64,1]{3,1,2,0,4:T(4,128)S(1)} %bitcast.76, f32[4,4,64,64]{3,1,2,0:T(4,128)S(1)} %get-tuple-element.7), kind=kOutput, calls=%fused_computation.11 | convolution fusion | flops 201326592 | bytes 786432 | tf_op jit(solution)/shard_map/isbc,sgcd->igbd/dot_general | solution.py:75
  44.4 1.1 collective-permute-done.1
  45.5 2.1 %convolution_bitcast_fusion = f32[4,1,4,64,64]{3,4,0,2,1:T(8,128)S(1)} fusion(f32[1,4,4,64,64]{3,4,1,2,0:T(8,128)} %collective-permute-done.1, f32[4,4,64,64]{3,1,2,0:T(4,128)S(1)} %get-tuple-element.6), kind=kOutput, calls=%fused_computation.10 | convolution fusion | flops 201326592 | bytes 786432 | tf_op jit(solution)/shard_map/isbc,sgcd->igbd/dot_general | solution.py:81
  47.6 9.5 %collective-permute-done = f32[1,4,4,64,64]{3,4,1,2,0:T(8,128)S(1)} collective-permute-done((f32[1,4,4,64,64]{3,4,1,2,0:T(8,128)}, f32[1,4,4,64,64]{3,4,1,2,0:T(8,128)S(1)}, u32[]{:S(2)}, u32[]{:S(2)}) %collective-permute-start) | collective-permute-done | bytes 262176 | tf_op jit(solution)/shard_map/ppermute | solution.py:17
  57.1 1.0 convolution_bitcast_fusion.2
  58.1 2.7 %fusion.7 = f32[4,3,4,64,64]{3,4,0,2,1:T(8,128)} fusion(f32[4,1,4,64,64]{3,4,0,2,1:T(8,128)S(1)} %convolution_bitcast_fusion, f32[4,1,4,64,64]{3,4,0,2,1:T(8,128)S(1)} %convolution_bitcast_fusion.1, f32[4,1,4,64,64]{3,4,0,2,1:T(8,128)S(1)} %convolution_bitcast_fusion.2, f32[4,4,64,64,1,1]{3,1,2,0,5,4:T(4,128)S(1)} %bitcast.77), kind=kOutput, calls=%fused_computation.9 | convolution fusion | flops 604372992 | bytes 1835008 | tf_op jit(solution)/shard_map/igcb,iqhcd->gqhbd/dot_general | solution.py:88
  60.8 2.6 %copy.40 = f32[4,3,4,64,64]{4,2,1,0,3:T(4,128)} copy(f32[4,3,4,64,64]{3,4,0,2,1:T(8,128)} %fusion.7) | data formatting | bytes 1572864 | tf_op jit(solution)/shard_map/igcb,iqhcd->gqhbd/transpose | solution.py:88
  63.4 0.0 all-reduce.3.cloned.1.call-update
  63.4 0.6 copy-done.4
  64.1 0.6 dynamic-slice
  65.3 42.0 %all-reduce.3.cloned.1.call-done = f32[4,3,4,64,64]{4,2,1,0,3:T(4,128)} async-done(((f32[4,3,4,64,64]{4,2,1,0,3:T(4,128)}), f32[4,3,4,64,64]{4,2,1,0,3:T(4,128)}) %all-reduce.3.cloned.1.call-update) | async-done | bytes 786448
  107.3 1.0 constant_dynamic-slice_fusion
  108.3 13.0 %all_gather.7 = f32[4,3,4,64,64]{4,2,1,0,3:T(4,128)S(1)} all-gather(f32[4,3,4,16,64]{4,2,1,0,3:T(4,128)S(1)} %constant_dynamic-slice_fusion), channel_id=1, replica_groups=mesh['sub'=8,'inner'=4] {'inner'}, dimensions={3}, use_global_device_ids=true | all-gather | bytes 983040 | tf_op jit(solution)/shard_map/all_gather | solution.py:92
  121.3 1.6 %copy.41 = f32[4,3,4,64,64]{4,3,2,1,0:T(8,128)} copy(f32[4,3,4,64,64]{4,2,1,0,3:T(4,128)S(1)} %all_gather.7) | data formatting | bytes 1572864 | tf_op jit(solution)/shard_map/all_gather | solution.py:92
  (8 shorter events, 0.0 us)
Async XLA Ops:
  6.5 30.9 %copy-start = (f32[4,27,64,64]{3,2,1,0:T(8,128)S(1)}, f32[4,27,64,64]{3,2,1,0:T(8,128)}, u32[]{:S(2)}) copy-start(f32[4,27,64,64]{3,2,1,0:T(8,128)} %param.7) | copy-start | bytes 5308420
  6.5 100.7 %all-reduce.3.cloned.1.call-start = ((), (), s32[]{:S(2)}) async-start(), calls=%async_computation | async-start | bytes 3145728
  27.0 10.4 %copy-start.3 = (s32[4]{0:T(128)S(1)}, s32[4]{0:T(128)}, u32[]{:S(2)}) copy-start(s32[4]{0:T(128)} %param.9) | copy-start | bytes 52
  27.0 10.5 %copy-start.2 = (s32[4,27]{1,0:T(4,128)S(1)}, s32[4,27]{1,0:T(4,128)}, u32[]{:S(2)}) copy-start(s32[4,27]{1,0:T(4,128)} %param.8) | copy-start | bytes 1300
  29.0 16.5 %collective-permute-start.1 = (f32[1,4,4,64,64]{3,4,1,2,0:T(8,128)}, f32[1,4,4,64,64]{3,4,1,2,0:T(8,128)}, u32[]{:S(2)}, u32[]{:S(2)}) collective-permute-start(f32[1,4,4,64,64]{3,4,1,2,0:T(8,128)} %copy.37), channel_id=1, source_target_pairs={{4,0},{8,4},{12,8},{16,12},{20,16},{24,20},{28,24},{5,1},{9,5},{13... | collective-permute-start | bytes 786440 | tf_op jit(solution)/shard_map/ppermute | solution.py:19
  33.2 23.9 %collective-permute-start = (f32[1,4,4,64,64]{3,4,1,2,0:T(8,128)}, f32[1,4,4,64,64]{3,4,1,2,0:T(8,128)S(1)}, u32[]{:S(2)}, u32[]{:S(2)}) collective-permute-start(f32[1,4,4,64,64]{3,4,1,2,0:T(8,128)} %copy.31), channel_id=1, source_target_pairs={{0,4},{4,8},{8,12},{12,16},{16,20},{20,24},{24,28},{1,5},{5,9},{9,... | collective-permute-start | bytes 786440 | tf_op jit(solution)/shard_map/ppermute | solution.py:17
  41.5 1.0 copy-start.1
  63.4 0.7 copy-start.4
Sparse Core Ops, SparseCore 0:
  63.6 43.6 all-reduce.2
where the time goes:
time: 131 us; the launch traced here: 130 us
  waiting for transfers between devices  52.6 us (40%)
  blocking collectives  23.6 us (18%)
  local copies, waits for them, and re-layouts  16.1 us (12%)
  matrix products  14.6 us (11%)
  between operations  14.1 us (11%)
  starting transfers between devices  6.34 us (5%)
  other arithmetic  2.49 us (2%)
    unnamed x2, waiting for transfers between devices  42 us
    all_gather x1, blocking collectives, per_device(): gathered = lax.all_gather(shared, 'inner', axis=3, tiled=True)  13 us
    all_gather x1, blocking collectives, per_device(): grouped = lax.all_gather(outgoing, 'inner', axis=1, tiled=True)  10.6 us
    ppermute x1, waiting for transfers between devices, with_halo(): lax.ppermute(tail, axis, [(i, (i + 1) % count) for i in range(ends)])  9.5 us
    ppermute x1, starting transfers between devices, with_halo(): lax.ppermute(tail, axis, [(i, (i + 1) % count) for i in range(ends)])  4.19 us
    dot_general x1, matrix products, per_device(): jnp.einsum('iks,ikbc->isbc', slot_hits, operator_tiles, precision=lax.Pre...  4.03 us
    gather x2, local copies, waits for them, and re-layouts, per_device(): outgoing = dense_rows[fetch_rows]  3.39 us
    slice x2, local copies, waits for them, and re-layouts, with_halo(): lax.slice_in_dim(cells, cells.shape[dim] - width, cells.shape[dim], axis=...  3.13 us
  transfers between devices with their start and end apart: 3, of which 3 were waited for; matrix products, arithmetic and copies ran while one was open for 8% of the time, Pallas kernels for 0%

commit v1 on v0

v1 whole, which is shorter than its diff:
```python
import functools

import jax
import jax.numpy as jnp
from jax import lax
from jax.experimental import pallas as pl
from jax.experimental.pallas import tpu as pltpu
from jax.sharding import PartitionSpec as P

CG = 4
CORES = 2
VMEM_BYTES = 32 * 1024 * 1024


def halves(value):
    high = value.astype(jnp.bfloat16)
    low = (value - high.astype(jnp.float32)).astype(jnp.bfloat16)
    return high, low


def product(left, right):
    left_high, left_low = halves(left)
    right_high, right_low = halves(right)
    dot = functools.partial(jnp.dot, preferred_element_type=jnp.float32)
    return dot(left_high, right_high) + (dot(left_low, right_high) + dot(left_high, right_low))


def left_kernel(
    cols_ref,
    count_ref,
    prolong_cols_ref,
    prolong_count_ref,
    fetch_ref,
    place_ref,
    tiles_hbm,
    prolong_hbm,
    mine_ref,
    send_ref,
    straight_ref,
    crossed_ref,
    dense_ref,
    local_ref,
    tiles,
    prolong,
    slots,
    tile_sems,
    prolong_sem,
):
    rows, entries, size, _ = tiles.shape
    fetched = mine_ref.shape[1] // size
    prolong_copy = pltpu.make_async_copy(prolong_hbm, prolong, prolong_sem)
    prolong_copy.start()
    copies = [
        pltpu.make_async_copy(tiles_hbm.at[row], tiles.at[row], tile_sems.at[row])
        for row in range(rows)
    ]
    for copy in copies:
        copy.start()
    slots[...] = jnp.zeros_like(slots)
    first_coarse = place_ref[0] * CG
    core = place_ref[1]

    prolong_copy.wait()
    for row in range(rows):
        blocks = []
        for coarse in range(CG):
            block = None
            for m in range(prolong.shape[1]):
                hit = (prolong_cols_ref[row, m] == first_coarse + coarse) & (
                    m < prolong_count_ref[row]
                )
                term = prolong[row, m] * jnp.where(hit, 1.0, 0.0)
                block = term if block is None else block + term
            blocks.append(block)
        dense_ref[row * size : (row + 1) * size, :] = jnp.concatenate(blocks, axis=1)

    for target, ref in ((core, straight_ref), (1 - core, crossed_ref)):
        taken = pl.multiple_of(fetch_ref[1 - target, 0] * size, size)
        ref[...] = dense_ref[pl.ds(taken, size), :]

    for row in range(rows):
        copies[row].wait()
        for entry in range(entries):
            col = cols_ref[row, entry]
            ghost = col - rows
            above = ghost >= fetched
            within = jnp.where(above, ghost - fetched, ghost)
            is_mine = above == (core == 1)
            slot = jnp.where(col < rows, col, rows + jnp.where(is_mine, within, fetched + within))
            slot = jnp.where(entry < count_ref[row], slot, rows + 2 * fetched)
            slots[row, slot] += tiles[row, entry]

    def gathered(first, count):
        return jnp.concatenate(
            [
                jnp.concatenate([slots[row, first + j] for j in range(count)], axis=1)
                for row in range(rows)
            ],
            axis=0,
        )

    turned = dense_ref[...].T
    mine_ref[...] = product(turned, gathered(rows, fetched))
    send_ref[...] = product(turned, gathered(rows + fetched, fetched))
    local_ref[...] = gathered(0, rows)


def middle_kernel(place_ref, dense_ref, local_ref, mine_ref, send_ref, whole):
    core = place_ref[1]
    dense = dense_ref[...]
    whole[...] = product(product(dense.T, local_ref[...]), dense)
    half = mine_ref.shape[0]
    mine_ref[...] = whole[pl.ds(pl.multiple_of(core * half, half), half), :]
    send_ref[...] = whole[pl.ds(pl.multiple_of((1 - core) * half, half), half), :]


def window_kernel(place_ref, held_ref, came_ref, *refs):
    ghosts, result_ref, prolong = refs[:-2], refs[-2], refs[-1]
    core, chip = place_ref[1], place_ref[2]
    size = ghosts[0].shape[0]
    chips = len(ghosts) // CORES
    for index, ghost in enumerate(ghosts):
        shift, cross = divmod(index, CORES)
        source = lax.rem(chip + shift, chips) * CORES + lax.rem(core + cross, CORES)
        prolong[pl.ds(pl.multiple_of(source * size, size), size), :] = ghost[...]
    result_ref[...] = product(held_ref[...] + came_ref[...], prolong[...])


def write_blocks(out_ref, first, value):
    size = out_ref.shape[-1]
    for g in range(value.shape[0] // size):
        for h in range(value.shape[1] // size):
            out_ref[g, first + h] = value[g * size : (g + 1) * size, h * size : (h + 1) * size]


def outer_kernel(place_ref, own_ref, other_ref, out_ref):
    core = place_ref[1]
    write_blocks(out_ref, 2 * CG * core, own_ref[...])
    write_blocks(out_ref, 2 * CG * (1 - core), other_ref[...])


def inner_kernel(place_ref, held_ref, came_ref, far_held_ref, far_came_ref, _, out_ref, whole):
    core = place_ref[1]
    half = held_ref.shape[0]
    whole[pl.ds(pl.multiple_of(core * half, half), half), :] = held_ref[...] + came_ref[...]
    whole[pl.ds(pl.multiple_of((1 - core) * half, half), half), :] = (
        far_held_ref[...] + far_came_ref[...]
    )
    write_blocks(out_ref, 0, whole[...])


SMEM = pl.BlockSpec(memory_space=pltpu.SMEM)
VMEM = pl.BlockSpec(memory_space=pltpu.VMEM)
ANY = pl.BlockSpec(memory_space=pl.ANY)
PARAMS = pltpu.CompilerParams(vmem_limit_bytes=VMEM_BYTES)


def f32(*shape):
    return jax.ShapeDtypeStruct(shape, jnp.float32)


def per_device(
    operator_tiles,
    operator_cols,
    operator_count,
    prolong_tiles,
    prolong_cols,
    prolong_count,
    fetch_rows,
):
    rows, entries, size, _ = operator_tiles.shape
    subs, fetched = lax.axis_size("sub"), lax.axis_size("inner")
    chips = fetched // CORES
    width = CG * size
    position = lax.axis_index("inner")
    place = jnp.stack(
        [lax.axis_index("sub"), lax.rem(position, CORES), lax.div(position, CORES)]
    ).astype(jnp.int32)

    held, send, straight, crossed, dense, local = pl.pallas_call(
        left_kernel,
        out_shape=[
            f32(width, fetched * size),
            f32(width, fetched * size),
            f32(size, width),
            f32(size, width),
            f32(rows * size, width),
            f32(rows * size, rows * size),
        ],
        in_specs=[SMEM] * 6 + [ANY] * 2,
        out_specs=[VMEM] * 6,
        scratch_shapes=[
            pltpu.VMEM(operator_tiles.shape, jnp.float32),
            pltpu.VMEM(prolong_tiles.shape, jnp.float32),
            pltpu.VMEM((rows, rows + 2 * fetched + 1, size, size), jnp.float32),
            pltpu.SemaphoreType.DMA((rows,)),
            pltpu.SemaphoreType.DMA,
        ],
        compiler_params=PARAMS,
        name="left",
    )(
        operator_cols,
        operator_count,
        prolong_cols,
        prolong_count,
        fetch_rows,
        place,
        operator_tiles,
        prolong_tiles,
    )

    swap_cores = [(i, i ^ 1) for i in range(fetched)]
    both = ("sub", "inner")

    def other_core(value):
        return lax.ppermute(value, "inner", swap_cores)

    def chip_sum(value):
        step = 1
        while step < chips:
            came = lax.ppermute(
                value, "inner", [(i, i ^ (step * CORES)) for i in range(fetched)]
            )
            step *= 2
            if step < chips:
                value = value + came
        return value, came

    ghosts = []
    for shift in range(chips):
        for cross in range(CORES):
            pairs = []
            for sub in range(subs):
                for chip in range(chips):
                    for core in range(CORES):
                        source_sub = sub - 1 if core == 0 else sub + 1
                        if 0 <= source_sub < subs:
                            source = (chip + shift) % chips * CORES + (core + cross) % CORES
                            pairs.append(
                                (source_sub * fetched + source, sub * fetched + chip * CORES + core)
                            )
            ghosts.append(lax.ppermute(crossed if cross else straight, both, pairs))

    middle_held, middle_send = pl.pallas_call(
        middle_kernel,
        out_shape=[f32(width // CORES, width)] * 2,
        in_specs=[SMEM, VMEM, VMEM],
        out_specs=[VMEM] * 2,
        scratch_shapes=[pltpu.VMEM((width, width), jnp.float32)],
        compiler_params=PARAMS,
        name="middle",
    )(place, dense, local)

    held, came = chip_sum(held + other_core(send))
    middle_held, middle_came = chip_sum(middle_held + other_core(middle_send))

    window = pl.pallas_call(
        window_kernel,
        out_shape=f32(width, width),
        in_specs=[SMEM] + [VMEM] * (2 + len(ghosts)),
        out_specs=VMEM,
        scratch_shapes=[pltpu.VMEM((fetched * size, width), jnp.float32)],
        compiler_params=PARAMS,
        name="window",
    )(place, held, came, *ghosts)

    out_shape = f32(CG, 3 * CG, size, size)
    outer = pl.pallas_call(
        outer_kernel,
        out_shape=out_shape,
        in_specs=[SMEM] + [VMEM] * 2,
        out_specs=VMEM,
        compiler_params=PARAMS,
        name="outer",
    )(place, window, other_core(window))

    def whole_block(*shape):
        return pl.BlockSpec(shape, lambda step: (0,) * len(shape))

    half_block = whole_block(width // CORES, width)
    return pl.pallas_call(
        inner_kernel,
        grid=(1,),
        out_shape=out_shape,
        in_specs=[SMEM] + [half_block] * 4 + [ANY],
        out_specs=pl.BlockSpec((CG, CG, size, size), lambda step: (0, 1, 0, 0)),
        scratch_shapes=[pltpu.VMEM((width, width), jnp.float32)],
        input_output_aliases={5: 0},
        compiler_params=PARAMS,
        name="inner",
    )(
        place,
        middle_held,
        middle_came,
        other_core(middle_held),
        other_core(middle_came),
        outer,
    )


def solution(mesh):
    placed = (
        P(("sub", "inner"), None, None, None),
        P(("sub", "inner"), None),
        P(("sub", "inner")),
        P(("sub", "inner"), None, None, None),
        P(("sub", "inner"), None),
        P(("sub", "inner")),
        P(("sub", "inner"), None),
    )
    return jax.shard_map(
        per_device,
        mesh=mesh,
        in_specs=placed,
        out_specs=P("sub", None, None, None),
        check_vma=False,
    )
```

time: 131 us -> 42.9 us (0.33)
  waiting for transfers between devices: 52.6 us -> 9.17 us
  blocking collectives: 23.6 us -> 0 us
  matrix products: 14.6 us -> 0 us
  between operations: 14.1 us -> 0.11 us
  starting transfers between devices: 6.34 us -> 18.1 us
  local copies, waits for them, and re-layouts: 16.1 us -> 6.41 us
  Pallas kernels: 0 us -> 8.63 us
  other arithmetic: 2.49 us -> 0.13 us
    unnamed x2 -> x0, waiting for transfers between devices: 42 us -> none
    all_gather x2 -> x0, blocking collectives: 23.6 us -> none  [the longest x1 13 us: per_device(): gathered = lax.all_gather(shared, 'inner', axis=3, tiled=True)]
    dot_general x6 -> x0, matrix products: 14.6 us -> none  [the longest x1 4.03 us: per_device(): jnp.einsum('iks,ikbc->isbc', slot_hits, operator_tiles, precision=lax.Pre...]
    ppermute x2 -> x11, starting transfers between devices: 6.34 us -> 18.1 us  [the longest x4 11.4 us: per_device(): ghosts.append(lax.ppermute(crossed if cross else straight, both, pairs))]
    pallas_call x0 -> x5, Pallas kernels: none -> 8.63 us  [the longest x1 3.2 us: per_device(): pl.pallas_call(left_kernel, out_shape=[f32(width, fetched * size), f32(wi...]
    slice x4 -> x0, local copies, waits for them, and re-layouts: 5.42 us -> none  [the longest x2 3.13 us: with_halo(): lax.slice_in_dim(cells, cells.shape[dim] - width, cells.shape[dim], axis=...]
    gather x2 -> x0, local copies, waits for them, and re-layouts: 3.39 us -> none  [per_device(): outgoing = dense_rows[fetch_rows]]
    unnamed x12 -> x13, local copies, waits for them, and re-layouts: 3.03 us -> 6.41 us
  transfers between devices with their start and end apart: 3 -> 11, of which waited for: 3 -> 3; matrix products, arithmetic and copies ran while one was open for 8% -> 0% of each run, Pallas kernels for 0% -> 9%
where the time goes in v1:
time: 42.9 us; the launch traced here: 42.5 us
  starting transfers between devices  18.1 us (42%)
  waiting for transfers between devices  9.17 us (21%)
  Pallas kernels  8.63 us (20%)
  local copies, waits for them, and re-layouts  6.41 us (15%)
    ppermute x4, starting transfers between devices, per_device(): ghosts.append(lax.ppermute(crossed if cross else straight, both, pairs))  11.4 us
    unnamed x13, local copies, waits for them, and re-layouts  6.41 us
    ppermute x5, starting transfers between devices, other_core(): return lax.ppermute(value, 'inner', swap_cores)  5.12 us
    ppermute x4, waiting for transfers between devices, per_device(): ghosts.append(lax.ppermute(crossed if cross else straight, both, pairs))  4.4 us
    ppermute x2, waiting for transfers between devices, chip_sum(): lax.ppermute(value, 'inner', [(i, i ^ step * CORES) for i in range(fetche...  3.6 us
    pallas_call x1, Pallas kernels, per_device(): pl.pallas_call(left_kernel, out_shape=[f32(width, fetched * size), f32(wi...  3.2 us
    pallas_call x1, Pallas kernels, per_device(): pl.pallas_call(outer_kernel, out_shape=out_shape, in_specs=[SMEM] + [VMEM...  1.89 us
    ppermute x2, starting transfers between devices, chip_sum(): lax.ppermute(value, 'inner', [(i, i ^ step * CORES) for i in range(fetche...  1.58 us
  transfers between devices with their start and end apart: 11, of which 3 were waited for; matrix products, arithmetic and copies ran while one was open for 0% of the time, Pallas kernels for 9%

profile of v1, /device:TPU:3, one launch (start us, length us, event | category | flops | bytes accessed | tf_op | source)
XLA Modules:
  0.0 42.5 jit_solution(606984324120798985)
XLA Ops:
  0.0 0.7 %copy.9.fetch_ref = s32[2,1]{1,0:T(2,128)S(1)} copy(s32[2,1]{0,1:T(1,128)} %param.13) | data formatting | bytes 16 | tf_op args[6]
  0.7 0.1 pad_add_fusion.place_ref
  0.8 2.0 %copy-done = f32[4,27,64,64]{3,2,1,0:T(8,128)S(1)} copy-done((f32[4,27,64,64]{3,2,1,0:T(8,128)S(1)}, f32[4,27,64,64]{3,2,1,0:T(8,128)}, u32[]{:S(2)}) %copy-start) | copy-done | bytes 1769496
  2.8 1.0 %copy-done.1 = f32[4,3,64,64]{3,2,1,0:T(8,128)S(1)} copy-done((f32[4,3,64,64]{3,2,1,0:T(8,128)S(1)}, f32[4,3,64,64]{3,2,1,0:T(8,128)}, u32[]{:S(2)}) %copy-start.1) | copy-done | bytes 196632
  3.8 0.7 %copy-done.2 = s32[4,27]{1,0:T(4,128)S(1)} copy-done((s32[4,27]{1,0:T(4,128)S(1)}, s32[4,27]{1,0:T(4,128)}, u32[]{:S(2)}) %copy-start.2) | copy-done | bytes 456
  4.5 0.7 %copy-done.3 = s32[4,3]{1,0:T(4,128)S(1)} copy-done((s32[4,3]{1,0:T(4,128)S(1)}, s32[4,3]{1,0:T(4,128)}, u32[]{:S(2)}) %copy-start.3) | copy-done | bytes 72
  5.2 0.7 %copy-done.4 = s32[4]{0:T(128)S(1)} copy-done((s32[4]{0:T(128)S(1)}, s32[4]{0:T(128)}, u32[]{:S(2)}) %copy-start.4) | copy-done | bytes 40
  5.8 0.7 %copy-done.5 = s32[4]{0:T(128)S(1)} copy-done((s32[4]{0:T(128)S(1)}, s32[4]{0:T(128)}, u32[]{:S(2)}) %copy-start.5) | copy-done | bytes 40
  6.5 3.2 %left.1 = (f32[256,256]{1,0:T(8,128)S(1)}, f32[256,256]{1,0:T(8,128)S(1)}, f32[64,256]{1,0:T(8,128)S(1)}, f32[64,256]{1,0:T(8,128)S(1)}, f32[256,256]{1,0:T(8,128)S(1)}, /*index=5*/f32[256,256]{1,0:T(8,128)S(1)}) custom-call(s32[4,27]{1,0:T(4,128)S(1)} %copy-done.2, s32[4]{0:T(128)S(1)} %copy-done.4, s32[4,3]{1,0:T(4,128)S(1)} %copy-done.3, s32[4]{0:T(128)S(1)} %copy-done.5, ...), custom_call_target="tpu_custom_call" | custom-call | tf_op jit(solution)/shard_map/left/pallas_call | solution.py:180
  9.7 0.7 %collective-permute-start.4 = (f32[256,256]{1,0:T(8,128)S(1)}, f32[256,256]{1,0:T(8,128)S(1)}, u32[]{:S(2)}, u32[]{:S(2)}) collective-permute-start(f32[256,256]{1,0:T(8,128)S(1)} %get-tuple-element.18), channel_id=1, source_target_pairs={{0,1},{1,0},{2,3},{3,2},{4,5},{5,4},{6,7},{7,6},{8,9},{9,8},{10,11... | collective-permute-start | bytes 786440 | tf_op jit(solution)/shard_map/ppermute | solution.py:216
  10.4 1.2 %collective-permute-done.4 = f32[256,256]{1,0:T(8,128)S(1)} collective-permute-done((f32[256,256]{1,0:T(8,128)S(1)}, f32[256,256]{1,0:T(8,128)S(1)}, u32[]{:S(2)}, u32[]{:S(2)}) %collective-permute-start.4) | collective-permute-done | bytes 262176 | tf_op jit(solution)/shard_map/ppermute | solution.py:216
  11.6 1.3 %collective-permute-start.5 = (f32[256,256]{1,0:T(8,128)S(1)}, f32[256,256]{1,0:T(8,128)S(1)}, u32[]{:S(2)}, u32[]{:S(2)}) collective-permute-start(f32[256,256]{1,0:T(8,128)S(1)} %add.7.held_ref), channel_id=1, source_target_pairs={{0,2},{1,3},{2,0},{3,1},{4,6},{5,7},{6,4},{7,5},{8,10},{9,11},{10,... | collective-permute-start | bytes 786440 | tf_op jit(solution)/shard_map/ppermute | solution.py:221
  12.9 1.9 %collective-permute-start.8 = (f32[64,256]{1,0:T(8,128)S(1)}, f32[64,256]{1,0:T(8,128)S(1)}, u32[]{:S(2)}, u32[]{:S(2)}) collective-permute-start(f32[64,256]{1,0:T(8,128)S(1)} %get-tuple-element.19), channel_id=1, source_target_pairs={{7,1},{5,3},{2,4},{11,5},{0,6},{9,7},{6,8},{15,9},{4,10},{13,11},{... | collective-permute-start | bytes 196616 | tf_op jit(solution)/shard_map/ppermute | solution.py:242
  14.8 1.2 %middle.1 = (f32[128,256]{1,0:T(8,128)S(1)}, f32[128,256]{1,0:T(8,128)S(1)}) custom-call(s32[3]{0:T(128)S(1)} %pad_add_fusion.place_ref, f32[256,256]{1,0:T(8,128)S(1)} %get-tuple-element.13.dense_ref, f32[256,256]{1,0:T(8,128)S(1)} %get-tuple-element.14.local_ref), custom_call_target="tpu_custom_call" | custom-call | tf_op jit(solution)/shard_map/middle/pallas_call | solution.py:244
  16.1 2.2 %collective-permute-start = (f32[128,256]{1,0:T(8,128)S(1)}, f32[128,256]{1,0:T(8,128)S(1)}, u32[]{:S(2)}, u32[]{:S(2)}) collective-permute-start(f32[128,256]{1,0:T(8,128)S(1)} %get-tuple-element.16), channel_id=1, source_target_pairs={{0,1},{1,0},{2,3},{3,2},{4,5},{5,4},{6,7},{7,6},{8,9},{9,8},{10,11... | collective-permute-start | bytes 393224 | tf_op jit(solution)/shard_map/ppermute | solution.py:216
  18.3 2.1 %collective-permute-start.6 = (f32[64,256]{1,0:T(8,128)S(1)}, f32[64,256]{1,0:T(8,128)S(1)}, u32[]{:S(2)}, u32[]{:S(2)}) collective-permute-start(f32[64,256]{1,0:T(8,128)S(1)} %get-tuple-element.19), channel_id=1, source_target_pairs={{5,1},{7,3},{0,4},{9,5},{2,6},{11,7},{4,8},{13,9},{6,10},{15,11},{... | collective-permute-start | bytes 196616 | tf_op jit(solution)/shard_map/ppermute | solution.py:242
  20.4 5.3 %collective-permute-start.9 = (f32[64,256]{1,0:T(8,128)S(1)}, f32[64,256]{1,0:T(8,128)S(1)}, u32[]{:S(2)}, u32[]{:S(2)}) collective-permute-start(f32[64,256]{1,0:T(8,128)S(1)} %get-tuple-element.20), channel_id=1, source_target_pairs={{6,1},{4,3},{3,4},{10,5},{1,6},{8,7},{7,8},{14,9},{5,10},{12,11},{... | collective-permute-start | bytes 196616 | tf_op jit(solution)/shard_map/ppermute | solution.py:242
  25.7 0.0 collective-permute-done.8.refs_2_
  25.7 2.1 %collective-permute-start.7 = (f32[64,256]{1,0:T(8,128)S(1)}, f32[64,256]{1,0:T(8,128)S(1)}, u32[]{:S(2)}, u32[]{:S(2)}) collective-permute-start(f32[64,256]{1,0:T(8,128)S(1)} %get-tuple-element.20), channel_id=1, source_target_pairs={{4,1},{6,3},{1,4},{8,5},{3,6},{10,7},{5,8},{12,9},{7,10},{14,11},{... | collective-permute-start | bytes 196616 | tf_op jit(solution)/shard_map/ppermute | solution.py:242
  27.8 0.0 collective-permute-done.6.refs_0_
  27.8 0.0 collective-permute-done.9.refs_3_
  27.8 4.4 %collective-permute-done.7.refs_1_ = f32[64,256]{1,0:T(8,128)S(1)} collective-permute-done((f32[64,256]{1,0:T(8,128)S(1)}, f32[64,256]{1,0:T(8,128)S(1)}, u32[]{:S(2)}, u32[]{:S(2)}) %collective-permute-start.7) | collective-permute-done | bytes 65568 | tf_op jit(solution)/shard_map/ppermute | solution.py:242
  32.2 0.8 %window.1.own_ref = f32[256,256]{1,0:T(8,128)S(1)} custom-call(s32[3]{0:T(128)S(1)} %pad_add_fusion.place_ref, f32[256,256]{1,0:T(8,128)S(1)} %add.7.held_ref, f32[256,256]{1,0:T(8,128)S(1)} %collective-permute-done.5.came_ref, f32[64,256]{1,0:T(8,128)S(1)} %collective-permute-done.6.refs_0_, f32[64,256]{1,0:T(8,128)S(1)} %collective-permute-done.7.refs_1_, ...), custom_call_target="tpu_custom_call" | custom-call | tf_op jit(solution)/shard_map/window/pallas_call | solution.py:257
  33.1 0.1 collective-permute-start.10
  33.2 0.3 collective-permute-start.1
  33.5 0.8 %collective-permute-start.2 = (f32[128,256]{1,0:T(8,128)S(1)}, f32[128,256]{1,0:T(8,128)S(1)}, u32[]{:S(2)}, u32[]{:S(2)}) collective-permute-start(f32[128,256]{1,0:T(8,128)S(1)} %add.6.held_ref), channel_id=1, source_target_pairs={{0,1},{1,0},{2,3},{3,2},{4,5},{5,4},{6,7},{7,6},{8,9},{9,8},{10,11... | collective-permute-start | bytes 393224 | tf_op jit(solution)/shard_map/ppermute | solution.py:216
  34.2 3.6 %collective-permute-done.1.came_ref = f32[128,256]{1,0:T(8,128)S(1)} collective-permute-done((f32[128,256]{1,0:T(8,128)S(1)}, f32[128,256]{1,0:T(8,128)S(1)}, u32[]{:S(2)}, u32[]{:S(2)}) %collective-permute-start.1) | collective-permute-done | bytes 131104 | tf_op jit(solution)/shard_map/ppermute | solution.py:221
  37.8 1.3 %collective-permute-start.3 = (f32[128,256]{1,0:T(8,128)S(1)}, f32[128,256]{1,0:T(8,128)S(1)}, u32[]{:S(2)}, u32[]{:S(2)}) collective-permute-start(f32[128,256]{1,0:T(8,128)S(1)} %collective-permute-done.1.came_ref), channel_id=1, source_target_pairs={{0,1},{1,0},{2,3},{3,2},{4,5},{5,4},{6,7},{7,6},{8,9},{9,8},{10,11... | collective-permute-start | bytes 393224 | tf_op jit(solution)/shard_map/ppermute | solution.py:216
  39.2 1.9 %outer.1._ = f32[4,12,64,64]{3,2,1,0:T(8,128)} custom-call(s32[3]{0:T(128)S(1)} %pad_add_fusion.place_ref, f32[256,256]{1,0:T(8,128)S(1)} %window.1.own_ref, f32[256,256]{1,0:T(8,128)S(1)} %collective-permute-done.10.other_ref), custom_call_target="tpu_custom_call" | custom-call | tf_op jit(solution)/shard_map/outer/pallas_call | solution.py:268
  41.0 0.0 collective-permute-done.2.far_held_ref
  41.0 0.0 collective-permute-done.3.far_came_ref
  41.0 1.5 %inner.1 = f32[4,12,64,64]{3,2,1,0:T(8,128)} custom-call(s32[3]{0:T(128)S(1)} %pad_add_fusion.place_ref, f32[128,256]{1,0:T(8,128)S(1)} %add.6.held_ref, f32[128,256]{1,0:T(8,128)S(1)} %collective-permute-done.1.came_ref, f32[128,256]{1,0:T(8,128)S(1)} %collective-permute-done.2.far_held_ref, ...), custom_call_target="tpu_custom_call", output_to_operand_aliasing={{}: (5, {})} | custom-call | tf_op jit(solution)/shard_map/inner/pallas_call | solution.py:281
  (11 shorter events, 0.1 us)
Async XLA Ops:
  0.8 2.0 %copy-start = (f32[4,27,64,64]{3,2,1,0:T(8,128)S(1)}, f32[4,27,64,64]{3,2,1,0:T(8,128)}, u32[]{:S(2)}) copy-start(f32[4,27,64,64]{3,2,1,0:T(8,128)} %tiles_hbm.1) | copy-start | bytes 5308420
  2.8 1.0 %copy-start.1 = (f32[4,3,64,64]{3,2,1,0:T(8,128)S(1)}, f32[4,3,64,64]{3,2,1,0:T(8,128)}, u32[]{:S(2)}) copy-start(f32[4,3,64,64]{3,2,1,0:T(8,128)} %prolong_hbm.1) | copy-start | bytes 589828
  3.8 0.7 %copy-start.2 = (s32[4,27]{1,0:T(4,128)S(1)}, s32[4,27]{1,0:T(4,128)}, u32[]{:S(2)}) copy-start(s32[4,27]{1,0:T(4,128)} %cols_ref.1) | copy-start | bytes 1300
  4.5 0.7 %copy-start.3 = (s32[4,3]{1,0:T(4,128)S(1)}, s32[4,3]{1,0:T(4,128)}, u32[]{:S(2)}) copy-start(s32[4,3]{1,0:T(4,128)} %prolong_cols_ref.1) | copy-start | bytes 148
  5.2 0.7 %copy-start.4 = (s32[4]{0:T(128)S(1)}, s32[4]{0:T(128)}, u32[]{:S(2)}) copy-start(s32[4]{0:T(128)} %count_ref.1) | copy-start | bytes 52
  5.8 0.7 %copy-start.5 = (s32[4]{0:T(128)S(1)}, s32[4]{0:T(128)}, u32[]{:S(2)}) copy-start(s32[4]{0:T(128)} %prolong_count_ref.1) | copy-start | bytes 52
  9.7 1.9 %collective-permute-start.4 = (f32[256,256]{1,0:T(8,128)S(1)}, f32[256,256]{1,0:T(8,128)S(1)}, u32[]{:S(2)}, u32[]{:S(2)}) collective-permute-start(f32[256,256]{1,0:T(8,128)S(1)} %get-tuple-element.18), channel_id=1, source_target_pairs={{0,1},{1,0},{2,3},{3,2},{4,5},{5,4},{6,7},{7,6},{8,9},{9,8},{10,11... | collective-permute-start | bytes 786440 | tf_op jit(solution)/shard_map/ppermute | solution.py:216
  11.6 20.6 %collective-permute-start.5 = (f32[256,256]{1,0:T(8,128)S(1)}, f32[256,256]{1,0:T(8,128)S(1)}, u32[]{:S(2)}, u32[]{:S(2)}) collective-permute-start(f32[256,256]{1,0:T(8,128)S(1)} %add.7.held_ref), channel_id=1, source_target_pairs={{0,2},{1,3},{2,0},{3,1},{4,6},{5,7},{6,4},{7,5},{8,10},{9,11},{10,... | collective-permute-start | bytes 786440 | tf_op jit(solution)/shard_map/ppermute | solution.py:221
  12.9 12.8 %collective-permute-start.8 = (f32[64,256]{1,0:T(8,128)S(1)}, f32[64,256]{1,0:T(8,128)S(1)}, u32[]{:S(2)}, u32[]{:S(2)}) collective-permute-start(f32[64,256]{1,0:T(8,128)S(1)} %get-tuple-element.19), channel_id=1, source_target_pairs={{7,1},{5,3},{2,4},{11,5},{0,6},{9,7},{6,8},{15,9},{4,10},{13,11},{... | collective-permute-start | bytes 196616 | tf_op jit(solution)/shard_map/ppermute | solution.py:242
  16.1 17.1 %collective-permute-start = (f32[128,256]{1,0:T(8,128)S(1)}, f32[128,256]{1,0:T(8,128)S(1)}, u32[]{:S(2)}, u32[]{:S(2)}) collective-permute-start(f32[128,256]{1,0:T(8,128)S(1)} %get-tuple-element.16), channel_id=1, source_target_pairs={{0,1},{1,0},{2,3},{3,2},{4,5},{5,4},{6,7},{7,6},{8,9},{9,8},{10,11... | collective-permute-start | bytes 393224 | tf_op jit(solution)/shard_map/ppermute | solution.py:216
  18.3 9.5 %collective-permute-start.6 = (f32[64,256]{1,0:T(8,128)S(1)}, f32[64,256]{1,0:T(8,128)S(1)}, u32[]{:S(2)}, u32[]{:S(2)}) collective-permute-start(f32[64,256]{1,0:T(8,128)S(1)} %get-tuple-element.19), channel_id=1, source_target_pairs={{5,1},{7,3},{0,4},{9,5},{2,6},{11,7},{4,8},{13,9},{6,10},{15,11},{... | collective-permute-start | bytes 196616 | tf_op jit(solution)/shard_map/ppermute | solution.py:242
  20.4 7.5 %collective-permute-start.9 = (f32[64,256]{1,0:T(8,128)S(1)}, f32[64,256]{1,0:T(8,128)S(1)}, u32[]{:S(2)}, u32[]{:S(2)}) collective-permute-start(f32[64,256]{1,0:T(8,128)S(1)} %get-tuple-element.20), channel_id=1, source_target_pairs={{6,1},{4,3},{3,4},{10,5},{1,6},{8,7},{7,8},{14,9},{5,10},{12,11},{... | collective-permute-start | bytes 196616 | tf_op jit(solution)/shard_map/ppermute | solution.py:242
  25.7 6.5 %collective-permute-start.7 = (f32[64,256]{1,0:T(8,128)S(1)}, f32[64,256]{1,0:T(8,128)S(1)}, u32[]{:S(2)}, u32[]{:S(2)}) collective-permute-start(f32[64,256]{1,0:T(8,128)S(1)} %get-tuple-element.20), channel_id=1, source_target_pairs={{4,1},{6,3},{1,4},{8,5},{3,6},{10,7},{5,8},{12,9},{7,10},{14,11},{... | collective-permute-start | bytes 196616 | tf_op jit(solution)/shard_map/ppermute | solution.py:242
  33.1 6.1 %collective-permute-start.10 = (f32[256,256]{1,0:T(8,128)S(1)}, f32[256,256]{1,0:T(8,128)S(1)}, u32[]{:S(2)}, u32[]{:S(2)}) collective-permute-start(f32[256,256]{1,0:T(8,128)S(1)} %window.1.own_ref), channel_id=1, source_target_pairs={{0,1},{1,0},{2,3},{3,2},{4,5},{5,4},{6,7},{7,6},{8,9},{9,8},{10,11... | collective-permute-start | bytes 786440 | tf_op jit(solution)/shard_map/ppermute | solution.py:216
  33.2 4.6 %collective-permute-start.1 = (f32[128,256]{1,0:T(8,128)S(1)}, f32[128,256]{1,0:T(8,128)S(1)}, u32[]{:S(2)}, u32[]{:S(2)}) collective-permute-start(f32[128,256]{1,0:T(8,128)S(1)} %add.6.held_ref), channel_id=1, source_target_pairs={{0,2},{1,3},{2,0},{3,1},{4,6},{5,7},{6,4},{7,5},{8,10},{9,11},{10,... | collective-permute-start | bytes 393224 | tf_op jit(solution)/shard_map/ppermute | solution.py:221
  33.5 7.6 %collective-permute-start.2 = (f32[128,256]{1,0:T(8,128)S(1)}, f32[128,256]{1,0:T(8,128)S(1)}, u32[]{:S(2)}, u32[]{:S(2)}) collective-permute-start(f32[128,256]{1,0:T(8,128)S(1)} %add.6.held_ref), channel_id=1, source_target_pairs={{0,1},{1,0},{2,3},{3,2},{4,5},{5,4},{6,7},{7,6},{8,9},{9,8},{10,11... | collective-permute-start | bytes 393224 | tf_op jit(solution)/shard_map/ppermute | solution.py:216
  37.8 3.2 %collective-permute-start.3 = (f32[128,256]{1,0:T(8,128)S(1)}, f32[128,256]{1,0:T(8,128)S(1)}, u32[]{:S(2)}, u32[]{:S(2)}) collective-permute-start(f32[128,256]{1,0:T(8,128)S(1)} %collective-permute-done.1.came_ref), channel_id=1, source_target_pairs={{0,1},{1,0},{2,3},{3,2},{4,5},{5,4},{6,7},{7,6},{8,9},{9,8},{10,11... | collective-permute-start | bytes 393224 | tf_op jit(solution)/shard_map/ppermute | solution.py:216

commit v2 on v0

v2 whole, which is shorter than its diff:
```python
import functools

import jax
import jax.numpy as jnp
from jax import lax
from jax.experimental import pallas as pl
from jax.experimental.pallas import tpu as pltpu
from jax.sharding import PartitionSpec as P

CG = 4
CORES = 2
VMEM_BYTES = 32 * 1024 * 1024


def split(value):
    high = value.astype(jnp.bfloat16)
    low = (value - high.astype(jnp.float32)).astype(jnp.bfloat16)
    return high, low


def product(left, right):
    dot = functools.partial(jnp.dot, preferred_element_type=jnp.float32)
    return dot(left[0], right[0]) + (dot(left[1], right[0]) + dot(left[0], right[1]))


def left_kernel(
    cols_hbm,
    count_hbm,
    prolong_cols_hbm,
    prolong_count_hbm,
    fetch_hbm,
    tiles_hbm,
    prolong_hbm,
    keep_outer_ref,
    send_outer_ref,
    keep_inner_ref,
    send_inner_ref,
    straight_ref,
    cols,
    count,
    prolong_cols,
    prolong_count,
    fetch,
    tiles,
    prolong,
    dense,
    whole,
    *rest,
):
    slots, (tile_sems, small_sems) = rest[:-2], rest[-2:]
    rows, entries, size, _ = tiles.shape
    fetched = keep_outer_ref.shape[1] // size
    smalls = [
        pltpu.make_async_copy(source, target, small_sems.at[index])
        for index, (source, target) in enumerate(
            (
                (prolong_cols_hbm, prolong_cols),
                (prolong_count_hbm, prolong_count),
                (fetch_hbm, fetch),
                (cols_hbm, cols),
                (count_hbm, count),
                (prolong_hbm, prolong),
            )
        )
    ]
    copies = [
        pltpu.make_async_copy(tiles_hbm.at[row], tiles.at[row], tile_sems.at[row])
        for row in range(rows)
    ]
    for copy in smalls + copies:
        copy.start()
    for ref in slots:
        ref[...] = jnp.zeros_like(ref)
    first_coarse = lax.axis_index("sub") * CG
    core = lax.rem(lax.axis_index("inner"), CORES)
    for copy in smalls:
        copy.wait()

    for row in range(rows):
        blocks = []
        for coarse in range(CG):
            block = None
            for m in range(prolong.shape[1]):
                hit = (prolong_cols[row, m] == first_coarse + coarse) & (m < prolong_count[row])
                term = prolong[row, m] * jnp.where(hit, 1.0, 0.0)
                block = term if block is None else block + term
            blocks.append(block)
        dense[row * size : (row + 1) * size, :] = jnp.concatenate(blocks, axis=1)

    half = keep_inner_ref.shape[0]
    straight_ref[...] = dense[pl.ds(pl.multiple_of(fetch[1 - core] * size, size), size), :]
    send_inner_ref[half:, :] = dense[pl.ds(pl.multiple_of(fetch[core] * size, size), size), :]

    for first in range(0, rows, 2):
        pair = range(first, min(first + 2, rows))
        for row in pair:
            copies[row].wait()
        for entry in range(entries):
            for row in pair:
                slot = jnp.where(entry < count[row], cols[row, entry], rows + 2 * fetched)
                slots[row][slot] += tiles[row, entry]

    def gathered(first, length):
        return jnp.concatenate(
            [
                jnp.concatenate([slots[row][first + j] for j in range(length)], axis=1)
                for row in range(rows)
            ],
            axis=0,
        )

    value = dense[...]
    turned = split(value.T)
    keep_outer_ref[...] = product(turned, split(gathered(rows + core * fetched, fetched)))
    send_outer_ref[...] = product(turned, split(gathered(rows + (1 - core) * fetched, fetched)))
    local = product(turned, split(gathered(0, rows)))
    whole[...] = product(split(local), split(value))
    keep_inner_ref[...] = whole[pl.ds(pl.multiple_of(core * half, half), half), :]
    send_inner_ref[:half, :] = whole[pl.ds(pl.multiple_of((1 - core) * half, half), half), :]


def window_kernel(held_ref, came_ref, *refs):
    ghosts, result_ref, prolong = refs[:-2], refs[-2], refs[-1]
    position = lax.axis_index("inner")
    core, chip = lax.rem(position, CORES), lax.div(position, CORES)
    chips = len(ghosts)
    size = ghosts[0].shape[0] // CORES
    for shift, ghost in enumerate(ghosts):
        for cross in range(CORES):
            source = lax.rem(chip + shift, chips) * CORES + lax.rem(core + cross, CORES)
            prolong[pl.ds(pl.multiple_of(source * size, size), size), :] = ghost[
                cross * size : (cross + 1) * size, :
            ]
    result_ref[...] = product(split(held_ref[...] + came_ref[...]), split(prolong[...]))


def store_blocks(value, blocks, out_hbm, first_row, first_column, sem):
    size = blocks.shape[-1]
    copies = []
    for g in range(value.shape[0] // size):
        for h in range(value.shape[1] // size):
            blocks[g, h] = value[g * size : (g + 1) * size, h * size : (h + 1) * size]
        copy = pltpu.make_async_copy(
            blocks.at[g],
            out_hbm.at[first_row + g, pl.ds(first_column, blocks.shape[1])],
            sem.at[g],
        )
        copy.start()
        copies.append(copy)
    return copies


def outer_kernel(other, value_ref, *refs):
    out_hbm, blocks, sem = refs[-3:]
    core = lax.rem(lax.axis_index("inner"), CORES)
    owner = 1 - core if other else core
    for copy in store_blocks(value_ref[...], blocks, out_hbm, 0, owner * 2 * CG, sem):
        copy.wait()


def inner_kernel(other, held_ref, came_ref, _, out_hbm, blocks, sem):
    core = lax.rem(lax.axis_index("inner"), CORES)
    owner = 1 - core if other else core
    first_row = owner * (CG // CORES)
    for copy in store_blocks(
        held_ref[...] + came_ref[...], blocks, out_hbm, first_row, CG, sem
    ):
        copy.wait()


VMEM = pl.BlockSpec(memory_space=pltpu.VMEM)
HBM = pl.BlockSpec(memory_space=pltpu.HBM)
PARAMS = pltpu.CompilerParams(vmem_limit_bytes=VMEM_BYTES)


def f32(*shape):
    return jax.ShapeDtypeStruct(shape, jnp.float32)


def per_device(
    operator_tiles,
    operator_cols,
    operator_count,
    prolong_tiles,
    prolong_cols,
    prolong_count,
    fetch_rows,
):
    rows, entries, size, _ = operator_tiles.shape
    subs, fetched = lax.axis_size("sub"), lax.axis_size("inner")
    chips = fetched // CORES
    width = CG * size
    half = width // CORES

    smem = pltpu.SMEM
    keep_outer, send_outer, keep_inner, send_inner, straight = pl.pallas_call(
        left_kernel,
        out_shape=[
            f32(width, fetched * size),
            f32(width, fetched * size),
            f32(half, width),
            f32(half + size, width),
            f32(size, width),
        ],
        in_specs=[HBM] * 7,
        out_specs=[VMEM] * 5,
        scratch_shapes=[
            smem(operator_cols.shape, jnp.int32),
            smem(operator_count.shape, jnp.int32),
            smem(prolong_cols.shape, jnp.int32),
            smem(prolong_count.shape, jnp.int32),
            smem((2,), jnp.int32),
            pltpu.VMEM(operator_tiles.shape, jnp.float32),
            pltpu.VMEM(prolong_tiles.shape, jnp.float32),
            pltpu.VMEM((rows * size, width), jnp.float32),
            pltpu.VMEM((width, width), jnp.float32),
        ]
        + [pltpu.VMEM((rows + 2 * fetched + 1, size, size), jnp.float32)] * rows
        + [pltpu.SemaphoreType.DMA((rows,)), pltpu.SemaphoreType.DMA((6,))],
        compiler_params=PARAMS,
        name="left",
    )(
        *(
            pltpu.with_memory_space_constraint(value, pltpu.HBM)
            for value in (
                operator_cols,
                operator_count,
                prolong_cols,
                prolong_count,
                fetch_rows.reshape(-1),
                operator_tiles,
                prolong_tiles,
            )
        )
    )

    swap_cores = [(i, i ^ 1) for i in range(fetched)]

    def other_core(value):
        return lax.ppermute(value, "inner", swap_cores)

    def chip_sum(value):
        step = 1
        while step < chips:
            came = lax.ppermute(
                value, "inner", [(i, i ^ (step * CORES)) for i in range(fetched)]
            )
            step *= 2
            if step < chips:
                value = value + came
        return value, came

    held_outer, came_outer = chip_sum(keep_outer + other_core(send_outer))
    arrived = other_core(send_inner)

    edge = jnp.concatenate([straight, arrived[half:]], axis=0)
    ghosts = []
    for shift in range(chips):
        pairs = []
        for sub in range(subs):
            for chip in range(chips):
                for core in range(CORES):
                    source_sub = sub - 1 if core == 0 else sub + 1
                    if 0 <= source_sub < subs:
                        source = (chip + shift) % chips * CORES + core
                        pairs.append(
                            (source_sub * fetched + source, sub * fetched + chip * CORES + core)
                        )
        ghosts.append(lax.ppermute(edge, ("sub", "inner"), pairs))

    held_inner, came_inner = chip_sum(keep_inner + arrived[:half])

    window = pl.pallas_call(
        window_kernel,
        out_shape=f32(width, width),
        in_specs=[VMEM] * (2 + len(ghosts)),
        out_specs=VMEM,
        scratch_shapes=[pltpu.VMEM((fetched * size, width), jnp.float32)],
        compiler_params=PARAMS,
        name="window",
    )(held_outer, came_outer, *ghosts)

    def store(kernel, rows, *values, out=None, name):
        outs = () if out is None else (out,)
        return pl.pallas_call(
            kernel,
            out_shape=f32(CG, 3 * CG, size, size),
            in_specs=[VMEM] * len(values) + [HBM] * len(outs),
            out_specs=HBM,
            scratch_shapes=[
                pltpu.VMEM((rows, CG, size, size), jnp.float32),
                pltpu.SemaphoreType.DMA((rows,)),
            ],
            input_output_aliases={len(values): 0} if outs else {},
            compiler_params=PARAMS,
            name=name,
        )(*values, *outs)

    own = functools.partial
    out = store(own(outer_kernel, False), CG, window, name="outer_own")
    out = store(own(outer_kernel, True), CG, other_core(window), out=out, name="outer_other")
    out = store(
        own(inner_kernel, False), CG // CORES, held_inner, came_inner, out=out, name="inner_own"
    )
    return store(
        own(inner_kernel, True),
        CG // CORES,
        other_core(held_inner),
        other_core(came_inner),
        out=out,
        name="inner_other",
    )


def solution(mesh):
    placed = (
        P(("sub", "inner"), None, None, None),
        P(("sub", "inner"), None),
        P(("sub", "inner")),
        P(("sub", "inner"), None, None, None),
        P(("sub", "inner"), None),
        P(("sub", "inner")),
        P(("sub", "inner"), None),
    )
    return jax.shard_map(
        per_device,
        mesh=mesh,
        in_specs=placed,
        out_specs=P("sub", None, None, None),
        check_vma=False,
    )
```

time: 131 us -> 29.5 us (0.23)
  the two profiles are of different devices: /device:TPU:3 before, /device:TPU:25 now
where the time goes in v2:
time: 29.5 us; the launch traced here: 29.3 us
  starting transfers between devices  11.8 us (40%)
  waiting for transfers between devices  10.2 us (35%)
  Pallas kernels  7.14 us (24%)
    ppermute x2, starting transfers between devices, per_device(): ghosts.append(lax.ppermute(edge, ('sub', 'inner'), pairs))  5.11 us
    ppermute x5, starting transfers between devices, other_core(): return lax.ppermute(value, 'inner', swap_cores)  5.09 us
    ppermute x2, waiting for transfers between devices, chip_sum(): lax.ppermute(value, 'inner', [(i, i ^ step * CORES) for i in range(fetche...  4.59 us
    ppermute x2, waiting for transfers between devices, per_device(): ghosts.append(lax.ppermute(edge, ('sub', 'inner'), pairs))  4.49 us
    pallas_call x1, Pallas kernels, per_device(): pl.pallas_call(left_kernel, out_shape=[f32(width, fetched * size), f32(wi...  3.42 us
    pallas_call x4, Pallas kernels, store(): pl.pallas_call(kernel, out_shape=f32(CG, 3 * CG, size, size), in_specs=[V...  3.42 us
    ppermute x2, starting transfers between devices, chip_sum(): lax.ppermute(value, 'inner', [(i, i ^ step * CORES) for i in range(fetche...  1.6 us
    ppermute x5, waiting for transfers between devices, other_core(): return lax.ppermute(value, 'inner', swap_cores)  1.09 us
  transfers between devices with their start and end apart: 9, of which 4 were waited for; matrix products, arithmetic and copies ran while one was open for 0% of the time, Pallas kernels for 9%

profile of v2, /device:TPU:25, one launch (start us, length us, event | category | flops | bytes accessed | tf_op | source)
XLA Modules:
  0.0 29.3 jit_solution(8282715877217039977)
XLA Ops:
  0.0 3.4 %left.1 = (f32[256,256]{1,0:T(8,128)S(1)}, f32[256,256]{1,0:T(8,128)S(1)}, f32[128,256]{1,0:T(8,128)S(1)}, f32[192,256]{1,0:T(8,128)S(1)}, f32[64,256]{1,0:T(8,128)S(1)}) custom-call(s32[4,27]{1,0:T(4,128)} %cols_hbm.1, s32[4]{0:T(128)} %count_hbm.1, s32[4,3]{1,0:T(4,128)} %prolong_cols_hbm.1, s32[4]{0:T(128)} %prolong_count_hbm.1, s32[2]{0:T(128)} %bitcast.1, ...), custom_call_target="tpu_custom_call" | custom-call | tf_op jit(solution)/shard_map/left/pallas_call | solution.py:196
  3.4 0.7 %collective-permute-start.4 = (f32[256,256]{1,0:T(8,128)S(1)}, f32[256,256]{1,0:T(8,128)S(1)}, u32[]{:S(2)}, u32[]{:S(2)}) collective-permute-start(f32[256,256]{1,0:T(8,128)S(1)} %get-tuple-element.13), channel_id=1, source_target_pairs={{0,1},{1,0},{2,3},{3,2},{4,5},{5,4},{6,7},{7,6},{8,9},{9,8},{10,11... | collective-permute-start | bytes 786440 | tf_op jit(solution)/shard_map/ppermute | solution.py:240
  4.2 0.1 collective-permute-start
  4.2 1.1 %collective-permute-done.4 = f32[256,256]{1,0:T(8,128)S(1)} collective-permute-done((f32[256,256]{1,0:T(8,128)S(1)}, f32[256,256]{1,0:T(8,128)S(1)}, u32[]{:S(2)}, u32[]{:S(2)}) %collective-permute-start.4) | collective-permute-done | bytes 262176 | tf_op jit(solution)/shard_map/ppermute | solution.py:240
  5.4 1.3 %collective-permute-start.5 = (f32[256,256]{1,0:T(8,128)S(1)}, f32[256,256]{1,0:T(8,128)S(1)}, u32[]{:S(2)}, u32[]{:S(2)}) collective-permute-start(f32[256,256]{1,0:T(8,128)S(1)} %add.7.held_ref), channel_id=1, source_target_pairs={{0,2},{1,3},{2,0},{3,1},{4,6},{5,7},{6,4},{7,5},{8,10},{9,11},{10,... | collective-permute-start | bytes 786440 | tf_op jit(solution)/shard_map/ppermute | solution.py:245
  6.7 0.0 collective-permute-done
  6.7 3.0 %collective-permute-start.6 = (f32[128,256]{1,0:T(8,128)S(1)}, f32[128,256]{1,0:T(8,128)S(1)}, u32[]{:S(2)}, u32[]{:S(2)}) collective-permute-start(f32[128,256]{1,0:T(8,128)S(1)} %pad_maximum_fusion), channel_id=1, source_target_pairs={{5,1},{7,3},{0,4},{9,5},{2,6},{11,7},{4,8},{13,9},{6,10},{15,11},{... | collective-permute-start | bytes 393224 | tf_op jit(solution)/shard_map/ppermute | solution.py:269
  9.7 2.1 %collective-permute-start.7 = (f32[128,256]{1,0:T(8,128)S(1)}, f32[128,256]{1,0:T(8,128)S(1)}, u32[]{:S(2)}, u32[]{:S(2)}) collective-permute-start(f32[128,256]{1,0:T(8,128)S(1)} %pad_maximum_fusion), channel_id=1, source_target_pairs={{7,1},{5,3},{2,4},{11,5},{0,6},{9,7},{6,8},{15,9},{4,10},{13,11},{... | collective-permute-start | bytes 393224 | tf_op jit(solution)/shard_map/ppermute | solution.py:269
  11.8 0.9 %collective-permute-done.6.refs_0_ = f32[128,256]{1,0:T(8,128)S(1)} collective-permute-done((f32[128,256]{1,0:T(8,128)S(1)}, f32[128,256]{1,0:T(8,128)S(1)}, u32[]{:S(2)}, u32[]{:S(2)}) %collective-permute-start.6) | collective-permute-done | bytes 131104 | tf_op jit(solution)/shard_map/ppermute | solution.py:269
  12.7 3.6 %collective-permute-done.7.refs_1_ = f32[128,256]{1,0:T(8,128)S(1)} collective-permute-done((f32[128,256]{1,0:T(8,128)S(1)}, f32[128,256]{1,0:T(8,128)S(1)}, u32[]{:S(2)}, u32[]{:S(2)}) %collective-permute-start.7) | collective-permute-done | bytes 131104 | tf_op jit(solution)/shard_map/ppermute | solution.py:269
  16.3 0.0 collective-permute-done.5.came_ref
  16.3 0.3 %window.1.value_ref = f32[256,256]{1,0:T(8,128)S(1)} custom-call(f32[256,256]{1,0:T(8,128)S(1)} %add.7.held_ref, f32[256,256]{1,0:T(8,128)S(1)} %collective-permute-done.5.came_ref, f32[128,256]{1,0:T(8,128)S(1)} %collective-permute-done.6.refs_0_, f32[128,256]{1,0:T(8,128)S(1)} %collective-permute-done.7.refs_1_), custom_call_target="tpu_custom_call" | custom-call | tf_op jit(solution)/shard_map/window/pallas_call | solution.py:273
  16.6 3.2 %collective-permute-start.8 = (f32[256,256]{1,0:T(8,128)S(1)}, f32[256,256]{1,0:T(8,128)S(1)}, u32[]{:S(2)}, u32[]{:S(2)}) collective-permute-start(f32[256,256]{1,0:T(8,128)S(1)} %window.1.value_ref), channel_id=1, source_target_pairs={{0,1},{1,0},{2,3},{3,2},{4,5},{5,4},{6,7},{7,6},{8,9},{9,8},{10,11... | collective-permute-start | bytes 786440 | tf_op jit(solution)/shard_map/ppermute | solution.py:240
  19.8 0.3 collective-permute-start.2
  20.1 0.3 %collective-permute-start.1 = (f32[128,256]{1,0:T(8,128)S(1)}, f32[128,256]{1,0:T(8,128)S(1)}, u32[]{:S(2)}, u32[]{:S(2)}) collective-permute-start(f32[128,256]{1,0:T(8,128)S(1)} %slice_add_fusion.held_ref), channel_id=1, source_target_pairs={{0,1},{1,0},{2,3},{3,2},{4,5},{5,4},{6,7},{7,6},{8,9},{9,8},{10,11... | collective-permute-start | bytes 393224 | tf_op jit(solution)/shard_map/ppermute | solution.py:240
  20.4 4.6 %collective-permute-done.2.came_ref = f32[128,256]{1,0:T(8,128)S(1)} collective-permute-done((f32[128,256]{1,0:T(8,128)S(1)}, f32[128,256]{1,0:T(8,128)S(1)}, u32[]{:S(2)}, u32[]{:S(2)}) %collective-permute-start.2) | collective-permute-done | bytes 131104 | tf_op jit(solution)/shard_map/ppermute | solution.py:245
  25.0 0.8 %collective-permute-start.3 = (f32[128,256]{1,0:T(8,128)S(1)}, f32[128,256]{1,0:T(8,128)S(1)}, u32[]{:S(2)}, u32[]{:S(2)}) collective-permute-start(f32[128,256]{1,0:T(8,128)S(1)} %collective-permute-done.2.came_ref), channel_id=1, source_target_pairs={{0,1},{1,0},{2,3},{3,2},{4,5},{5,4},{6,7},{7,6},{8,9},{9,8},{10,11... | collective-permute-start | bytes 393224 | tf_op jit(solution)/shard_map/ppermute | solution.py:240
  25.8 0.9 %outer_own.1.refs_0_ = f32[4,12,64,64]{3,2,1,0:T(8,128)} custom-call(f32[256,256]{1,0:T(8,128)S(1)} %window.1.value_ref), custom_call_target="tpu_custom_call" | custom-call | tf_op jit(solution)/shard_map/outer_own/pallas_call | solution.py:285
  26.7 0.0 collective-permute-done.8.value_ref
  26.7 0.9 %outer_other.1._ = f32[4,12,64,64]{3,2,1,0:T(8,128)} custom-call(f32[256,256]{1,0:T(8,128)S(1)} %collective-permute-done.8.value_ref, f32[4,12,64,64]{3,2,1,0:T(8,128)} %outer_own.1.refs_0_), custom_call_target="tpu_custom_call", output_to_operand_aliasing={{}: (1, {})} | custom-call | tf_op jit(solution)/shard_map/outer_other/pallas_call | solution.py:285
  27.6 0.8 %inner_own.1._ = f32[4,12,64,64]{3,2,1,0:T(8,128)} custom-call(f32[128,256]{1,0:T(8,128)S(1)} %slice_add_fusion.held_ref, f32[128,256]{1,0:T(8,128)S(1)} %collective-permute-done.2.came_ref, f32[4,12,64,64]{3,2,1,0:T(8,128)} %outer_other.1._), custom_call_target="tpu_custom_call", output_to_operand_aliasing={{}: (2, {})} | custom-call | tf_op jit(solution)/shard_map/inner_own/pallas_call | solution.py:285
  28.5 0.0 collective-permute-done.1.held_ref
  28.5 0.0 collective-permute-done.3.came_ref
  28.5 0.8 %inner_other.1 = f32[4,12,64,64]{3,2,1,0:T(8,128)} custom-call(f32[128,256]{1,0:T(8,128)S(1)} %collective-permute-done.1.held_ref, f32[128,256]{1,0:T(8,128)S(1)} %collective-permute-done.3.came_ref, f32[4,12,64,64]{3,2,1,0:T(8,128)} %inner_own.1._), custom_call_target="tpu_custom_call", output_to_operand_aliasing={{}: (2, {})} | custom-call | tf_op jit(solution)/shard_map/inner_other/pallas_call | solution.py:285
  (4 shorter events, 0.1 us)
Async XLA Ops:
  3.4 1.9 %collective-permute-start.4 = (f32[256,256]{1,0:T(8,128)S(1)}, f32[256,256]{1,0:T(8,128)S(1)}, u32[]{:S(2)}, u32[]{:S(2)}) collective-permute-start(f32[256,256]{1,0:T(8,128)S(1)} %get-tuple-element.13), channel_id=1, source_target_pairs={{0,1},{1,0},{2,3},{3,2},{4,5},{5,4},{6,7},{7,6},{8,9},{9,8},{10,11... | collective-permute-start | bytes 786440 | tf_op jit(solution)/shard_map/ppermute | solution.py:240
  4.2 2.5 %collective-permute-start = (f32[192,256]{1,0:T(8,128)S(1)}, f32[192,256]{1,0:T(8,128)S(1)}, u32[]{:S(2)}, u32[]{:S(2)}) collective-permute-start(f32[192,256]{1,0:T(8,128)S(1)} %get-tuple-element.11), channel_id=1, source_target_pairs={{0,1},{1,0},{2,3},{3,2},{4,5},{5,4},{6,7},{7,6},{8,9},{9,8},{10,11... | collective-permute-start | bytes 589832 | tf_op jit(solution)/shard_map/ppermute | solution.py:240
  5.4 11.0 %collective-permute-start.5 = (f32[256,256]{1,0:T(8,128)S(1)}, f32[256,256]{1,0:T(8,128)S(1)}, u32[]{:S(2)}, u32[]{:S(2)}) collective-permute-start(f32[256,256]{1,0:T(8,128)S(1)} %add.7.held_ref), channel_id=1, source_target_pairs={{0,2},{1,3},{2,0},{3,1},{4,6},{5,7},{6,4},{7,5},{8,10},{9,11},{10,... | collective-permute-start | bytes 786440 | tf_op jit(solution)/shard_map/ppermute | solution.py:245
  6.7 6.0 %collective-permute-start.6 = (f32[128,256]{1,0:T(8,128)S(1)}, f32[128,256]{1,0:T(8,128)S(1)}, u32[]{:S(2)}, u32[]{:S(2)}) collective-permute-start(f32[128,256]{1,0:T(8,128)S(1)} %pad_maximum_fusion), channel_id=1, source_target_pairs={{5,1},{7,3},{0,4},{9,5},{2,6},{11,7},{4,8},{13,9},{6,10},{15,11},{... | collective-permute-start | bytes 393224 | tf_op jit(solution)/shard_map/ppermute | solution.py:269
  9.7 6.6 %collective-permute-start.7 = (f32[128,256]{1,0:T(8,128)S(1)}, f32[128,256]{1,0:T(8,128)S(1)}, u32[]{:S(2)}, u32[]{:S(2)}) collective-permute-start(f32[128,256]{1,0:T(8,128)S(1)} %pad_maximum_fusion), channel_id=1, source_target_pairs={{7,1},{5,3},{2,4},{11,5},{0,6},{9,7},{6,8},{15,9},{4,10},{13,11},{... | collective-permute-start | bytes 393224 | tf_op jit(solution)/shard_map/ppermute | solution.py:269
  16.6 10.1 %collective-permute-start.8 = (f32[256,256]{1,0:T(8,128)S(1)}, f32[256,256]{1,0:T(8,128)S(1)}, u32[]{:S(2)}, u32[]{:S(2)}) collective-permute-start(f32[256,256]{1,0:T(8,128)S(1)} %window.1.value_ref), channel_id=1, source_target_pairs={{0,1},{1,0},{2,3},{3,2},{4,5},{5,4},{6,7},{7,6},{8,9},{9,8},{10,11... | collective-permute-start | bytes 786440 | tf_op jit(solution)/shard_map/ppermute | solution.py:240
  19.8 5.2 %collective-permute-start.2 = (f32[128,256]{1,0:T(8,128)S(1)}, f32[128,256]{1,0:T(8,128)S(1)}, u32[]{:S(2)}, u32[]{:S(2)}) collective-permute-start(f32[128,256]{1,0:T(8,128)S(1)} %slice_add_fusion.held_ref), channel_id=1, source_target_pairs={{0,2},{1,3},{2,0},{3,1},{4,6},{5,7},{6,4},{7,5},{8,10},{9,11},{10,... | collective-permute-start | bytes 393224 | tf_op jit(solution)/shard_map/ppermute | solution.py:245
  20.1 8.3 %collective-permute-start.1 = (f32[128,256]{1,0:T(8,128)S(1)}, f32[128,256]{1,0:T(8,128)S(1)}, u32[]{:S(2)}, u32[]{:S(2)}) collective-permute-start(f32[128,256]{1,0:T(8,128)S(1)} %slice_add_fusion.held_ref), channel_id=1, source_target_pairs={{0,1},{1,0},{2,3},{3,2},{4,5},{5,4},{6,7},{7,6},{8,9},{9,8},{10,11... | collective-permute-start | bytes 393224 | tf_op jit(solution)/shard_map/ppermute | solution.py:240
  25.0 3.5 %collective-permute-start.3 = (f32[128,256]{1,0:T(8,128)S(1)}, f32[128,256]{1,0:T(8,128)S(1)}, u32[]{:S(2)}, u32[]{:S(2)}) collective-permute-start(f32[128,256]{1,0:T(8,128)S(1)} %collective-permute-done.2.came_ref), channel_id=1, source_target_pairs={{0,1},{1,0},{2,3},{3,2},{4,5},{5,4},{6,7},{7,6},{8,9},{9,8},{10,11... | collective-permute-start | bytes 393224 | tf_op jit(solution)/shard_map/ppermute | solution.py:240

commit v3 on v2

--- a/solution.py
+++ b/solution.py
@@ -88,8 +88,8 @@
         dense[row * size : (row + 1) * size, :] = jnp.concatenate(blocks, axis=1)
 
     half = keep_inner_ref.shape[0]
-    straight_ref[...] = dense[pl.ds(pl.multiple_of(fetch[1 - core] * size, size), size), :]
-    send_inner_ref[half:, :] = dense[pl.ds(pl.multiple_of(fetch[core] * size, size), size), :]
+    straight_ref[...] = dense[pl.ds(pl.multiple_of(fetch[core] * size, size), size), :]
+    send_inner_ref[half:, :] = dense[pl.ds(pl.multiple_of(fetch[1 - core] * size, size), size), :]
 
     for first in range(0, rows, 2):
         pair = range(first, min(first + 2, rows))
@@ -127,44 +127,35 @@
     size = ghosts[0].shape[0] // CORES
     for shift, ghost in enumerate(ghosts):
         for cross in range(CORES):
-            source = lax.rem(chip + shift, chips) * CORES + lax.rem(core + cross, CORES)
+            source = lax.rem(shift - chip + chips, chips) * CORES + lax.rem(1 - core + cross, CORES)
             prolong[pl.ds(pl.multiple_of(source * size, size), size), :] = ghost[
                 cross * size : (cross + 1) * size, :
             ]
     result_ref[...] = product(split(held_ref[...] + came_ref[...]), split(prolong[...]))
 
 
-def store_blocks(value, blocks, out_hbm, first_row, first_column, sem):
-    size = blocks.shape[-1]
-    copies = []
-    for g in range(value.shape[0] // size):
-        for h in range(value.shape[1] // size):
-            blocks[g, h] = value[g * size : (g + 1) * size, h * size : (h + 1) * size]
-        copy = pltpu.make_async_copy(
-            blocks.at[g],
-            out_hbm.at[first_row + g, pl.ds(first_column, blocks.shape[1])],
-            sem.at[g],
-        )
-        copy.start()
-        copies.append(copy)
-    return copies
-
-
-def outer_kernel(other, value_ref, *refs):
-    out_hbm, blocks, sem = refs[-3:]
+def store_kernel(other, window_ref, held_ref, came_ref, *refs):
+    out_hbm, outer, inner, outer_sem, inner_sem = refs[-5:]
     core = lax.rem(lax.axis_index("inner"), CORES)
     owner = 1 - core if other else core
-    for copy in store_blocks(value_ref[...], blocks, out_hbm, 0, owner * 2 * CG, sem):
-        copy.wait()
-
-
-def inner_kernel(other, held_ref, came_ref, _, out_hbm, blocks, sem):
-    core = lax.rem(lax.axis_index("inner"), CORES)
-    owner = 1 - core if other else core
-    first_row = owner * (CG // CORES)
-    for copy in store_blocks(
-        held_ref[...] + came_ref[...], blocks, out_hbm, first_row, CG, sem
-    ):
+    size = outer.shape[-1]
+    copies = []
+
+    def store(value, blocks, first_row, first_column, sem):
+        for g in range(blocks.shape[0]):
+            for h in range(blocks.shape[1]):
+                blocks[g, h] = value[g * size : (g + 1) * size, h * size : (h + 1) * size]
+            copy = pltpu.make_async_copy(
+                blocks.at[g],
+                out_hbm.at[first_row + g, pl.ds(first_column, blocks.shape[1])],
+                sem.at[g],
+            )
+            copy.start()
+            copies.append(copy)
+
+    store(window_ref[...], outer, 0, owner * 2 * CG, outer_sem)
+    store(held_ref[...] + came_ref[...], inner, owner * (CG // CORES), CG, inner_sem)
+    for copy in copies:
         copy.wait()
 
 
@@ -257,15 +248,11 @@
     ghosts = []
     for shift in range(chips):
         pairs = []
-        for sub in range(subs):
+        for sub in range(subs - 1):
             for chip in range(chips):
-                for core in range(CORES):
-                    source_sub = sub - 1 if core == 0 else sub + 1
-                    if 0 <= source_sub < subs:
-                        source = (chip + shift) % chips * CORES + core
-                        pairs.append(
-                            (source_sub * fetched + source, sub * fetched + chip * CORES + core)
-                        )
+                below = (sub * chips + chip) * CORES + 1
+                above = ((sub + 1) * chips + (shift - chip) % chips) * CORES
+                pairs += [(below, above), (above, below)]
         ghosts.append(lax.ppermute(edge, ("sub", "inner"), pairs))
 
     held_inner, came_inner = chip_sum(keep_inner + arrived[:half])
@@ -280,36 +267,25 @@
         name="window",
     )(held_outer, came_outer, *ghosts)
 
-    def store(kernel, rows, *values, out=None, name):
-        outs = () if out is None else (out,)
+    def store(other, *values):
         return pl.pallas_call(
-            kernel,
+            functools.partial(store_kernel, other),
             out_shape=f32(CG, 3 * CG, size, size),
-            in_specs=[VMEM] * len(values) + [HBM] * len(outs),
+            in_specs=[VMEM] * 3 + [HBM] * (len(values) - 3),
             out_specs=HBM,
             scratch_shapes=[
-                pltpu.VMEM((rows, CG, size, size), jnp.float32),
-                pltpu.SemaphoreType.DMA((rows,)),
+                pltpu.VMEM((CG, CG, size, size), jnp.float32),
+                pltpu.VMEM((CG // CORES, CG, size, size), jnp.float32),
+                pltpu.SemaphoreType.DMA((CG,)),
+                pltpu.SemaphoreType.DMA((CG // CORES,)),
             ],
-            input_output_aliases={len(values): 0} if outs else {},
+            input_output_aliases={3: 0} if other else {},
             compiler_params=PARAMS,
-            name=name,
-        )(*values, *outs)
-
-    own = functools.partial
-    out = store(own(outer_kernel, False), CG, window, name="outer_own")
-    out = store(own(outer_kernel, True), CG, other_core(window), out=out, name="outer_other")
-    out = store(
-        own(inner_kernel, False), CG // CORES, held_inner, came_inner, out=out, name="inner_own"
-    )
-    return store(
-        own(inner_kernel, True),
-        CG // CORES,
-        other_core(held_inner),
-        other_core(came_inner),
-        out=out,
-        name="inner_other",
-    )
+            name="store_other" if other else "store_own",
+        )(*values)
+
+    own = (window, held_inner, came_inner)
+    return store(True, *map(other_core, own), store(False, *own))
 
 
 def solution(mesh):

time: 29.5 us -> 22.3 us (0.76)
  the two profiles are of different devices: /device:TPU:25 before, /device:TPU:3 now
where the time goes in v3:
time: 22.3 us; the launch traced here: 22.1 us
  starting transfers between devices  11.4 us (51%)
  Pallas kernels  5.74 us (26%)
  waiting for transfers between devices  4.84 us (22%)
    ppermute x2, starting transfers between devices, per_device(): ghosts.append(lax.ppermute(edge, ('sub', 'inner'), pairs))  6.41 us
    pallas_call x1, Pallas kernels, per_device(): pl.pallas_call(left_kernel, out_shape=[f32(width, fetched * size), f32(wi...  3.43 us
    ppermute x2, waiting for transfers between devices, per_device(): ghosts.append(lax.ppermute(edge, ('sub', 'inner'), pairs))  3.1 us
    ppermute x2, starting transfers between devices, chip_sum(): lax.ppermute(value, 'inner', [(i, i ^ step * CORES) for i in range(fetche...  2.6 us
    ppermute x5, starting transfers between devices, other_core(): return lax.ppermute(value, 'inner', swap_cores)  2.37 us
    pallas_call x2, Pallas kernels, store(): pl.pallas_call(functools.partial(store_kernel, other), out_shape=f32(CG,...  2.01 us
    ppermute x5, waiting for transfers between devices, other_core(): return lax.ppermute(value, 'inner', swap_cores)  1.37 us
  transfers between devices with their start and end apart: 9, of which 4 were waited for; matrix products, arithmetic and copies ran while one was open for 0% of the time, Pallas kernels for 6%

profile of v3, /device:TPU:3, one launch (start us, length us, event | category | flops | bytes accessed | tf_op | source)
XLA Modules:
  0.0 22.1 jit_solution(2516049738949376203)
XLA Ops:
  0.0 3.4 %left.1 = (f32[256,256]{1,0:T(8,128)S(1)}, f32[256,256]{1,0:T(8,128)S(1)}, f32[128,256]{1,0:T(8,128)S(1)}, f32[192,256]{1,0:T(8,128)S(1)}, f32[64,256]{1,0:T(8,128)S(1)}) custom-call(s32[4,27]{1,0:T(4,128)} %cols_hbm.1, s32[4]{0:T(128)} %count_hbm.1, s32[4,3]{1,0:T(4,128)} %prolong_cols_hbm.1, s32[4]{0:T(128)} %prolong_count_hbm.1, s32[2]{0:T(128)} %bitcast.1, ...), custom_call_target="tpu_custom_call" | custom-call | tf_op jit(solution)/shard_map/left/pallas_call | solution.py:187
  3.4 0.7 %collective-permute-start = (f32[256,256]{1,0:T(8,128)S(1)}, f32[256,256]{1,0:T(8,128)S(1)}, u32[]{:S(2)}, u32[]{:S(2)}) collective-permute-start(f32[256,256]{1,0:T(8,128)S(1)} %get-tuple-element.11), channel_id=1, source_target_pairs={{0,1},{1,0},{2,3},{3,2},{4,5},{5,4},{6,7},{7,6},{8,9},{9,8},{10,11... | collective-permute-start | bytes 786440 | tf_op jit(solution)/shard_map/ppermute | solution.py:231
  4.2 0.1 collective-permute-start.2
  4.2 1.4 %collective-permute-done.2 = f32[192,256]{1,0:T(8,128)S(1)} collective-permute-done((f32[192,256]{1,0:T(8,128)S(1)}, f32[192,256]{1,0:T(8,128)S(1)}, u32[]{:S(2)}, u32[]{:S(2)}) %collective-permute-start.2) | collective-permute-done | bytes 196640 | tf_op jit(solution)/shard_map/ppermute | solution.py:231
  5.6 0.0 collective-permute-done
  5.7 1.3 %collective-permute-start.1 = (f32[256,256]{1,0:T(8,128)S(1)}, f32[256,256]{1,0:T(8,128)S(1)}, u32[]{:S(2)}, u32[]{:S(2)}) collective-permute-start(f32[256,256]{1,0:T(8,128)S(1)} %add.6.held_ref), channel_id=1, source_target_pairs={{0,2},{1,3},{2,0},{3,1},{4,6},{5,7},{6,4},{7,5},{8,10},{9,11},{10,... | collective-permute-start | bytes 786440 | tf_op jit(solution)/shard_map/ppermute | solution.py:236
  7.0 3.7 %collective-permute-start.4 = (f32[128,256]{1,0:T(8,128)S(1)}, f32[128,256]{1,0:T(8,128)S(1)}, u32[]{:S(2)}, u32[]{:S(2)}) collective-permute-start(f32[128,256]{1,0:T(8,128)S(1)} %pad_maximum_fusion), channel_id=1, source_target_pairs={{1,6},{6,1},{3,4},{4,3},{5,10},{10,5},{7,8},{8,7},{9,14},{14,9},{1... | collective-permute-start | bytes 393224 | tf_op jit(solution)/shard_map/ppermute | solution.py:256
  10.6 2.7 %collective-permute-start.3 = (f32[128,256]{1,0:T(8,128)S(1)}, f32[128,256]{1,0:T(8,128)S(1)}, u32[]{:S(2)}, u32[]{:S(2)}) collective-permute-start(f32[128,256]{1,0:T(8,128)S(1)} %pad_maximum_fusion), channel_id=1, source_target_pairs={{1,4},{4,1},{3,6},{6,3},{5,8},{8,5},{7,10},{10,7},{9,12},{12,9},{1... | collective-permute-start | bytes 393224 | tf_op jit(solution)/shard_map/ppermute | solution.py:256
  13.4 1.3 %collective-permute-start.7 = (f32[128,256]{1,0:T(8,128)S(1)}, f32[128,256]{1,0:T(8,128)S(1)}, u32[]{:S(2)}, u32[]{:S(2)}) collective-permute-start(f32[128,256]{1,0:T(8,128)S(1)} %slice_add_fusion.held_ref), channel_id=1, source_target_pairs={{0,2},{1,3},{2,0},{3,1},{4,6},{5,7},{6,4},{7,5},{8,10},{9,11},{10,... | collective-permute-start | bytes 393224 | tf_op jit(solution)/shard_map/ppermute | solution.py:236
  14.7 0.5 %collective-permute-done.4.refs_1_ = f32[128,256]{1,0:T(8,128)S(1)} collective-permute-done((f32[128,256]{1,0:T(8,128)S(1)}, f32[128,256]{1,0:T(8,128)S(1)}, u32[]{:S(2)}, u32[]{:S(2)}) %collective-permute-start.4) | collective-permute-done | bytes 131104 | tf_op jit(solution)/shard_map/ppermute | solution.py:256
  15.3 2.6 %collective-permute-done.3.refs_0_ = f32[128,256]{1,0:T(8,128)S(1)} collective-permute-done((f32[128,256]{1,0:T(8,128)S(1)}, f32[128,256]{1,0:T(8,128)S(1)}, u32[]{:S(2)}, u32[]{:S(2)}) %collective-permute-start.3) | collective-permute-done | bytes 131104 | tf_op jit(solution)/shard_map/ppermute | solution.py:256
  17.8 0.0 collective-permute-done.1.came_ref
  17.8 0.3 %window.1.window_ref = f32[256,256]{1,0:T(8,128)S(1)} custom-call(f32[256,256]{1,0:T(8,128)S(1)} %add.6.held_ref, f32[256,256]{1,0:T(8,128)S(1)} %collective-permute-done.1.came_ref, f32[128,256]{1,0:T(8,128)S(1)} %collective-permute-done.3.refs_0_, f32[128,256]{1,0:T(8,128)S(1)} %collective-permute-done.4.refs_1_), custom_call_target="tpu_custom_call" | custom-call | tf_op jit(solution)/shard_map/window/pallas_call | solution.py:260
  18.1 0.1 collective-permute-start.5
  18.2 0.5 %collective-permute-start.6 = (f32[128,256]{1,0:T(8,128)S(1)}, f32[128,256]{1,0:T(8,128)S(1)}, u32[]{:S(2)}, u32[]{:S(2)}) collective-permute-start(f32[128,256]{1,0:T(8,128)S(1)} %slice_add_fusion.held_ref), channel_id=1, source_target_pairs={{0,1},{1,0},{2,3},{3,2},{4,5},{5,4},{6,7},{7,6},{8,9},{9,8},{10,11... | collective-permute-start | bytes 393224 | tf_op jit(solution)/shard_map/ppermute | solution.py:231
  18.7 0.4 %collective-permute-done.7.came_ref = f32[128,256]{1,0:T(8,128)S(1)} collective-permute-done((f32[128,256]{1,0:T(8,128)S(1)}, f32[128,256]{1,0:T(8,128)S(1)}, u32[]{:S(2)}, u32[]{:S(2)}) %collective-permute-start.7) | collective-permute-done | bytes 131104 | tf_op jit(solution)/shard_map/ppermute | solution.py:236
  19.1 1.0 %collective-permute-start.8 = (f32[128,256]{1,0:T(8,128)S(1)}, f32[128,256]{1,0:T(8,128)S(1)}, u32[]{:S(2)}, u32[]{:S(2)}) collective-permute-start(f32[128,256]{1,0:T(8,128)S(1)} %collective-permute-done.7.came_ref), channel_id=1, source_target_pairs={{0,1},{1,0},{2,3},{3,2},{4,5},{5,4},{6,7},{7,6},{8,9},{9,8},{10,11... | collective-permute-start | bytes 393224 | tf_op jit(solution)/shard_map/ppermute | solution.py:231
  20.1 1.0 %store_own.1.refs_0_ = f32[4,12,64,64]{3,2,1,0:T(8,128)} custom-call(f32[256,256]{1,0:T(8,128)S(1)} %window.1.window_ref, f32[128,256]{1,0:T(8,128)S(1)} %slice_add_fusion.held_ref, f32[128,256]{1,0:T(8,128)S(1)} %collective-permute-done.7.came_ref), custom_call_target="tpu_custom_call" | custom-call | tf_op jit(solution)/shard_map/store_own/pallas_call | solution.py:271
  21.1 0.0 collective-permute-done.6.held_ref
  21.1 0.0 collective-permute-done.8.came_ref
  21.1 0.0 collective-permute-done.5.window_ref
  21.1 1.0 %store_other.1 = f32[4,12,64,64]{3,2,1,0:T(8,128)} custom-call(f32[256,256]{1,0:T(8,128)S(1)} %collective-permute-done.5.window_ref, f32[128,256]{1,0:T(8,128)S(1)} %collective-permute-done.6.held_ref, f32[128,256]{1,0:T(8,128)S(1)} %collective-permute-done.8.came_ref, f32[4,12,64,64]{3,2,1,0:T(8,128)} %store_own.1.refs_0_), custom_call_target="tpu_custom_call", output_to_operand_aliasing={{}: (3, {})} | custom-call | tf_op jit(solution)/shard_map/store_other/pallas_call | solution.py:271
  (4 shorter events, 0.1 us)
Async XLA Ops:
  3.4 2.2 %collective-permute-start = (f32[256,256]{1,0:T(8,128)S(1)}, f32[256,256]{1,0:T(8,128)S(1)}, u32[]{:S(2)}, u32[]{:S(2)}) collective-permute-start(f32[256,256]{1,0:T(8,128)S(1)} %get-tuple-element.11), channel_id=1, source_target_pairs={{0,1},{1,0},{2,3},{3,2},{4,5},{5,4},{6,7},{7,6},{8,9},{9,8},{10,11... | collective-permute-start | bytes 786440 | tf_op jit(solution)/shard_map/ppermute | solution.py:231
  4.2 1.4 %collective-permute-start.2 = (f32[192,256]{1,0:T(8,128)S(1)}, f32[192,256]{1,0:T(8,128)S(1)}, u32[]{:S(2)}, u32[]{:S(2)}) collective-permute-start(f32[192,256]{1,0:T(8,128)S(1)} %get-tuple-element.13), channel_id=1, source_target_pairs={{0,1},{1,0},{2,3},{3,2},{4,5},{5,4},{6,7},{7,6},{8,9},{9,8},{10,11... | collective-permute-start | bytes 589832 | tf_op jit(solution)/shard_map/ppermute | solution.py:231
  5.7 12.2 %collective-permute-start.1 = (f32[256,256]{1,0:T(8,128)S(1)}, f32[256,256]{1,0:T(8,128)S(1)}, u32[]{:S(2)}, u32[]{:S(2)}) collective-permute-start(f32[256,256]{1,0:T(8,128)S(1)} %add.6.held_ref), channel_id=1, source_target_pairs={{0,2},{1,3},{2,0},{3,1},{4,6},{5,7},{6,4},{7,5},{8,10},{9,11},{10,... | collective-permute-start | bytes 786440 | tf_op jit(solution)/shard_map/ppermute | solution.py:236
  7.0 8.3 %collective-permute-start.4 = (f32[128,256]{1,0:T(8,128)S(1)}, f32[128,256]{1,0:T(8,128)S(1)}, u32[]{:S(2)}, u32[]{:S(2)}) collective-permute-start(f32[128,256]{1,0:T(8,128)S(1)} %pad_maximum_fusion), channel_id=1, source_target_pairs={{1,6},{6,1},{3,4},{4,3},{5,10},{10,5},{7,8},{8,7},{9,14},{14,9},{1... | collective-permute-start | bytes 393224 | tf_op jit(solution)/shard_map/ppermute | solution.py:256
  10.6 7.2 %collective-permute-start.3 = (f32[128,256]{1,0:T(8,128)S(1)}, f32[128,256]{1,0:T(8,128)S(1)}, u32[]{:S(2)}, u32[]{:S(2)}) collective-permute-start(f32[128,256]{1,0:T(8,128)S(1)} %pad_maximum_fusion), channel_id=1, source_target_pairs={{1,4},{4,1},{3,6},{6,3},{5,8},{8,5},{7,10},{10,7},{9,12},{12,9},{1... | collective-permute-start | bytes 393224 | tf_op jit(solution)/shard_map/ppermute | solution.py:256
  13.4 5.6 %collective-permute-start.7 = (f32[128,256]{1,0:T(8,128)S(1)}, f32[128,256]{1,0:T(8,128)S(1)}, u32[]{:S(2)}, u32[]{:S(2)}) collective-permute-start(f32[128,256]{1,0:T(8,128)S(1)} %slice_add_fusion.held_ref), channel_id=1, source_target_pairs={{0,2},{1,3},{2,0},{3,1},{4,6},{5,7},{6,4},{7,5},{8,10},{9,11},{10,... | collective-permute-start | bytes 393224 | tf_op jit(solution)/shard_map/ppermute | solution.py:236
  18.1 3.0 %collective-permute-start.5 = (f32[256,256]{1,0:T(8,128)S(1)}, f32[256,256]{1,0:T(8,128)S(1)}, u32[]{:S(2)}, u32[]{:S(2)}) collective-permute-start(f32[256,256]{1,0:T(8,128)S(1)} %window.1.window_ref), channel_id=1, source_target_pairs={{0,1},{1,0},{2,3},{3,2},{4,5},{5,4},{6,7},{7,6},{8,9},{9,8},{10,11... | collective-permute-start | bytes 786440 | tf_op jit(solution)/shard_map/ppermute | solution.py:231
  18.2 2.9 %collective-permute-start.6 = (f32[128,256]{1,0:T(8,128)S(1)}, f32[128,256]{1,0:T(8,128)S(1)}, u32[]{:S(2)}, u32[]{:S(2)}) collective-permute-start(f32[128,256]{1,0:T(8,128)S(1)} %slice_add_fusion.held_ref), channel_id=1, source_target_pairs={{0,1},{1,0},{2,3},{3,2},{4,5},{5,4},{6,7},{7,6},{8,9},{9,8},{10,11... | collective-permute-start | bytes 393224 | tf_op jit(solution)/shard_map/ppermute | solution.py:231
  19.1 2.0 %collective-permute-start.8 = (f32[128,256]{1,0:T(8,128)S(1)}, f32[128,256]{1,0:T(8,128)S(1)}, u32[]{:S(2)}, u32[]{:S(2)}) collective-permute-start(f32[128,256]{1,0:T(8,128)S(1)} %collective-permute-done.7.came_ref), channel_id=1, source_target_pairs={{0,1},{1,0},{2,3},{3,2},{4,5},{5,4},{6,7},{7,6},{8,9},{9,8},{10,11... | collective-permute-start | bytes 393224 | tf_op jit(solution)/shard_map/ppermute | solution.py:231

commit v4 on v3

--- a/solution.py
+++ b/solution.py
@@ -9,6 +9,7 @@
 
 CG = 4
 CORES = 2
+META = 8
 VMEM_BYTES = 32 * 1024 * 1024
 
 
@@ -88,8 +89,23 @@
         dense[row * size : (row + 1) * size, :] = jnp.concatenate(blocks, axis=1)
 
     half = keep_inner_ref.shape[0]
-    straight_ref[...] = dense[pl.ds(pl.multiple_of(fetch[core] * size, size), size), :]
-    send_inner_ref[half:, :] = dense[pl.ds(pl.multiple_of(fetch[1 - core] * size, size), size), :]
+    packed = straight_ref.shape[0] - META
+    quarter = size // CG
+    line = lax.broadcasted_iota(jnp.int32, (META, CG * size), 0)
+    lane = lax.broadcasted_iota(jnp.int32, (META, CG * size), 1)
+    for cross, (ref, first) in enumerate(((straight_ref, 0), (send_inner_ref, half))):
+        row = fetch[core if cross == 0 else 1 - core]
+        meta = jnp.zeros((META, CG * size), jnp.float32)
+        for m in range(prolong.shape[1]):
+            tile = prolong[row, m]
+            ref[first + m * quarter : first + (m + 1) * quarter, :] = jnp.concatenate(
+                [tile[part * quarter : (part + 1) * quarter, :] for part in range(CG)], axis=1
+            )
+            column = jnp.where(
+                m < prolong_count[row], prolong_cols[row, m] - first_coarse, -1
+            ).astype(jnp.float32)
+            meta = jnp.where((line == cross) & (lane == m), column, meta)
+        ref[first + packed : first + packed + META, :] = meta
 
     for first in range(0, rows, 2):
         pair = range(first, min(first + 2, rows))
@@ -124,13 +140,29 @@
     position = lax.axis_index("inner")
     core, chip = lax.rem(position, CORES), lax.div(position, CORES)
     chips = len(ghosts)
-    size = ghosts[0].shape[0] // CORES
+    size = result_ref.shape[0] // CG
+    quarter = size // CG
+    packed = (ghosts[0].shape[0] - META) // CORES
     for shift, ghost in enumerate(ghosts):
         for cross in range(CORES):
             source = lax.rem(shift - chip + chips, chips) * CORES + lax.rem(1 - core + cross, CORES)
-            prolong[pl.ds(pl.multiple_of(source * size, size), size), :] = ghost[
-                cross * size : (cross + 1) * size, :
-            ]
+            blocks = [None] * CG
+            for m in range(packed // quarter):
+                first = cross * packed + m * quarter
+                column = ghost[CORES * packed + cross : CORES * packed + cross + 1, m : m + 1]
+                tile = jnp.concatenate(
+                    [
+                        ghost[first : first + quarter, part * size : (part + 1) * size]
+                        for part in range(CG)
+                    ],
+                    axis=0,
+                )
+                for coarse in range(CG):
+                    term = tile * jnp.where(column == coarse, 1.0, 0.0)
+                    blocks[coarse] = term if m == 0 else blocks[coarse] + term
+            prolong[pl.ds(pl.multiple_of(source * size, size), size), :] = jnp.concatenate(
+                blocks, axis=1
+            )
     result_ref[...] = product(split(held_ref[...] + came_ref[...]), split(prolong[...]))
 
 
@@ -182,6 +214,7 @@
     chips = fetched // CORES
     width = CG * size
     half = width // CORES
+    packed = prolong_tiles.shape[1] * size // CG
 
     smem = pltpu.SMEM
     keep_outer, send_outer, keep_inner, send_inner, straight = pl.pallas_call(
@@ -190,8 +223,8 @@
             f32(width, fetched * size),
             f32(width, fetched * size),
             f32(half, width),
-            f32(half + size, width),
-            f32(size, width),
+            f32(half + packed + META, width),
+            f32(packed + META, width),
         ],
         in_specs=[HBM] * 7,
         out_specs=[VMEM] * 5,
@@ -244,7 +277,10 @@
     held_outer, came_outer = chip_sum(keep_outer + other_core(send_outer))
     arrived = other_core(send_inner)
 
-    edge = jnp.concatenate([straight, arrived[half:]], axis=0)
+    crossed = arrived[half:]
+    edge = jnp.concatenate(
+        [straight[:packed], crossed[:packed], straight[packed:] + crossed[packed:]], axis=0
+    )
     ghosts = []
     for shift in range(chips):
         pairs = []

time: 22.3 us -> 21.9 us (0.982)
  starting transfers between devices: 11.4 us -> 10.9 us
  Pallas kernels: 5.74 us -> 6 us
    ppermute x5, starting transfers between devices: 2.37 us -> 1.86 us  [other_core(): return lax.ppermute(value, 'inner', swap_cores)]
    ppermute x2, waiting for transfers between devices: 3.1 us -> 2.73 us  [per_device(): ghosts.append(lax.ppermute(edge, ('sub', 'inner'), pairs))]
    pallas_call x1, Pallas kernels: 0.3 us -> 0.56 us  [per_device(): pl.pallas_call(window_kernel, out_shape=f32(width, width), in_specs=[VMEM...]
  transfers between devices with their start and end apart: 9 -> 9, of which waited for: 4 -> 5; matrix products, arithmetic and copies ran while one was open for 0% -> 0% of each run, Pallas kernels for 6% -> 7%
where the time goes in v4:
time: 21.9 us; the launch traced here: 21.7 us
  starting transfers between devices  10.9 us (50%)
  Pallas kernels  6 us (27%)
  waiting for transfers between devices  4.64 us (21%)
    ppermute x2, starting transfers between devices, per_device(): ghosts.append(lax.ppermute(edge, ('sub', 'inner'), pairs))  6.4 us
    pallas_call x1, Pallas kernels, per_device(): pl.pallas_call(left_kernel, out_shape=[f32(width, fetched * size), f32(wi...  3.43 us
    ppermute x2, waiting for transfers between devices, per_device(): ghosts.append(lax.ppermute(edge, ('sub', 'inner'), pairs))  2.73 us
    ppermute x2, starting transfers between devices, chip_sum(): lax.ppermute(value, 'inner', [(i, i ^ step * CORES) for i in range(fetche...  2.62 us
    pallas_call x2, Pallas kernels, store(): pl.pallas_call(functools.partial(store_kernel, other), out_shape=f32(CG,...  2.01 us
    ppermute x5, starting transfers between devices, other_core(): return lax.ppermute(value, 'inner', swap_cores)  1.86 us
    ppermute x5, waiting for transfers between devices, other_core(): return lax.ppermute(value, 'inner', swap_cores)  1.45 us
    pallas_call x1, Pallas kernels, per_device(): pl.pallas_call(window_kernel, out_shape=f32(width, width), in_specs=[VMEM...  0.56 us
  transfers between devices with their start and end apart: 9, of which 5 were waited for; matrix products, arithmetic and copies ran while one was open for 0% of the time, Pallas kernels for 7%

profile of v4, /device:TPU:3, one launch (start us, length us, event | category | flops | bytes accessed | tf_op | source)
XLA Modules:
  0.0 21.7 jit_solution(9365258196822037057)
XLA Ops:
  0.0 3.4 %left.1 = (f32[256,256]{1,0:T(8,128)S(1)}, f32[256,256]{1,0:T(8,128)S(1)}, f32[128,256]{1,0:T(8,128)S(1)}, f32[184,256]{1,0:T(8,128)S(1)}, f32[56,256]{1,0:T(8,128)S(1)}) custom-call(s32[4,27]{1,0:T(4,128)} %cols_hbm.1, s32[4]{0:T(128)} %count_hbm.1, s32[4,3]{1,0:T(4,128)} %prolong_cols_hbm.1, s32[4]{0:T(128)} %prolong_count_hbm.1, s32[2]{0:T(128)} %bitcast.1, ...), custom_call_target="tpu_custom_call" | custom-call | tf_op jit(solution)/shard_map/left/pallas_call | solution.py:220
  3.4 0.7 %collective-permute-start.2 = (f32[184,256]{1,0:T(8,128)S(1)}, f32[184,256]{1,0:T(8,128)S(1)}, u32[]{:S(2)}, u32[]{:S(2)}) collective-permute-start(f32[184,256]{1,0:T(8,128)S(1)} %get-tuple-element.13), channel_id=1, source_target_pairs={{0,1},{1,0},{2,3},{3,2},{4,5},{5,4},{6,7},{7,6},{8,9},{9,8},{10,11... | collective-permute-start | bytes 565256 | tf_op jit(solution)/shard_map/ppermute | solution.py:264
  4.2 0.1 collective-permute-start
  4.3 1.0 %collective-permute-done.2 = f32[184,256]{1,0:T(8,128)S(1)} collective-permute-done((f32[184,256]{1,0:T(8,128)S(1)}, f32[184,256]{1,0:T(8,128)S(1)}, u32[]{:S(2)}, u32[]{:S(2)}) %collective-permute-start.2) | collective-permute-done | bytes 188448 | tf_op jit(solution)/shard_map/ppermute | solution.py:264
  5.2 0.5 %collective-permute-done = f32[256,256]{1,0:T(8,128)S(1)} collective-permute-done((f32[256,256]{1,0:T(8,128)S(1)}, f32[256,256]{1,0:T(8,128)S(1)}, u32[]{:S(2)}, u32[]{:S(2)}) %collective-permute-start) | collective-permute-done | bytes 262176 | tf_op jit(solution)/shard_map/ppermute | solution.py:264
  5.8 1.3 %collective-permute-start.1 = (f32[256,256]{1,0:T(8,128)S(1)}, f32[256,256]{1,0:T(8,128)S(1)}, u32[]{:S(2)}, u32[]{:S(2)}) collective-permute-start(f32[256,256]{1,0:T(8,128)S(1)} %add.9.held_ref), channel_id=1, source_target_pairs={{0,2},{1,3},{2,0},{3,1},{4,6},{5,7},{6,4},{7,5},{8,10},{9,11},{10,... | collective-permute-start | bytes 786440 | tf_op jit(solution)/shard_map/ppermute | solution.py:269
  7.1 3.6 %collective-permute-start.4 = (f32[104,256]{1,0:T(8,128)S(1)}, f32[104,256]{1,0:T(8,128)S(1)}, u32[]{:S(2)}, u32[]{:S(2)}) collective-permute-start(f32[104,256]{1,0:T(8,128)S(1)} %pad_maximum_fusion), channel_id=1, source_target_pairs={{1,6},{6,1},{3,4},{4,3},{5,10},{10,5},{7,8},{8,7},{9,14},{14,9},{1... | collective-permute-start | bytes 319496 | tf_op jit(solution)/shard_map/ppermute | solution.py:292
  10.6 2.8 %collective-permute-start.3 = (f32[104,256]{1,0:T(8,128)S(1)}, f32[104,256]{1,0:T(8,128)S(1)}, u32[]{:S(2)}, u32[]{:S(2)}) collective-permute-start(f32[104,256]{1,0:T(8,128)S(1)} %pad_maximum_fusion), channel_id=1, source_target_pairs={{1,4},{4,1},{3,6},{6,3},{5,8},{8,5},{7,10},{10,7},{9,12},{12,9},{1... | collective-permute-start | bytes 319496 | tf_op jit(solution)/shard_map/ppermute | solution.py:292
  13.5 1.3 %collective-permute-start.7 = (f32[128,256]{1,0:T(8,128)S(1)}, f32[128,256]{1,0:T(8,128)S(1)}, u32[]{:S(2)}, u32[]{:S(2)}) collective-permute-start(f32[128,256]{1,0:T(8,128)S(1)} %slice_add_fusion.held_ref), channel_id=1, source_target_pairs={{0,2},{1,3},{2,0},{3,1},{4,6},{5,7},{6,4},{7,5},{8,10},{9,11},{10,... | collective-permute-start | bytes 393224 | tf_op jit(solution)/shard_map/ppermute | solution.py:269
  14.8 0.2 %collective-permute-done.4.refs_1_ = f32[104,256]{1,0:T(8,128)S(1)} collective-permute-done((f32[104,256]{1,0:T(8,128)S(1)}, f32[104,256]{1,0:T(8,128)S(1)}, u32[]{:S(2)}, u32[]{:S(2)}) %collective-permute-start.4) | collective-permute-done | bytes 106528 | tf_op jit(solution)/shard_map/ppermute | solution.py:292
  15.1 2.5 %collective-permute-done.3.refs_0_ = f32[104,256]{1,0:T(8,128)S(1)} collective-permute-done((f32[104,256]{1,0:T(8,128)S(1)}, f32[104,256]{1,0:T(8,128)S(1)}, u32[]{:S(2)}, u32[]{:S(2)}) %collective-permute-start.3) | collective-permute-done | bytes 106528 | tf_op jit(solution)/shard_map/ppermute | solution.py:292
  17.6 0.0 collective-permute-done.1.came_ref
  17.6 0.6 %window.1.window_ref = f32[256,256]{1,0:T(8,128)S(1)} custom-call(f32[256,256]{1,0:T(8,128)S(1)} %add.9.held_ref, f32[256,256]{1,0:T(8,128)S(1)} %collective-permute-done.1.came_ref, f32[104,256]{1,0:T(8,128)S(1)} %collective-permute-done.3.refs_0_, f32[104,256]{1,0:T(8,128)S(1)} %collective-permute-done.4.refs_1_), custom_call_target="tpu_custom_call" | custom-call | tf_op jit(solution)/shard_map/window/pallas_call | solution.py:296
  18.1 0.1 collective-permute-start.5
  18.2 0.5 %collective-permute-start.6 = (f32[128,256]{1,0:T(8,128)S(1)}, f32[128,256]{1,0:T(8,128)S(1)}, u32[]{:S(2)}, u32[]{:S(2)}) collective-permute-start(f32[128,256]{1,0:T(8,128)S(1)} %slice_add_fusion.held_ref), channel_id=1, source_target_pairs={{0,1},{1,0},{2,3},{3,2},{4,5},{5,4},{6,7},{7,6},{8,9},{9,8},{10,11... | collective-permute-start | bytes 393224 | tf_op jit(solution)/shard_map/ppermute | solution.py:264
  18.7 0.5 %collective-permute-done.7.came_ref = f32[128,256]{1,0:T(8,128)S(1)} collective-permute-done((f32[128,256]{1,0:T(8,128)S(1)}, f32[128,256]{1,0:T(8,128)S(1)}, u32[]{:S(2)}, u32[]{:S(2)}) %collective-permute-start.7) | collective-permute-done | bytes 131104 | tf_op jit(solution)/shard_map/ppermute | solution.py:269
  19.2 0.5 %collective-permute-start.8 = (f32[128,256]{1,0:T(8,128)S(1)}, f32[128,256]{1,0:T(8,128)S(1)}, u32[]{:S(2)}, u32[]{:S(2)}) collective-permute-start(f32[128,256]{1,0:T(8,128)S(1)} %collective-permute-done.7.came_ref), channel_id=1, source_target_pairs={{0,1},{1,0},{2,3},{3,2},{4,5},{5,4},{6,7},{7,6},{8,9},{9,8},{10,11... | collective-permute-start | bytes 393224 | tf_op jit(solution)/shard_map/ppermute | solution.py:264
  19.6 1.0 %store_own.1.refs_0_ = f32[4,12,64,64]{3,2,1,0:T(8,128)} custom-call(f32[256,256]{1,0:T(8,128)S(1)} %window.1.window_ref, f32[128,256]{1,0:T(8,128)S(1)} %slice_add_fusion.held_ref, f32[128,256]{1,0:T(8,128)S(1)} %collective-permute-done.7.came_ref), custom_call_target="tpu_custom_call" | custom-call | tf_op jit(solution)/shard_map/store_own/pallas_call | solution.py:307
  20.6 0.0 collective-permute-done.6.held_ref
  20.7 0.0 collective-permute-done.8.came_ref
  20.7 0.0 collective-permute-done.5.window_ref
  20.7 1.0 %store_other.1 = f32[4,12,64,64]{3,2,1,0:T(8,128)} custom-call(f32[256,256]{1,0:T(8,128)S(1)} %collective-permute-done.5.window_ref, f32[128,256]{1,0:T(8,128)S(1)} %collective-permute-done.6.held_ref, f32[128,256]{1,0:T(8,128)S(1)} %collective-permute-done.8.came_ref, f32[4,12,64,64]{3,2,1,0:T(8,128)} %store_own.1.refs_0_), custom_call_target="tpu_custom_call", output_to_operand_aliasing={{}: (3, {})} | custom-call | tf_op jit(solution)/shard_map/store_other/pallas_call | solution.py:307
  (6 shorter events, 0.1 us)
Async XLA Ops:
  3.4 1.8 %collective-permute-start.2 = (f32[184,256]{1,0:T(8,128)S(1)}, f32[184,256]{1,0:T(8,128)S(1)}, u32[]{:S(2)}, u32[]{:S(2)}) collective-permute-start(f32[184,256]{1,0:T(8,128)S(1)} %get-tuple-element.13), channel_id=1, source_target_pairs={{0,1},{1,0},{2,3},{3,2},{4,5},{5,4},{6,7},{7,6},{8,9},{9,8},{10,11... | collective-permute-start | bytes 565256 | tf_op jit(solution)/shard_map/ppermute | solution.py:264
  4.2 1.5 %collective-permute-start = (f32[256,256]{1,0:T(8,128)S(1)}, f32[256,256]{1,0:T(8,128)S(1)}, u32[]{:S(2)}, u32[]{:S(2)}) collective-permute-start(f32[256,256]{1,0:T(8,128)S(1)} %get-tuple-element.11), channel_id=1, source_target_pairs={{0,1},{1,0},{2,3},{3,2},{4,5},{5,4},{6,7},{7,6},{8,9},{9,8},{10,11... | collective-permute-start | bytes 786440 | tf_op jit(solution)/shard_map/ppermute | solution.py:264
  5.8 11.8 %collective-permute-start.1 = (f32[256,256]{1,0:T(8,128)S(1)}, f32[256,256]{1,0:T(8,128)S(1)}, u32[]{:S(2)}, u32[]{:S(2)}) collective-permute-start(f32[256,256]{1,0:T(8,128)S(1)} %add.9.held_ref), channel_id=1, source_target_pairs={{0,2},{1,3},{2,0},{3,1},{4,6},{5,7},{6,4},{7,5},{8,10},{9,11},{10,... | collective-permute-start | bytes 786440 | tf_op jit(solution)/shard_map/ppermute | solution.py:269
  7.1 8.0 %collective-permute-start.4 = (f32[104,256]{1,0:T(8,128)S(1)}, f32[104,256]{1,0:T(8,128)S(1)}, u32[]{:S(2)}, u32[]{:S(2)}) collective-permute-start(f32[104,256]{1,0:T(8,128)S(1)} %pad_maximum_fusion), channel_id=1, source_target_pairs={{1,6},{6,1},{3,4},{4,3},{5,10},{10,5},{7,8},{8,7},{9,14},{14,9},{1... | collective-permute-start | bytes 319496 | tf_op jit(solution)/shard_map/ppermute | solution.py:292
  10.6 6.9 %collective-permute-start.3 = (f32[104,256]{1,0:T(8,128)S(1)}, f32[104,256]{1,0:T(8,128)S(1)}, u32[]{:S(2)}, u32[]{:S(2)}) collective-permute-start(f32[104,256]{1,0:T(8,128)S(1)} %pad_maximum_fusion), channel_id=1, source_target_pairs={{1,4},{4,1},{3,6},{6,3},{5,8},{8,5},{7,10},{10,7},{9,12},{12,9},{1... | collective-permute-start | bytes 319496 | tf_op jit(solution)/shard_map/ppermute | solution.py:292
  13.5 5.6 %collective-permute-start.7 = (f32[128,256]{1,0:T(8,128)S(1)}, f32[128,256]{1,0:T(8,128)S(1)}, u32[]{:S(2)}, u32[]{:S(2)}) collective-permute-start(f32[128,256]{1,0:T(8,128)S(1)} %slice_add_fusion.held_ref), channel_id=1, source_target_pairs={{0,2},{1,3},{2,0},{3,1},{4,6},{5,7},{6,4},{7,5},{8,10},{9,11},{10,... | collective-permute-start | bytes 393224 | tf_op jit(solution)/shard_map/ppermute | solution.py:269
  18.1 2.5 %collective-permute-start.5 = (f32[256,256]{1,0:T(8,128)S(1)}, f32[256,256]{1,0:T(8,128)S(1)}, u32[]{:S(2)}, u32[]{:S(2)}) collective-permute-start(f32[256,256]{1,0:T(8,128)S(1)} %window.1.window_ref), channel_id=1, source_target_pairs={{0,1},{1,0},{2,3},{3,2},{4,5},{5,4},{6,7},{7,6},{8,9},{9,8},{10,11... | collective-permute-start | bytes 786440 | tf_op jit(solution)/shard_map/ppermute | solution.py:264
  18.2 2.4 %collective-permute-start.6 = (f32[128,256]{1,0:T(8,128)S(1)}, f32[128,256]{1,0:T(8,128)S(1)}, u32[]{:S(2)}, u32[]{:S(2)}) collective-permute-start(f32[128,256]{1,0:T(8,128)S(1)} %slice_add_fusion.held_ref), channel_id=1, source_target_pairs={{0,1},{1,0},{2,3},{3,2},{4,5},{5,4},{6,7},{7,6},{8,9},{9,8},{10,11... | collective-permute-start | bytes 393224 | tf_op jit(solution)/shard_map/ppermute | solution.py:264
  19.2 1.5 %collective-permute-start.8 = (f32[128,256]{1,0:T(8,128)S(1)}, f32[128,256]{1,0:T(8,128)S(1)}, u32[]{:S(2)}, u32[]{:S(2)}) collective-permute-start(f32[128,256]{1,0:T(8,128)S(1)} %collective-permute-done.7.came_ref), channel_id=1, source_target_pairs={{0,1},{1,0},{2,3},{3,2},{4,5},{5,4},{6,7},{7,6},{8,9},{9,8},{10,11... | collective-permute-start | bytes 393224 | tf_op jit(solution)/shard_map/ppermute | solution.py:264

commit v5 on v4

--- a/solution.py
+++ b/solution.py
@@ -32,11 +32,12 @@
     fetch_hbm,
     tiles_hbm,
     prolong_hbm,
-    keep_outer_ref,
     send_outer_ref,
-    keep_inner_ref,
-    send_inner_ref,
+    outer_ref,
+    local_ref,
+    dense,
     straight_ref,
+    crossed_ref,
     cols,
     count,
     prolong_cols,
@@ -44,13 +45,11 @@
     fetch,
     tiles,
     prolong,
-    dense,
-    whole,
     *rest,
 ):
     slots, (tile_sems, small_sems) = rest[:-2], rest[-2:]
     rows, entries, size, _ = tiles.shape
-    fetched = keep_outer_ref.shape[1] // size
+    fetched = outer_ref.shape[1] // size
     smalls = [
         pltpu.make_async_copy(source, target, small_sems.at[index])
         for index, (source, target) in enumerate(
@@ -88,24 +87,23 @@
             blocks.append(block)
         dense[row * size : (row + 1) * size, :] = jnp.concatenate(blocks, axis=1)
 
-    half = keep_inner_ref.shape[0]
     packed = straight_ref.shape[0] - META
     quarter = size // CG
     line = lax.broadcasted_iota(jnp.int32, (META, CG * size), 0)
     lane = lax.broadcasted_iota(jnp.int32, (META, CG * size), 1)
-    for cross, (ref, first) in enumerate(((straight_ref, 0), (send_inner_ref, half))):
+    for cross, ref in enumerate((straight_ref, crossed_ref)):
         row = fetch[core if cross == 0 else 1 - core]
         meta = jnp.zeros((META, CG * size), jnp.float32)
         for m in range(prolong.shape[1]):
             tile = prolong[row, m]
-            ref[first + m * quarter : first + (m + 1) * quarter, :] = jnp.concatenate(
+            ref[m * quarter : (m + 1) * quarter, :] = jnp.concatenate(
                 [tile[part * quarter : (part + 1) * quarter, :] for part in range(CG)], axis=1
             )
             column = jnp.where(
                 m < prolong_count[row], prolong_cols[row, m] - first_coarse, -1
             ).astype(jnp.float32)
             meta = jnp.where((line == cross) & (lane == m), column, meta)
-        ref[first + packed : first + packed + META, :] = meta
+        ref[packed:, :] = meta
 
     for first in range(0, rows, 2):
         pair = range(first, min(first + 2, rows))
@@ -125,14 +123,22 @@
             axis=0,
         )
 
-    value = dense[...]
+    turned = split(dense[...].T)
+    send_outer_ref[...] = product(turned, split(gathered(rows + (1 - core) * fetched, fetched)))
+    outer_ref[...] = gathered(rows + core * fetched, fetched)
+    local_ref[...] = gathered(0, rows)
+
+
+def middle_kernel(dense_ref, outer_ref, local_ref, outer_keep_ref, keep_ref, send_ref, whole):
+    core = lax.rem(lax.axis_index("inner"), CORES)
+    half = keep_ref.shape[0]
+    value = dense_ref[...]
     turned = split(value.T)
-    keep_outer_ref[...] = product(turned, split(gathered(rows + core * fetched, fetched)))
-    send_outer_ref[...] = product(turned, split(gathered(rows + (1 - core) * fetched, fetched)))
-    local = product(turned, split(gathered(0, rows)))
-    whole[...] = product(split(local), split(value))
-    keep_inner_ref[...] = whole[pl.ds(pl.multiple_of(core * half, half), half), :]
-    send_inner_ref[:half, :] = whole[pl.ds(pl.multiple_of((1 - core) * half, half), half), :]
+    outer_keep_ref[...] = product(turned, split(outer_ref[...]))
+    applied = product(split(local_ref[...]), split(value))
+    whole[...] = product(turned, split(applied))
+    for ref, side in ((keep_ref, core), (send_ref, 1 - core)):
+        ref[...] = whole[pl.ds(pl.multiple_of(side * half, half), half), :]
 
 
 def window_kernel(held_ref, came_ref, *refs):
@@ -166,7 +172,7 @@
     result_ref[...] = product(split(held_ref[...] + came_ref[...]), split(prolong[...]))
 
 
-def store_kernel(other, window_ref, held_ref, came_ref, *refs):
+def store_kernel(other, window_ref, middle_ref, *refs):
     out_hbm, outer, inner, outer_sem, inner_sem = refs[-5:]
     core = lax.rem(lax.axis_index("inner"), CORES)
     owner = 1 - core if other else core
@@ -186,7 +192,7 @@
             copies.append(copy)
 
     store(window_ref[...], outer, 0, owner * 2 * CG, outer_sem)
-    store(held_ref[...] + came_ref[...], inner, owner * (CG // CORES), CG, inner_sem)
+    store(middle_ref[...], inner, owner * (CG // CORES), CG, inner_sem)
     for copy in copies:
         copy.wait()
 
@@ -217,17 +223,18 @@
     packed = prolong_tiles.shape[1] * size // CG
 
     smem = pltpu.SMEM
-    keep_outer, send_outer, keep_inner, send_inner, straight = pl.pallas_call(
+    send_outer, outer, local, dense, straight, crossed = pl.pallas_call(
         left_kernel,
         out_shape=[
             f32(width, fetched * size),
-            f32(width, fetched * size),
-            f32(half, width),
-            f32(half + packed + META, width),
+            f32(rows * size, fetched * size),
+            f32(rows * size, rows * size),
+            f32(rows * size, width),
+            f32(packed + META, width),
             f32(packed + META, width),
         ],
         in_specs=[HBM] * 7,
-        out_specs=[VMEM] * 5,
+        out_specs=[VMEM] * 6,
         scratch_shapes=[
             smem(operator_cols.shape, jnp.int32),
             smem(operator_count.shape, jnp.int32),
@@ -236,8 +243,6 @@
             smem((2,), jnp.int32),
             pltpu.VMEM(operator_tiles.shape, jnp.float32),
             pltpu.VMEM(prolong_tiles.shape, jnp.float32),
-            pltpu.VMEM((rows * size, width), jnp.float32),
-            pltpu.VMEM((width, width), jnp.float32),
         ]
         + [pltpu.VMEM((rows + 2 * fetched + 1, size, size), jnp.float32)] * rows
         + [pltpu.SemaphoreType.DMA((rows,)), pltpu.SemaphoreType.DMA((6,))],
@@ -258,6 +263,16 @@
         )
     )
 
+    keep_outer, keep_inner, send_inner = pl.pallas_call(
+        middle_kernel,
+        out_shape=[f32(width, fetched * size), f32(half, width), f32(half, width)],
+        in_specs=[VMEM] * 3,
+        out_specs=[VMEM] * 3,
+        scratch_shapes=[pltpu.VMEM((width, width), jnp.float32)],
+        compiler_params=PARAMS,
+        name="middle",
+    )(dense, outer, local)
+
     swap_cores = [(i, i ^ 1) for i in range(fetched)]
 
     def other_core(value):
@@ -275,9 +290,7 @@
         return value, came
 
     held_outer, came_outer = chip_sum(keep_outer + other_core(send_outer))
-    arrived = other_core(send_inner)
-
-    crossed = arrived[half:]
+    crossed = other_core(crossed)
     edge = jnp.concatenate(
         [straight[:packed], crossed[:packed], straight[packed:] + crossed[packed:]], axis=0
     )
@@ -291,7 +304,7 @@
                 pairs += [(below, above), (above, below)]
         ghosts.append(lax.ppermute(edge, ("sub", "inner"), pairs))
 
-    held_inner, came_inner = chip_sum(keep_inner + arrived[:half])
+    held_inner, came_inner = chip_sum(keep_inner + other_core(send_inner))
 
     window = pl.pallas_call(
         window_kernel,
@@ -307,7 +320,7 @@
         return pl.pallas_call(
             functools.partial(store_kernel, other),
             out_shape=f32(CG, 3 * CG, size, size),
-            in_specs=[VMEM] * 3 + [HBM] * (len(values) - 3),
+            in_specs=[VMEM] * 2 + [HBM] * (len(values) - 2),
             out_specs=HBM,
             scratch_shapes=[
                 pltpu.VMEM((CG, CG, size, size), jnp.float32),
@@ -315,12 +328,12 @@
                 pltpu.SemaphoreType.DMA((CG,)),
                 pltpu.SemaphoreType.DMA((CG // CORES,)),
             ],
-            input_output_aliases={3: 0} if other else {},
+            input_output_aliases={2: 0} if other else {},
             compiler_params=PARAMS,
             name="store_other" if other else "store_own",
         )(*values)
 
-    own = (window, held_inner, came_inner)
+    own = (window, held_inner + came_inner)
     return store(True, *map(other_core, own), store(False, *own))
 
 

time: 21.9 us -> 21.3 us (0.973)
  waiting for transfers between devices: 4.64 us -> 3.72 us
  Pallas kernels: 6 us -> 6.29 us
    ppermute x5, waiting for transfers between devices: 1.45 us -> 0.01 us  [other_core(): return lax.ppermute(value, 'inner', swap_cores)]
    ppermute x2, waiting for transfers between devices: 0.46 us -> 1.19 us  [chip_sum(): lax.ppermute(value, 'inner', [(i, i ^ step * CORES) for i in range(fetche...]
    pallas_call x1 -> x2, Pallas kernels: 3.43 us -> 3.72 us  [the longest x1 2.84 us: per_device(): pl.pallas_call(left_kernel, out_shape=[f32(width, fetched * size), f32(ro...]
    ppermute x2, waiting for transfers between devices: 2.73 us -> 2.51 us  [per_device(): ghosts.append(lax.ppermute(edge, ('sub', 'inner'), pairs))]
  transfers between devices with their start and end apart: 9 -> 9, of which waited for: 5 -> 3; matrix products, arithmetic and copies ran while one was open for 0% -> 0% of each run, Pallas kernels for 7% -> 12%
where the time goes in v5:
time: 21.3 us; the launch traced here: 21.1 us
  starting transfers between devices  10.9 us (51%)
  Pallas kernels  6.29 us (30%)
  waiting for transfers between devices  3.72 us (17%)
    ppermute x2, starting transfers between devices, per_device(): ghosts.append(lax.ppermute(edge, ('sub', 'inner'), pairs))  6.41 us
    pallas_call x1, Pallas kernels, per_device(): pl.pallas_call(left_kernel, out_shape=[f32(width, fetched * size), f32(ro...  2.84 us
    ppermute x2, starting transfers between devices, chip_sum(): lax.ppermute(value, 'inner', [(i, i ^ step * CORES) for i in range(fetche...  2.62 us
    ppermute x2, waiting for transfers between devices, per_device(): ghosts.append(lax.ppermute(edge, ('sub', 'inner'), pairs))  2.51 us
    pallas_call x2, Pallas kernels, store(): pl.pallas_call(functools.partial(store_kernel, other), out_shape=f32(CG,...  2.01 us
    ppermute x5, starting transfers between devices, other_core(): return lax.ppermute(value, 'inner', swap_cores)  1.89 us
    ppermute x2, waiting for transfers between devices, chip_sum(): lax.ppermute(value, 'inner', [(i, i ^ step * CORES) for i in range(fetche...  1.19 us
    pallas_call x1, Pallas kernels, per_device(): pl.pallas_call(middle_kernel, out_shape=[f32(width, fetched * size), f32(...  0.88 us
  transfers between devices with their start and end apart: 9, of which 3 were waited for; matrix products, arithmetic and copies ran while one was open for 0% of the time, Pallas kernels for 12%

profile of v5, /device:TPU:3, one launch (start us, length us, event | category | flops | bytes accessed | tf_op | source)
XLA Modules:
  0.0 21.1 jit_solution(1204528994960493391)
XLA Ops:
  0.0 2.8 %left.1 = (f32[256,256]{1,0:T(8,128)S(1)}, f32[256,256]{1,0:T(8,128)S(1)}, f32[256,256]{1,0:T(8,128)S(1)}, f32[256,256]{1,0:T(8,128)S(1)}, f32[56,256]{1,0:T(8,128)S(1)}, /*index=5*/f32[56,256]{1,0:T(8,128)S(1)}) custom-call(s32[4,27]{1,0:T(4,128)} %cols_hbm.1, s32[4]{0:T(128)} %count_hbm.1, s32[4,3]{1,0:T(4,128)} %prolong_cols_hbm.1, s32[4]{0:T(128)} %prolong_count_hbm.1, ...), custom_call_target="tpu_custom_call" | custom-call | tf_op jit(solution)/shard_map/left/pallas_call | solution.py:226
  2.8 0.7 %collective-permute-start = (f32[256,256]{1,0:T(8,128)S(1)}, f32[256,256]{1,0:T(8,128)S(1)}, u32[]{:S(2)}, u32[]{:S(2)}) collective-permute-start(f32[256,256]{1,0:T(8,128)S(1)} %get-tuple-element.18), channel_id=1, source_target_pairs={{0,1},{1,0},{2,3},{3,2},{4,5},{5,4},{6,7},{7,6},{8,9},{9,8},{10,11... | collective-permute-start | bytes 786440 | tf_op jit(solution)/shard_map/ppermute | solution.py:279
  3.6 0.1 collective-permute-start.2
  3.7 0.9 %middle.1 = (f32[256,256]{1,0:T(8,128)S(1)}, f32[128,256]{1,0:T(8,128)S(1)}, f32[128,256]{1,0:T(8,128)S(1)}) custom-call(f32[256,256]{1,0:T(8,128)S(1)} %get-tuple-element.14.dense_ref, f32[256,256]{1,0:T(8,128)S(1)} %get-tuple-element.15.outer_ref, f32[256,256]{1,0:T(8,128)S(1)} %get-tuple-element.16.local_ref), custom_call_target="tpu_custom_call" | custom-call | tf_op jit(solution)/shard_map/middle/pallas_call | solution.py:266
  4.6 0.5 %collective-permute-start.6 = (f32[128,256]{1,0:T(8,128)S(1)}, f32[128,256]{1,0:T(8,128)S(1)}, u32[]{:S(2)}, u32[]{:S(2)}) collective-permute-start(f32[128,256]{1,0:T(8,128)S(1)} %get-tuple-element.22), channel_id=1, source_target_pairs={{0,1},{1,0},{2,3},{3,2},{4,5},{5,4},{6,7},{7,6},{8,9},{9,8},{10,11... | collective-permute-start | bytes 393224 | tf_op jit(solution)/shard_map/ppermute | solution.py:279
  5.1 0.0 collective-permute-done
  5.1 1.3 %collective-permute-start.1 = (f32[256,256]{1,0:T(8,128)S(1)}, f32[256,256]{1,0:T(8,128)S(1)}, u32[]{:S(2)}, u32[]{:S(2)}) collective-permute-start(f32[256,256]{1,0:T(8,128)S(1)} %add.12.held_ref), channel_id=1, source_target_pairs={{0,2},{1,3},{2,0},{3,1},{4,6},{5,7},{6,4},{7,5},{8,10},{9,11},{10,... | collective-permute-start | bytes 786440 | tf_op jit(solution)/shard_map/ppermute | solution.py:284
  6.4 0.0 collective-permute-done.2
  6.4 3.3 %collective-permute-start.4 = (f32[104,256]{1,0:T(8,128)S(1)}, f32[104,256]{1,0:T(8,128)S(1)}, u32[]{:S(2)}, u32[]{:S(2)}) collective-permute-start(f32[104,256]{1,0:T(8,128)S(1)} %pad_maximum_fusion), channel_id=1, source_target_pairs={{1,6},{6,1},{3,4},{4,3},{5,10},{10,5},{7,8},{8,7},{9,14},{14,9},{1... | collective-permute-start | bytes 319496 | tf_op jit(solution)/shard_map/ppermute | solution.py:305
  9.8 3.1 %collective-permute-start.3 = (f32[104,256]{1,0:T(8,128)S(1)}, f32[104,256]{1,0:T(8,128)S(1)}, u32[]{:S(2)}, u32[]{:S(2)}) collective-permute-start(f32[104,256]{1,0:T(8,128)S(1)} %pad_maximum_fusion), channel_id=1, source_target_pairs={{1,4},{4,1},{3,6},{6,3},{5,8},{8,5},{7,10},{10,7},{9,12},{12,9},{1... | collective-permute-start | bytes 319496 | tf_op jit(solution)/shard_map/ppermute | solution.py:305
  12.9 0.0 collective-permute-done.6
  12.9 1.3 %collective-permute-start.7 = (f32[128,256]{1,0:T(8,128)S(1)}, f32[128,256]{1,0:T(8,128)S(1)}, u32[]{:S(2)}, u32[]{:S(2)}) collective-permute-start(f32[128,256]{1,0:T(8,128)S(1)} %add.14), channel_id=1, source_target_pairs={{0,2},{1,3},{2,0},{3,1},{4,6},{5,7},{6,4},{7,5},{8,10},{9,11},{10,... | collective-permute-start | bytes 393224 | tf_op jit(solution)/shard_map/ppermute | solution.py:284
  14.2 0.1 collective-permute-done.4.refs_1_
  14.3 2.4 %collective-permute-done.3.refs_0_ = f32[104,256]{1,0:T(8,128)S(1)} collective-permute-done((f32[104,256]{1,0:T(8,128)S(1)}, f32[104,256]{1,0:T(8,128)S(1)}, u32[]{:S(2)}, u32[]{:S(2)}) %collective-permute-start.3) | collective-permute-done | bytes 106528 | tf_op jit(solution)/shard_map/ppermute | solution.py:305
  16.7 0.0 collective-permute-done.1.came_ref
  16.7 0.6 %window.1.window_ref = f32[256,256]{1,0:T(8,128)S(1)} custom-call(f32[256,256]{1,0:T(8,128)S(1)} %add.12.held_ref, f32[256,256]{1,0:T(8,128)S(1)} %collective-permute-done.1.came_ref, f32[104,256]{1,0:T(8,128)S(1)} %collective-permute-done.3.refs_0_, f32[104,256]{1,0:T(8,128)S(1)} %collective-permute-done.4.refs_1_), custom_call_target="tpu_custom_call" | custom-call | tf_op jit(solution)/shard_map/window/pallas_call | solution.py:309
  17.3 0.1 collective-permute-start.5
  17.4 1.2 %collective-permute-done.7 = f32[128,256]{1,0:T(8,128)S(1)} collective-permute-done((f32[128,256]{1,0:T(8,128)S(1)}, f32[128,256]{1,0:T(8,128)S(1)}, u32[]{:S(2)}, u32[]{:S(2)}) %collective-permute-start.7) | collective-permute-done | bytes 131104 | tf_op jit(solution)/shard_map/ppermute | solution.py:284
  18.6 0.5 %collective-permute-start.8 = (f32[128,256]{1,0:T(8,128)S(1)}, f32[128,256]{1,0:T(8,128)S(1)}, u32[]{:S(2)}, u32[]{:S(2)}) collective-permute-start(f32[128,256]{1,0:T(8,128)S(1)} %add.15.middle_ref), channel_id=1, source_target_pairs={{0,1},{1,0},{2,3},{3,2},{4,5},{5,4},{6,7},{7,6},{8,9},{9,8},{10,11... | collective-permute-start | bytes 393224 | tf_op jit(solution)/shard_map/ppermute | solution.py:279
  19.1 1.0 %store_own.1.refs_0_ = f32[4,12,64,64]{3,2,1,0:T(8,128)} custom-call(f32[256,256]{1,0:T(8,128)S(1)} %window.1.window_ref, f32[128,256]{1,0:T(8,128)S(1)} %add.15.middle_ref), custom_call_target="tpu_custom_call" | custom-call | tf_op jit(solution)/shard_map/store_own/pallas_call | solution.py:320
  20.1 0.0 collective-permute-done.8.middle_ref
  20.1 0.0 collective-permute-done.5.window_ref
  20.1 1.0 %store_other.1 = f32[4,12,64,64]{3,2,1,0:T(8,128)} custom-call(f32[256,256]{1,0:T(8,128)S(1)} %collective-permute-done.5.window_ref, f32[128,256]{1,0:T(8,128)S(1)} %collective-permute-done.8.middle_ref, f32[4,12,64,64]{3,2,1,0:T(8,128)} %store_own.1.refs_0_), custom_call_target="tpu_custom_call", output_to_operand_aliasing={{}: (2, {})} | custom-call | tf_op jit(solution)/shard_map/store_other/pallas_call | solution.py:320
  (7 shorter events, 0.1 us)
Async XLA Ops:
  2.8 2.2 %collective-permute-start = (f32[256,256]{1,0:T(8,128)S(1)}, f32[256,256]{1,0:T(8,128)S(1)}, u32[]{:S(2)}, u32[]{:S(2)}) collective-permute-start(f32[256,256]{1,0:T(8,128)S(1)} %get-tuple-element.18), channel_id=1, source_target_pairs={{0,1},{1,0},{2,3},{3,2},{4,5},{5,4},{6,7},{7,6},{8,9},{9,8},{10,11... | collective-permute-start | bytes 786440 | tf_op jit(solution)/shard_map/ppermute | solution.py:279
  3.6 2.8 %collective-permute-start.2 = (f32[56,256]{1,0:T(8,128)S(1)}, f32[56,256]{1,0:T(8,128)S(1)}, u32[]{:S(2)}, u32[]{:S(2)}) collective-permute-start(f32[56,256]{1,0:T(8,128)S(1)} %get-tuple-element.20), channel_id=1, source_target_pairs={{0,1},{1,0},{2,3},{3,2},{4,5},{5,4},{6,7},{7,6},{8,9},{9,8},{10,11... | collective-permute-start | bytes 172040 | tf_op jit(solution)/shard_map/ppermute | solution.py:279
  4.6 8.3 %collective-permute-start.6 = (f32[128,256]{1,0:T(8,128)S(1)}, f32[128,256]{1,0:T(8,128)S(1)}, u32[]{:S(2)}, u32[]{:S(2)}) collective-permute-start(f32[128,256]{1,0:T(8,128)S(1)} %get-tuple-element.22), channel_id=1, source_target_pairs={{0,1},{1,0},{2,3},{3,2},{4,5},{5,4},{6,7},{7,6},{8,9},{9,8},{10,11... | collective-permute-start | bytes 393224 | tf_op jit(solution)/shard_map/ppermute | solution.py:279
  5.1 11.6 %collective-permute-start.1 = (f32[256,256]{1,0:T(8,128)S(1)}, f32[256,256]{1,0:T(8,128)S(1)}, u32[]{:S(2)}, u32[]{:S(2)}) collective-permute-start(f32[256,256]{1,0:T(8,128)S(1)} %add.12.held_ref), channel_id=1, source_target_pairs={{0,2},{1,3},{2,0},{3,1},{4,6},{5,7},{6,4},{7,5},{8,10},{9,11},{10,... | collective-permute-start | bytes 786440 | tf_op jit(solution)/shard_map/ppermute | solution.py:284
  6.4 7.9 %collective-permute-start.4 = (f32[104,256]{1,0:T(8,128)S(1)}, f32[104,256]{1,0:T(8,128)S(1)}, u32[]{:S(2)}, u32[]{:S(2)}) collective-permute-start(f32[104,256]{1,0:T(8,128)S(1)} %pad_maximum_fusion), channel_id=1, source_target_pairs={{1,6},{6,1},{3,4},{4,3},{5,10},{10,5},{7,8},{8,7},{9,14},{14,9},{1... | collective-permute-start | bytes 319496 | tf_op jit(solution)/shard_map/ppermute | solution.py:305
  9.8 6.9 %collective-permute-start.3 = (f32[104,256]{1,0:T(8,128)S(1)}, f32[104,256]{1,0:T(8,128)S(1)}, u32[]{:S(2)}, u32[]{:S(2)}) collective-permute-start(f32[104,256]{1,0:T(8,128)S(1)} %pad_maximum_fusion), channel_id=1, source_target_pairs={{1,4},{4,1},{3,6},{6,3},{5,8},{8,5},{7,10},{10,7},{9,12},{12,9},{1... | collective-permute-start | bytes 319496 | tf_op jit(solution)/shard_map/ppermute | solution.py:305
  12.9 5.6 %collective-permute-start.7 = (f32[128,256]{1,0:T(8,128)S(1)}, f32[128,256]{1,0:T(8,128)S(1)}, u32[]{:S(2)}, u32[]{:S(2)}) collective-permute-start(f32[128,256]{1,0:T(8,128)S(1)} %add.14), channel_id=1, source_target_pairs={{0,2},{1,3},{2,0},{3,1},{4,6},{5,7},{6,4},{7,5},{8,10},{9,11},{10,... | collective-permute-start | bytes 393224 | tf_op jit(solution)/shard_map/ppermute | solution.py:284
  17.3 2.8 %collective-permute-start.5 = (f32[256,256]{1,0:T(8,128)S(1)}, f32[256,256]{1,0:T(8,128)S(1)}, u32[]{:S(2)}, u32[]{:S(2)}) collective-permute-start(f32[256,256]{1,0:T(8,128)S(1)} %window.1.window_ref), channel_id=1, source_target_pairs={{0,1},{1,0},{2,3},{3,2},{4,5},{5,4},{6,7},{7,6},{8,9},{9,8},{10,11... | collective-permute-start | bytes 786440 | tf_op jit(solution)/shard_map/ppermute | solution.py:279
  18.6 1.5 %collective-permute-start.8 = (f32[128,256]{1,0:T(8,128)S(1)}, f32[128,256]{1,0:T(8,128)S(1)}, u32[]{:S(2)}, u32[]{:S(2)}) collective-permute-start(f32[128,256]{1,0:T(8,128)S(1)} %add.15.middle_ref), channel_id=1, source_target_pairs={{0,1},{1,0},{2,3},{3,2},{4,5},{5,4},{6,7},{7,6},{8,9},{9,8},{10,11... | collective-permute-start | bytes 393224 | tf_op jit(solution)/shard_map/ppermute | solution.py:279

commit v6 on v5

--- a/solution.py
+++ b/solution.py
@@ -172,29 +172,42 @@
     result_ref[...] = product(split(held_ref[...] + came_ref[...]), split(prolong[...]))
 
 
-def store_kernel(other, window_ref, middle_ref, *refs):
-    out_hbm, outer, inner, outer_sem, inner_sem = refs[-5:]
+def store_kernel(places, *refs):
+    values, (out_hbm, blocks, sems) = refs[: len(places)], refs[-3:]
     core = lax.rem(lax.axis_index("inner"), CORES)
-    owner = 1 - core if other else core
-    size = outer.shape[-1]
+    size = blocks.shape[-1]
     copies = []
-
-    def store(value, blocks, first_row, first_column, sem):
-        for g in range(blocks.shape[0]):
-            for h in range(blocks.shape[1]):
-                blocks[g, h] = value[g * size : (g + 1) * size, h * size : (h + 1) * size]
+    for value, place in zip(values, places):
+        first_row, first_column = place(core)
+        for g in range(value.shape[0] // size):
+            index = len(copies)
+            for h in range(CG):
+                blocks[index, h] = value[g * size : (g + 1) * size, h * size : (h + 1) * size]
             copy = pltpu.make_async_copy(
-                blocks.at[g],
-                out_hbm.at[first_row + g, pl.ds(first_column, blocks.shape[1])],
-                sem.at[g],
+                blocks.at[index],
+                out_hbm.at[first_row + g, pl.ds(first_column, CG)],
+                sems.at[index],
             )
             copy.start()
             copies.append(copy)
-
-    store(window_ref[...], outer, 0, owner * 2 * CG, outer_sem)
-    store(middle_ref[...], inner, owner * (CG // CORES), CG, inner_sem)
     for copy in copies:
         copy.wait()
+
+
+def outer_place(core):
+    return 0, 2 * CG * core
+
+
+def middle_place(core):
+    return core * (CG // CORES), CG
+
+
+def other_outer_place(core):
+    return outer_place(1 - core)
+
+
+def other_middle_place(core):
+    return middle_place(1 - core)
 
 
 VMEM = pl.BlockSpec(memory_space=pltpu.VMEM)
@@ -302,6 +315,10 @@
                 below = (sub * chips + chip) * CORES + 1
                 above = ((sub + 1) * chips + (shift - chip) % chips) * CORES
                 pairs += [(below, above), (above, below)]
+        first = [CORES * chip for chip in range(chips)]
+        last = [subs * fetched - CORES * (chips - chip) + 1 for chip in range(chips)]
+        if shift == 0:
+            pairs += [*zip(first, last), *zip(last, first)]
         ghosts.append(lax.ppermute(edge, ("sub", "inner"), pairs))
 
     held_inner, came_inner = chip_sum(keep_inner + other_core(send_inner))
@@ -316,25 +333,31 @@
         name="window",
     )(held_outer, came_outer, *ghosts)
 
-    def store(other, *values):
-        return pl.pallas_call(
-            functools.partial(store_kernel, other),
-            out_shape=f32(CG, 3 * CG, size, size),
-            in_specs=[VMEM] * 2 + [HBM] * (len(values) - 2),
-            out_specs=HBM,
-            scratch_shapes=[
-                pltpu.VMEM((CG, CG, size, size), jnp.float32),
-                pltpu.VMEM((CG // CORES, CG, size, size), jnp.float32),
-                pltpu.SemaphoreType.DMA((CG,)),
-                pltpu.SemaphoreType.DMA((CG // CORES,)),
-            ],
-            input_output_aliases={2: 0} if other else {},
-            compiler_params=PARAMS,
-            name="store_other" if other else "store_own",
-        )(*values)
-
-    own = (window, held_inner + came_inner)
-    return store(True, *map(other_core, own), store(False, *own))
+    def store(name, places, values, out=()):
+        rows_stored = sum(value.shape[0] for value in values) // size
+        return (
+            pl.pallas_call(
+                functools.partial(store_kernel, places),
+                out_shape=f32(CG, 3 * CG, size, size),
+                in_specs=[VMEM] * len(values) + [HBM] * len(out),
+                out_specs=HBM,
+                scratch_shapes=[
+                    pltpu.VMEM((rows_stored, CG, size, size), jnp.float32),
+                    pltpu.SemaphoreType.DMA((rows_stored,)),
+                ],
+                input_output_aliases={len(values): 0} if out else {},
+                compiler_params=PARAMS,
+                name=name,
+            )(*values, *out),
+        )
+
+    out = store("store_own", (outer_place,), (window,))
+    came_inner, *out = lax.optimization_barrier((came_inner, *out))
+    middle = held_inner + came_inner
+    out = store(
+        "store_both", (other_outer_place, middle_place), (other_core(window), middle), out
+    )
+    return store("store_other", (other_middle_place,), (other_core(middle),), out)[0]
 
 
 def solution(mesh):

time: 21.3 us -> 21.1 us (level)
  waiting for transfers between devices: 3.72 us -> 2.98 us
  Pallas kernels: 6.29 us -> 6.98 us
    ppermute x2, starting transfers between devices: 6.41 us -> 4.55 us  [per_device(): ghosts.append(lax.ppermute(edge, ('sub', 'inner'), pairs))]
    ppermute x5, starting transfers between devices: 1.89 us -> 3.56 us  [other_core(): return lax.ppermute(value, 'inner', swap_cores)]
    ppermute x2, waiting for transfers between devices: 1.19 us -> 0.35 us  [chip_sum(): lax.ppermute(value, 'inner', [(i, i ^ step * CORES) for i in range(fetche...]
    pallas_call x2 -> x3, Pallas kernels: 2.01 us -> 2.71 us  [store(): pl.pallas_call(functools.partial(store_kernel, places), out_shape=f32(CG,...]
  transfers between devices with their start and end apart: 9 -> 9, of which waited for: 3 -> 3; matrix products, arithmetic and copies ran while one was open for 0% -> 0% of each run, Pallas kernels for 12% -> 16%
where the time goes in v6:
time: 21.1 us; the launch traced here: 20.9 us
  starting transfers between devices  10.8 us (51%)
  Pallas kernels  6.98 us (33%)
  waiting for transfers between devices  2.98 us (14%)
    ppermute x2, starting transfers between devices, per_device(): ghosts.append(lax.ppermute(edge, ('sub', 'inner'), pairs))  4.55 us
    ppermute x5, starting transfers between devices, other_core(): return lax.ppermute(value, 'inner', swap_cores)  3.56 us
    pallas_call x1, Pallas kernels, per_device(): pl.pallas_call(left_kernel, out_shape=[f32(width, fetched * size), f32(ro...  2.84 us
    pallas_call x3, Pallas kernels, store(): pl.pallas_call(functools.partial(store_kernel, places), out_shape=f32(CG,...  2.71 us
    ppermute x2, starting transfers between devices, chip_sum(): lax.ppermute(value, 'inner', [(i, i ^ step * CORES) for i in range(fetche...  2.64 us
    ppermute x2, waiting for transfers between devices, per_device(): ghosts.append(lax.ppermute(edge, ('sub', 'inner'), pairs))  2.62 us
    pallas_call x1, Pallas kernels, per_device(): pl.pallas_call(middle_kernel, out_shape=[f32(width, fetched * size), f32(...  0.88 us
    pallas_call x1, Pallas kernels, per_device(): pl.pallas_call(window_kernel, out_shape=f32(width, width), in_specs=[VMEM...  0.55 us
  transfers between devices with their start and end apart: 9, of which 3 were waited for; matrix products, arithmetic and copies ran while one was open for 0% of the time, Pallas kernels for 16%

profile of v6, /device:TPU:3, one launch (start us, length us, event | category | flops | bytes accessed | tf_op | source)
XLA Modules:
  0.0 20.9 jit_solution(1376331440343263352)
XLA Ops:
  0.0 2.8 %left.1 = (f32[256,256]{1,0:T(8,128)S(1)}, f32[256,256]{1,0:T(8,128)S(1)}, f32[256,256]{1,0:T(8,128)S(1)}, f32[256,256]{1,0:T(8,128)S(1)}, f32[56,256]{1,0:T(8,128)S(1)}, /*index=5*/f32[56,256]{1,0:T(8,128)S(1)}) custom-call(s32[4,27]{1,0:T(4,128)} %cols_hbm.1, s32[4]{0:T(128)} %count_hbm.1, s32[4,3]{1,0:T(4,128)} %prolong_cols_hbm.1, s32[4]{0:T(128)} %prolong_count_hbm.1, ...), custom_call_target="tpu_custom_call" | custom-call | tf_op jit(solution)/shard_map/left/pallas_call | solution.py:239
  2.9 0.7 %collective-permute-start.2 = (f32[256,256]{1,0:T(8,128)S(1)}, f32[256,256]{1,0:T(8,128)S(1)}, u32[]{:S(2)}, u32[]{:S(2)}) collective-permute-start(f32[256,256]{1,0:T(8,128)S(1)} %get-tuple-element.22), channel_id=1, source_target_pairs={{0,1},{1,0},{2,3},{3,2},{4,5},{5,4},{6,7},{7,6},{8,9},{9,8},{10,11... | collective-permute-start | bytes 786440 | tf_op jit(solution)/shard_map/ppermute | solution.py:292
  3.6 0.1 collective-permute-start.4
  3.7 0.9 %middle.1 = (f32[256,256]{1,0:T(8,128)S(1)}, f32[128,256]{1,0:T(8,128)S(1)}, f32[128,256]{1,0:T(8,128)S(1)}) custom-call(f32[256,256]{1,0:T(8,128)S(1)} %get-tuple-element.16.dense_ref, f32[256,256]{1,0:T(8,128)S(1)} %get-tuple-element.17.outer_ref, f32[256,256]{1,0:T(8,128)S(1)} %get-tuple-element.18.local_ref), custom_call_target="tpu_custom_call" | custom-call | tf_op jit(solution)/shard_map/middle/pallas_call | solution.py:279
  4.5 0.5 %collective-permute-start = (f32[128,256]{1,0:T(8,128)S(1)}, f32[128,256]{1,0:T(8,128)S(1)}, u32[]{:S(2)}, u32[]{:S(2)}) collective-permute-start(f32[128,256]{1,0:T(8,128)S(1)} %get-tuple-element.20), channel_id=1, source_target_pairs={{0,1},{1,0},{2,3},{3,2},{4,5},{5,4},{6,7},{7,6},{8,9},{9,8},{10,11... | collective-permute-start | bytes 393224 | tf_op jit(solution)/shard_map/ppermute | solution.py:292
  5.0 0.0 collective-permute-done.2
  5.1 1.3 %collective-permute-start.3 = (f32[256,256]{1,0:T(8,128)S(1)}, f32[256,256]{1,0:T(8,128)S(1)}, u32[]{:S(2)}, u32[]{:S(2)}) collective-permute-start(f32[256,256]{1,0:T(8,128)S(1)} %add.13.held_ref), channel_id=1, source_target_pairs={{0,2},{1,3},{2,0},{3,1},{4,6},{5,7},{6,4},{7,5},{8,10},{9,11},{10,... | collective-permute-start | bytes 786440 | tf_op jit(solution)/shard_map/ppermute | solution.py:297
  6.4 0.0 collective-permute-done.4
  6.4 3.4 %collective-permute-start.6 = (f32[104,256]{1,0:T(8,128)S(1)}, f32[104,256]{1,0:T(8,128)S(1)}, u32[]{:S(2)}, u32[]{:S(2)}) collective-permute-start(f32[104,256]{1,0:T(8,128)S(1)} %pad_maximum_fusion), channel_id=1, source_target_pairs={{1,6},{6,1},{3,4},{4,3},{5,10},{10,5},{7,8},{8,7},{9,14},{14,9},{1... | collective-permute-start | bytes 319496 | tf_op jit(solution)/shard_map/ppermute | solution.py:322
  9.8 1.2 %collective-permute-start.5 = (f32[104,256]{1,0:T(8,128)S(1)}, f32[104,256]{1,0:T(8,128)S(1)}, u32[]{:S(2)}, u32[]{:S(2)}) collective-permute-start(f32[104,256]{1,0:T(8,128)S(1)} %pad_maximum_fusion), channel_id=1, source_target_pairs={{1,4},{4,1},{3,6},{6,3},{5,8},{8,5},{7,10},{10,7},{9,12},{12,9},{1... | collective-permute-start | bytes 319496 | tf_op jit(solution)/shard_map/ppermute | solution.py:322
  11.0 0.0 collective-permute-done
  11.0 1.3 %collective-permute-start.1 = (f32[128,256]{1,0:T(8,128)S(1)}, f32[128,256]{1,0:T(8,128)S(1)}, u32[]{:S(2)}, u32[]{:S(2)}) collective-permute-start(f32[128,256]{1,0:T(8,128)S(1)} %add.12), channel_id=1, source_target_pairs={{0,2},{1,3},{2,0},{3,1},{4,6},{5,7},{6,4},{7,5},{8,10},{9,11},{10,... | collective-permute-start | bytes 393224 | tf_op jit(solution)/shard_map/ppermute | solution.py:297
  12.3 2.1 %collective-permute-done.6.refs_1_ = f32[104,256]{1,0:T(8,128)S(1)} collective-permute-done((f32[104,256]{1,0:T(8,128)S(1)}, f32[104,256]{1,0:T(8,128)S(1)}, u32[]{:S(2)}, u32[]{:S(2)}) %collective-permute-start.6) | collective-permute-done | bytes 106528 | tf_op jit(solution)/shard_map/ppermute | solution.py:322
  14.4 0.5 %collective-permute-done.5.refs_0_ = f32[104,256]{1,0:T(8,128)S(1)} collective-permute-done((f32[104,256]{1,0:T(8,128)S(1)}, f32[104,256]{1,0:T(8,128)S(1)}, u32[]{:S(2)}, u32[]{:S(2)}) %collective-permute-start.5) | collective-permute-done | bytes 106528 | tf_op jit(solution)/shard_map/ppermute | solution.py:322
  15.0 0.3 %collective-permute-done.3.came_ref = f32[256,256]{1,0:T(8,128)S(1)} collective-permute-done((f32[256,256]{1,0:T(8,128)S(1)}, f32[256,256]{1,0:T(8,128)S(1)}, u32[]{:S(2)}, u32[]{:S(2)}) %collective-permute-start.3) | collective-permute-done | bytes 262176 | tf_op jit(solution)/shard_map/ppermute | solution.py:297
  15.3 0.6 %window.1.refs_0_ = f32[256,256]{1,0:T(8,128)S(1)} custom-call(f32[256,256]{1,0:T(8,128)S(1)} %add.13.held_ref, f32[256,256]{1,0:T(8,128)S(1)} %collective-permute-done.3.came_ref, f32[104,256]{1,0:T(8,128)S(1)} %collective-permute-done.5.refs_0_, f32[104,256]{1,0:T(8,128)S(1)} %collective-permute-done.6.refs_1_), custom_call_target="tpu_custom_call" | custom-call | tf_op jit(solution)/shard_map/window/pallas_call | solution.py:326
  15.9 1.4 %collective-permute-start.8 = (f32[256,256]{1,0:T(8,128)S(1)}, f32[256,256]{1,0:T(8,128)S(1)}, u32[]{:S(2)}, u32[]{:S(2)}) collective-permute-start(f32[256,256]{1,0:T(8,128)S(1)} %window.1.refs_0_), channel_id=1, source_target_pairs={{0,1},{1,0},{2,3},{3,2},{4,5},{5,4},{6,7},{7,6},{8,9},{9,8},{10,11... | collective-permute-start | bytes 786440 | tf_op jit(solution)/shard_map/ppermute | solution.py:292
  17.3 0.9 %store_own.1.refs_2_ = f32[4,12,64,64]{3,2,1,0:T(8,128)} custom-call(f32[256,256]{1,0:T(8,128)S(1)} %window.1.refs_0_), custom_call_target="tpu_custom_call" | custom-call | tf_op jit(solution)/shard_map/store_own/pallas_call | solution.py:339
  18.2 0.0 collective-permute-done.1
  18.2 0.9 %collective-permute-start.7 = (f32[128,256]{1,0:T(8,128)S(1)}, f32[128,256]{1,0:T(8,128)S(1)}, u32[]{:S(2)}, u32[]{:S(2)}) collective-permute-start(f32[128,256]{1,0:T(8,128)S(1)} %add.15.refs_1_), channel_id=1, source_target_pairs={{0,1},{1,0},{2,3},{3,2},{4,5},{5,4},{6,7},{7,6},{8,9},{9,8},{10,11... | collective-permute-start | bytes 393224 | tf_op jit(solution)/shard_map/ppermute | solution.py:292
  19.1 0.0 collective-permute-done.8.refs_0_
  19.1 1.0 %store_both.1.refs_1_ = f32[4,12,64,64]{3,2,1,0:T(8,128)} custom-call(f32[256,256]{1,0:T(8,128)S(1)} %collective-permute-done.8.refs_0_, f32[128,256]{1,0:T(8,128)S(1)} %add.15.refs_1_, f32[4,12,64,64]{3,2,1,0:T(8,128)} %store_own.1.refs_2_), custom_call_target="tpu_custom_call", output_to_operand_aliasing={{}: (2, {})} | custom-call | tf_op jit(solution)/shard_map/store_both/pallas_call | solution.py:339
  20.1 0.0 collective-permute-done.7.refs_0_
  20.1 0.8 %store_other.1 = f32[4,12,64,64]{3,2,1,0:T(8,128)} custom-call(f32[128,256]{1,0:T(8,128)S(1)} %collective-permute-done.7.refs_0_, f32[4,12,64,64]{3,2,1,0:T(8,128)} %store_both.1.refs_1_), custom_call_target="tpu_custom_call", output_to_operand_aliasing={{}: (1, {})} | custom-call | tf_op jit(solution)/shard_map/store_other/pallas_call | solution.py:339
  (7 shorter events, 0.1 us)
Async XLA Ops:
  2.9 2.2 %collective-permute-start.2 = (f32[256,256]{1,0:T(8,128)S(1)}, f32[256,256]{1,0:T(8,128)S(1)}, u32[]{:S(2)}, u32[]{:S(2)}) collective-permute-start(f32[256,256]{1,0:T(8,128)S(1)} %get-tuple-element.22), channel_id=1, source_target_pairs={{0,1},{1,0},{2,3},{3,2},{4,5},{5,4},{6,7},{7,6},{8,9},{9,8},{10,11... | collective-permute-start | bytes 786440 | tf_op jit(solution)/shard_map/ppermute | solution.py:292
  3.6 2.8 %collective-permute-start.4 = (f32[56,256]{1,0:T(8,128)S(1)}, f32[56,256]{1,0:T(8,128)S(1)}, u32[]{:S(2)}, u32[]{:S(2)}) collective-permute-start(f32[56,256]{1,0:T(8,128)S(1)} %get-tuple-element.24), channel_id=1, source_target_pairs={{0,1},{1,0},{2,3},{3,2},{4,5},{5,4},{6,7},{7,6},{8,9},{9,8},{10,11... | collective-permute-start | bytes 172040 | tf_op jit(solution)/shard_map/ppermute | solution.py:292
  4.5 6.5 %collective-permute-start = (f32[128,256]{1,0:T(8,128)S(1)}, f32[128,256]{1,0:T(8,128)S(1)}, u32[]{:S(2)}, u32[]{:S(2)}) collective-permute-start(f32[128,256]{1,0:T(8,128)S(1)} %get-tuple-element.20), channel_id=1, source_target_pairs={{0,1},{1,0},{2,3},{3,2},{4,5},{5,4},{6,7},{7,6},{8,9},{9,8},{10,11... | collective-permute-start | bytes 393224 | tf_op jit(solution)/shard_map/ppermute | solution.py:292
  5.1 10.2 %collective-permute-start.3 = (f32[256,256]{1,0:T(8,128)S(1)}, f32[256,256]{1,0:T(8,128)S(1)}, u32[]{:S(2)}, u32[]{:S(2)}) collective-permute-start(f32[256,256]{1,0:T(8,128)S(1)} %add.13.held_ref), channel_id=1, source_target_pairs={{0,2},{1,3},{2,0},{3,1},{4,6},{5,7},{6,4},{7,5},{8,10},{9,11},{10,... | collective-permute-start | bytes 786440 | tf_op jit(solution)/shard_map/ppermute | solution.py:297
  6.4 8.0 %collective-permute-start.6 = (f32[104,256]{1,0:T(8,128)S(1)}, f32[104,256]{1,0:T(8,128)S(1)}, u32[]{:S(2)}, u32[]{:S(2)}) collective-permute-start(f32[104,256]{1,0:T(8,128)S(1)} %pad_maximum_fusion), channel_id=1, source_target_pairs={{1,6},{6,1},{3,4},{4,3},{5,10},{10,5},{7,8},{8,7},{9,14},{14,9},{1... | collective-permute-start | bytes 319496 | tf_op jit(solution)/shard_map/ppermute | solution.py:322
  9.8 5.2 %collective-permute-start.5 = (f32[104,256]{1,0:T(8,128)S(1)}, f32[104,256]{1,0:T(8,128)S(1)}, u32[]{:S(2)}, u32[]{:S(2)}) collective-permute-start(f32[104,256]{1,0:T(8,128)S(1)} %pad_maximum_fusion), channel_id=1, source_target_pairs={{1,4},{4,1},{3,6},{6,3},{5,8},{8,5},{7,10},{10,7},{9,12},{12,9},{1... | collective-permute-start | bytes 319496 | tf_op jit(solution)/shard_map/ppermute | solution.py:322
  11.0 7.1 %collective-permute-start.1 = (f32[128,256]{1,0:T(8,128)S(1)}, f32[128,256]{1,0:T(8,128)S(1)}, u32[]{:S(2)}, u32[]{:S(2)}) collective-permute-start(f32[128,256]{1,0:T(8,128)S(1)} %add.12), channel_id=1, source_target_pairs={{0,2},{1,3},{2,0},{3,1},{4,6},{5,7},{6,4},{7,5},{8,10},{9,11},{10,... | collective-permute-start | bytes 393224 | tf_op jit(solution)/shard_map/ppermute | solution.py:297
  15.9 3.2 %collective-permute-start.8 = (f32[256,256]{1,0:T(8,128)S(1)}, f32[256,256]{1,0:T(8,128)S(1)}, u32[]{:S(2)}, u32[]{:S(2)}) collective-permute-start(f32[256,256]{1,0:T(8,128)S(1)} %window.1.refs_0_), channel_id=1, source_target_pairs={{0,1},{1,0},{2,3},{3,2},{4,5},{5,4},{6,7},{7,6},{8,9},{9,8},{10,11... | collective-permute-start | bytes 786440 | tf_op jit(solution)/shard_map/ppermute | solution.py:292
  18.2 1.9 %collective-permute-start.7 = (f32[128,256]{1,0:T(8,128)S(1)}, f32[128,256]{1,0:T(8,128)S(1)}, u32[]{:S(2)}, u32[]{:S(2)}) collective-permute-start(f32[128,256]{1,0:T(8,128)S(1)} %add.15.refs_1_), channel_id=1, source_target_pairs={{0,1},{1,0},{2,3},{3,2},{4,5},{5,4},{6,7},{7,6},{8,9},{9,8},{10,11... | collective-permute-start | bytes 393224 | tf_op jit(solution)/shard_map/ppermute | solution.py:292

commit v7 on v6

--- a/solution.py
+++ b/solution.py
@@ -10,6 +10,7 @@
 CG = 4
 CORES = 2
 META = 8
+TOGETHER = 2
 VMEM_BYTES = 32 * 1024 * 1024
 
 
@@ -22,6 +23,14 @@
 def product(left, right):
     dot = functools.partial(jnp.dot, preferred_element_type=jnp.float32)
     return dot(left[0], right[0]) + (dot(left[1], right[0]) + dot(left[0], right[1]))
+
+
+def side_of(position):
+    return lax.rem(position + lax.div(position, CORES), CORES)
+
+
+def device_of(chip, side):
+    return chip * CORES + (side + chip) % CORES
 
 
 def left_kernel(
@@ -64,15 +73,19 @@
         )
     ]
     copies = [
-        pltpu.make_async_copy(tiles_hbm.at[row], tiles.at[row], tile_sems.at[row])
-        for row in range(rows)
+        pltpu.make_async_copy(
+            tiles_hbm.at[pl.ds(first, TOGETHER)],
+            tiles.at[pl.ds(first, TOGETHER)],
+            tile_sems.at[first // TOGETHER],
+        )
+        for first in range(0, rows, TOGETHER)
     ]
     for copy in smalls + copies:
         copy.start()
     for ref in slots:
         ref[...] = jnp.zeros_like(ref)
     first_coarse = lax.axis_index("sub") * CG
-    core = lax.rem(lax.axis_index("inner"), CORES)
+    side = side_of(lax.axis_index("inner"))
     for copy in smalls:
         copy.wait()
 
@@ -92,7 +105,7 @@
     line = lax.broadcasted_iota(jnp.int32, (META, CG * size), 0)
     lane = lax.broadcasted_iota(jnp.int32, (META, CG * size), 1)
     for cross, ref in enumerate((straight_ref, crossed_ref)):
-        row = fetch[core if cross == 0 else 1 - core]
+        row = fetch[side if cross == 0 else 1 - side]
         meta = jnp.zeros((META, CG * size), jnp.float32)
         for m in range(prolong.shape[1]):
             tile = prolong[row, m]
@@ -105,10 +118,9 @@
             meta = jnp.where((line == cross) & (lane == m), column, meta)
         ref[packed:, :] = meta
 
-    for first in range(0, rows, 2):
-        pair = range(first, min(first + 2, rows))
-        for row in pair:
-            copies[row].wait()
+    for copy, first in zip(copies, range(0, rows, TOGETHER)):
+        pair = range(first, first + TOGETHER)
+        copy.wait()
         for entry in range(entries):
             for row in pair:
                 slot = jnp.where(entry < count[row], cols[row, entry], rows + 2 * fetched)
@@ -124,34 +136,35 @@
         )
 
     turned = split(dense[...].T)
-    send_outer_ref[...] = product(turned, split(gathered(rows + (1 - core) * fetched, fetched)))
-    outer_ref[...] = gathered(rows + core * fetched, fetched)
+    send_outer_ref[...] = product(turned, split(gathered(rows + (1 - side) * fetched, fetched)))
+    outer_ref[...] = gathered(rows + side * fetched, fetched)
     local_ref[...] = gathered(0, rows)
 
 
 def middle_kernel(dense_ref, outer_ref, local_ref, outer_keep_ref, keep_ref, send_ref, whole):
-    core = lax.rem(lax.axis_index("inner"), CORES)
+    side = side_of(lax.axis_index("inner"))
     half = keep_ref.shape[0]
     value = dense_ref[...]
     turned = split(value.T)
     outer_keep_ref[...] = product(turned, split(outer_ref[...]))
     applied = product(split(local_ref[...]), split(value))
     whole[...] = product(turned, split(applied))
-    for ref, side in ((keep_ref, core), (send_ref, 1 - core)):
-        ref[...] = whole[pl.ds(pl.multiple_of(side * half, half), half), :]
+    for ref, owner in ((keep_ref, side), (send_ref, 1 - side)):
+        ref[...] = whole[pl.ds(pl.multiple_of(owner * half, half), half), :]
 
 
 def window_kernel(held_ref, came_ref, *refs):
     ghosts, result_ref, prolong = refs[:-2], refs[-2], refs[-1]
     position = lax.axis_index("inner")
-    core, chip = lax.rem(position, CORES), lax.div(position, CORES)
+    side, chip = side_of(position), lax.div(position, CORES)
     chips = len(ghosts)
     size = result_ref.shape[0] // CG
     quarter = size // CG
     packed = (ghosts[0].shape[0] - META) // CORES
     for shift, ghost in enumerate(ghosts):
         for cross in range(CORES):
-            source = lax.rem(shift - chip + chips, chips) * CORES + lax.rem(1 - core + cross, CORES)
+            there = lax.rem(shift - chip + chips, chips)
+            source = there * CORES + lax.rem(1 - side + there + cross, CORES)
             blocks = [None] * CG
             for m in range(packed // quarter):
                 first = cross * packed + m * quarter
@@ -174,11 +187,11 @@
 
 def store_kernel(places, *refs):
     values, (out_hbm, blocks, sems) = refs[: len(places)], refs[-3:]
-    core = lax.rem(lax.axis_index("inner"), CORES)
+    side = side_of(lax.axis_index("inner"))
     size = blocks.shape[-1]
     copies = []
     for value, place in zip(values, places):
-        first_row, first_column = place(core)
+        first_row, first_column = place(side)
         for g in range(value.shape[0] // size):
             index = len(copies)
             for h in range(CG):
@@ -194,20 +207,20 @@
         copy.wait()
 
 
-def outer_place(core):
-    return 0, 2 * CG * core
-
-
-def middle_place(core):
-    return core * (CG // CORES), CG
-
-
-def other_outer_place(core):
-    return outer_place(1 - core)
-
-
-def other_middle_place(core):
-    return middle_place(1 - core)
+def outer_place(side):
+    return 0, 2 * CG * side
+
+
+def middle_place(side):
+    return side * (CG // CORES), CG
+
+
+def other_outer_place(side):
+    return outer_place(1 - side)
+
+
+def other_middle_place(side):
+    return middle_place(1 - side)
 
 
 VMEM = pl.BlockSpec(memory_space=pltpu.VMEM)
@@ -294,9 +307,12 @@
     def chip_sum(value):
         step = 1
         while step < chips:
-            came = lax.ppermute(
-                value, "inner", [(i, i ^ (step * CORES)) for i in range(fetched)]
-            )
+            pairs = [
+                (device_of(chip, side), device_of(chip ^ step, side))
+                for chip in range(chips)
+                for side in range(CORES)
+            ]
+            came = lax.ppermute(value, "inner", pairs)
             step *= 2
             if step < chips:
                 value = value + came
@@ -312,11 +328,11 @@
         pairs = []
         for sub in range(subs - 1):
             for chip in range(chips):
-                below = (sub * chips + chip) * CORES + 1
-                above = ((sub + 1) * chips + (shift - chip) % chips) * CORES
+                below = sub * fetched + device_of(chip, 1)
+                above = (sub + 1) * fetched + device_of((shift - chip) % chips, 0)
                 pairs += [(below, above), (above, below)]
-        first = [CORES * chip for chip in range(chips)]
-        last = [subs * fetched - CORES * (chips - chip) + 1 for chip in range(chips)]
+        first = [device_of(chip, 0) for chip in range(chips)]
+        last = [(subs - 1) * fetched + device_of(chip, 1) for chip in range(chips)]
         if shift == 0:
             pairs += [*zip(first, last), *zip(last, first)]
         ghosts.append(lax.ppermute(edge, ("sub", "inner"), pairs))

time: 21.1 us -> 20.8 us (0.986)
  starting transfers between devices: 10.8 us -> 9.53 us
  waiting for transfers between devices: 2.98 us -> 3.87 us
    ppermute x5, starting transfers between devices: 3.56 us -> 2.39 us  [other_core(): return lax.ppermute(value, 'inner', swap_cores)]
    ppermute x2, waiting for transfers between devices: 0.35 us -> 0.88 us  [chip_sum(): came = lax.ppermute(value, 'inner', pairs)]
    ppermute x2, starting transfers between devices: 2.64 us -> 2.26 us  [chip_sum(): came = lax.ppermute(value, 'inner', pairs)]
    ppermute x2, starting transfers between devices: 4.55 us -> 4.88 us  [per_device(): ghosts.append(lax.ppermute(edge, ('sub', 'inner'), pairs))]
  transfers between devices with their start and end apart: 9 -> 9, of which waited for: 3 -> 4; matrix products, arithmetic and copies ran while one was open for 0% -> 0% of each run, Pallas kernels for 16% -> 16%
where the time goes in v7:
time: 20.8 us; the launch traced here: 20.5 us
  starting transfers between devices  9.53 us (46%)
  Pallas kernels  6.94 us (33%)
  waiting for transfers between devices  3.87 us (19%)
    ppermute x2, starting transfers between devices, per_device(): ghosts.append(lax.ppermute(edge, ('sub', 'inner'), pairs))  4.88 us
    pallas_call x1, Pallas kernels, per_device(): pl.pallas_call(left_kernel, out_shape=[f32(width, fetched * size), f32(ro...  2.8 us
    ppermute x2, waiting for transfers between devices, per_device(): ghosts.append(lax.ppermute(edge, ('sub', 'inner'), pairs))  2.77 us
    pallas_call x3, Pallas kernels, store(): pl.pallas_call(functools.partial(store_kernel, places), out_shape=f32(CG,...  2.7 us
    ppermute x5, starting transfers between devices, other_core(): return lax.ppermute(value, 'inner', swap_cores)  2.39 us
    ppermute x2, starting transfers between devices, chip_sum(): came = lax.ppermute(value, 'inner', pairs)  2.26 us
    ppermute x2, waiting for transfers between devices, chip_sum(): came = lax.ppermute(value, 'inner', pairs)  0.88 us
    pallas_call x1, Pallas kernels, per_device(): pl.pallas_call(middle_kernel, out_shape=[f32(width, fetched * size), f32(...  0.88 us
  transfers between devices with their start and end apart: 9, of which 4 were waited for; matrix products, arithmetic and copies ran while one was open for 0% of the time, Pallas kernels for 16%

profile of v7, /device:TPU:3, one launch (start us, length us, event | category | flops | bytes accessed | tf_op | source)
XLA Modules:
  0.0 20.5 jit_solution(16494349798537008946)
XLA Ops:
  0.0 2.8 %left.1 = (f32[256,256]{1,0:T(8,128)S(1)}, f32[256,256]{1,0:T(8,128)S(1)}, f32[256,256]{1,0:T(8,128)S(1)}, f32[256,256]{1,0:T(8,128)S(1)}, f32[56,256]{1,0:T(8,128)S(1)}, /*index=5*/f32[56,256]{1,0:T(8,128)S(1)}) custom-call(s32[4,27]{1,0:T(4,128)} %cols_hbm.1, s32[4]{0:T(128)} %count_hbm.1, s32[4,3]{1,0:T(4,128)} %prolong_cols_hbm.1, s32[4]{0:T(128)} %prolong_count_hbm.1, ...), custom_call_target="tpu_custom_call" | custom-call | tf_op jit(solution)/shard_map/left/pallas_call | solution.py:252
  2.8 0.7 %collective-permute-start.2 = (f32[256,256]{1,0:T(8,128)S(1)}, f32[256,256]{1,0:T(8,128)S(1)}, u32[]{:S(2)}, u32[]{:S(2)}) collective-permute-start(f32[256,256]{1,0:T(8,128)S(1)} %get-tuple-element.22), channel_id=1, source_target_pairs={{0,1},{1,0},{2,3},{3,2},{4,5},{5,4},{6,7},{7,6},{8,9},{9,8},{10,11... | collective-permute-start | bytes 786440 | tf_op jit(solution)/shard_map/ppermute | solution.py:305
  3.5 0.1 collective-permute-start.4
  3.6 0.9 %middle.1 = (f32[256,256]{1,0:T(8,128)S(1)}, f32[128,256]{1,0:T(8,128)S(1)}, f32[128,256]{1,0:T(8,128)S(1)}) custom-call(f32[256,256]{1,0:T(8,128)S(1)} %get-tuple-element.16.dense_ref, f32[256,256]{1,0:T(8,128)S(1)} %get-tuple-element.17.outer_ref, f32[256,256]{1,0:T(8,128)S(1)} %get-tuple-element.18.local_ref), custom_call_target="tpu_custom_call" | custom-call | tf_op jit(solution)/shard_map/middle/pallas_call | solution.py:292
  4.5 0.5 %collective-permute-start = (f32[128,256]{1,0:T(8,128)S(1)}, f32[128,256]{1,0:T(8,128)S(1)}, u32[]{:S(2)}, u32[]{:S(2)}) collective-permute-start(f32[128,256]{1,0:T(8,128)S(1)} %get-tuple-element.20), channel_id=1, source_target_pairs={{0,1},{1,0},{2,3},{3,2},{4,5},{5,4},{6,7},{7,6},{8,9},{9,8},{10,11... | collective-permute-start | bytes 393224 | tf_op jit(solution)/shard_map/ppermute | solution.py:305
  5.0 0.0 collective-permute-done.2
  5.0 1.3 %collective-permute-start.3 = (f32[256,256]{1,0:T(8,128)S(1)}, f32[256,256]{1,0:T(8,128)S(1)}, u32[]{:S(2)}, u32[]{:S(2)}) collective-permute-start(f32[256,256]{1,0:T(8,128)S(1)} %add.13.held_ref), channel_id=1, source_target_pairs={{0,3},{1,2},{3,0},{2,1},{4,7},{5,6},{7,4},{6,5},{8,11},{9,10},{11,... | collective-permute-start | bytes 786440 | tf_op jit(solution)/shard_map/ppermute | solution.py:315
  6.3 0.0 collective-permute-done.4
  6.4 3.1 %collective-permute-start.6 = (f32[104,256]{1,0:T(8,128)S(1)}, f32[104,256]{1,0:T(8,128)S(1)}, u32[]{:S(2)}, u32[]{:S(2)}) collective-permute-start(f32[104,256]{1,0:T(8,128)S(1)} %pad_maximum_fusion), channel_id=1, source_target_pairs={{1,7},{7,1},{2,4},{4,2},{5,11},{11,5},{6,8},{8,6},{9,15},{15,9},{1... | collective-permute-start | bytes 319496 | tf_op jit(solution)/shard_map/ppermute | solution.py:338
  9.5 1.8 %collective-permute-start.5 = (f32[104,256]{1,0:T(8,128)S(1)}, f32[104,256]{1,0:T(8,128)S(1)}, u32[]{:S(2)}, u32[]{:S(2)}) collective-permute-start(f32[104,256]{1,0:T(8,128)S(1)} %pad_maximum_fusion), channel_id=1, source_target_pairs={{1,4},{4,1},{2,7},{7,2},{5,8},{8,5},{6,11},{11,6},{9,12},{12,9},{1... | collective-permute-start | bytes 319496 | tf_op jit(solution)/shard_map/ppermute | solution.py:338
  11.2 0.0 collective-permute-done
  11.3 1.0 %collective-permute-start.1 = (f32[128,256]{1,0:T(8,128)S(1)}, f32[128,256]{1,0:T(8,128)S(1)}, u32[]{:S(2)}, u32[]{:S(2)}) collective-permute-start(f32[128,256]{1,0:T(8,128)S(1)} %add.12), channel_id=1, source_target_pairs={{0,3},{1,2},{3,0},{2,1},{4,7},{5,6},{7,4},{6,5},{8,11},{9,10},{11,... | collective-permute-start | bytes 393224 | tf_op jit(solution)/shard_map/ppermute | solution.py:315
  12.3 1.5 %collective-permute-done.6.refs_1_ = f32[104,256]{1,0:T(8,128)S(1)} collective-permute-done((f32[104,256]{1,0:T(8,128)S(1)}, f32[104,256]{1,0:T(8,128)S(1)}, u32[]{:S(2)}, u32[]{:S(2)}) %collective-permute-start.6) | collective-permute-done | bytes 106528 | tf_op jit(solution)/shard_map/ppermute | solution.py:338
  13.8 1.2 %collective-permute-done.5.refs_0_ = f32[104,256]{1,0:T(8,128)S(1)} collective-permute-done((f32[104,256]{1,0:T(8,128)S(1)}, f32[104,256]{1,0:T(8,128)S(1)}, u32[]{:S(2)}, u32[]{:S(2)}) %collective-permute-start.5) | collective-permute-done | bytes 106528 | tf_op jit(solution)/shard_map/ppermute | solution.py:338
  15.0 0.9 %collective-permute-done.3.came_ref = f32[256,256]{1,0:T(8,128)S(1)} collective-permute-done((f32[256,256]{1,0:T(8,128)S(1)}, f32[256,256]{1,0:T(8,128)S(1)}, u32[]{:S(2)}, u32[]{:S(2)}) %collective-permute-start.3) | collective-permute-done | bytes 262176 | tf_op jit(solution)/shard_map/ppermute | solution.py:315
  15.9 0.5 %window.1.refs_0_ = f32[256,256]{1,0:T(8,128)S(1)} custom-call(f32[256,256]{1,0:T(8,128)S(1)} %add.13.held_ref, f32[256,256]{1,0:T(8,128)S(1)} %collective-permute-done.3.came_ref, f32[104,256]{1,0:T(8,128)S(1)} %collective-permute-done.5.refs_0_, f32[104,256]{1,0:T(8,128)S(1)} %collective-permute-done.6.refs_1_), custom_call_target="tpu_custom_call" | custom-call | tf_op jit(solution)/shard_map/window/pallas_call | solution.py:342
  16.5 0.9 %collective-permute-start.8 = (f32[256,256]{1,0:T(8,128)S(1)}, f32[256,256]{1,0:T(8,128)S(1)}, u32[]{:S(2)}, u32[]{:S(2)}) collective-permute-start(f32[256,256]{1,0:T(8,128)S(1)} %window.1.refs_0_), channel_id=1, source_target_pairs={{0,1},{1,0},{2,3},{3,2},{4,5},{5,4},{6,7},{7,6},{8,9},{9,8},{10,11... | collective-permute-start | bytes 786440 | tf_op jit(solution)/shard_map/ppermute | solution.py:305
  17.4 0.9 %store_own.1.refs_2_ = f32[4,12,64,64]{3,2,1,0:T(8,128)} custom-call(f32[256,256]{1,0:T(8,128)S(1)} %window.1.refs_0_), custom_call_target="tpu_custom_call" | custom-call | tf_op jit(solution)/shard_map/store_own/pallas_call | solution.py:355
  18.3 0.0 collective-permute-done.1
  18.3 0.2 collective-permute-start.7
  18.5 0.0 collective-permute-done.8.refs_0_
  18.5 1.0 %store_both.1.refs_1_ = f32[4,12,64,64]{3,2,1,0:T(8,128)} custom-call(f32[256,256]{1,0:T(8,128)S(1)} %collective-permute-done.8.refs_0_, f32[128,256]{1,0:T(8,128)S(1)} %add.15.refs_1_, f32[4,12,64,64]{3,2,1,0:T(8,128)} %store_own.1.refs_2_), custom_call_target="tpu_custom_call", output_to_operand_aliasing={{}: (2, {})} | custom-call | tf_op jit(solution)/shard_map/store_both/pallas_call | solution.py:355
  19.5 0.2 collective-permute-done.7.refs_0_
  19.7 0.8 %store_other.1 = f32[4,12,64,64]{3,2,1,0:T(8,128)} custom-call(f32[128,256]{1,0:T(8,128)S(1)} %collective-permute-done.7.refs_0_, f32[4,12,64,64]{3,2,1,0:T(8,128)} %store_both.1.refs_1_), custom_call_target="tpu_custom_call", output_to_operand_aliasing={{}: (1, {})} | custom-call | tf_op jit(solution)/shard_map/store_other/pallas_call | solution.py:355
  (7 shorter events, 0.1 us)
Async XLA Ops:
  2.8 2.2 %collective-permute-start.2 = (f32[256,256]{1,0:T(8,128)S(1)}, f32[256,256]{1,0:T(8,128)S(1)}, u32[]{:S(2)}, u32[]{:S(2)}) collective-permute-start(f32[256,256]{1,0:T(8,128)S(1)} %get-tuple-element.22), channel_id=1, source_target_pairs={{0,1},{1,0},{2,3},{3,2},{4,5},{5,4},{6,7},{7,6},{8,9},{9,8},{10,11... | collective-permute-start | bytes 786440 | tf_op jit(solution)/shard_map/ppermute | solution.py:305
  3.5 2.8 %collective-permute-start.4 = (f32[56,256]{1,0:T(8,128)S(1)}, f32[56,256]{1,0:T(8,128)S(1)}, u32[]{:S(2)}, u32[]{:S(2)}) collective-permute-start(f32[56,256]{1,0:T(8,128)S(1)} %get-tuple-element.24), channel_id=1, source_target_pairs={{0,1},{1,0},{2,3},{3,2},{4,5},{5,4},{6,7},{7,6},{8,9},{9,8},{10,11... | collective-permute-start | bytes 172040 | tf_op jit(solution)/shard_map/ppermute | solution.py:305
  4.5 6.7 %collective-permute-start = (f32[128,256]{1,0:T(8,128)S(1)}, f32[128,256]{1,0:T(8,128)S(1)}, u32[]{:S(2)}, u32[]{:S(2)}) collective-permute-start(f32[128,256]{1,0:T(8,128)S(1)} %get-tuple-element.20), channel_id=1, source_target_pairs={{0,1},{1,0},{2,3},{3,2},{4,5},{5,4},{6,7},{7,6},{8,9},{9,8},{10,11... | collective-permute-start | bytes 393224 | tf_op jit(solution)/shard_map/ppermute | solution.py:305
  5.0 10.9 %collective-permute-start.3 = (f32[256,256]{1,0:T(8,128)S(1)}, f32[256,256]{1,0:T(8,128)S(1)}, u32[]{:S(2)}, u32[]{:S(2)}) collective-permute-start(f32[256,256]{1,0:T(8,128)S(1)} %add.13.held_ref), channel_id=1, source_target_pairs={{0,3},{1,2},{3,0},{2,1},{4,7},{5,6},{7,4},{6,5},{8,11},{9,10},{11,... | collective-permute-start | bytes 786440 | tf_op jit(solution)/shard_map/ppermute | solution.py:315
  6.4 7.4 %collective-permute-start.6 = (f32[104,256]{1,0:T(8,128)S(1)}, f32[104,256]{1,0:T(8,128)S(1)}, u32[]{:S(2)}, u32[]{:S(2)}) collective-permute-start(f32[104,256]{1,0:T(8,128)S(1)} %pad_maximum_fusion), channel_id=1, source_target_pairs={{1,7},{7,1},{2,4},{4,2},{5,11},{11,5},{6,8},{8,6},{9,15},{15,9},{1... | collective-permute-start | bytes 319496 | tf_op jit(solution)/shard_map/ppermute | solution.py:338
  9.5 5.5 %collective-permute-start.5 = (f32[104,256]{1,0:T(8,128)S(1)}, f32[104,256]{1,0:T(8,128)S(1)}, u32[]{:S(2)}, u32[]{:S(2)}) collective-permute-start(f32[104,256]{1,0:T(8,128)S(1)} %pad_maximum_fusion), channel_id=1, source_target_pairs={{1,4},{4,1},{2,7},{7,2},{5,8},{8,5},{6,11},{11,6},{9,12},{12,9},{1... | collective-permute-start | bytes 319496 | tf_op jit(solution)/shard_map/ppermute | solution.py:338
  11.3 7.0 %collective-permute-start.1 = (f32[128,256]{1,0:T(8,128)S(1)}, f32[128,256]{1,0:T(8,128)S(1)}, u32[]{:S(2)}, u32[]{:S(2)}) collective-permute-start(f32[128,256]{1,0:T(8,128)S(1)} %add.12), channel_id=1, source_target_pairs={{0,3},{1,2},{3,0},{2,1},{4,7},{5,6},{7,4},{6,5},{8,11},{9,10},{11,... | collective-permute-start | bytes 393224 | tf_op jit(solution)/shard_map/ppermute | solution.py:315
  16.5 2.1 %collective-permute-start.8 = (f32[256,256]{1,0:T(8,128)S(1)}, f32[256,256]{1,0:T(8,128)S(1)}, u32[]{:S(2)}, u32[]{:S(2)}) collective-permute-start(f32[256,256]{1,0:T(8,128)S(1)} %window.1.refs_0_), channel_id=1, source_target_pairs={{0,1},{1,0},{2,3},{3,2},{4,5},{5,4},{6,7},{7,6},{8,9},{9,8},{10,11... | collective-permute-start | bytes 786440 | tf_op jit(solution)/shard_map/ppermute | solution.py:305
  18.3 1.4 %collective-permute-start.7 = (f32[128,256]{1,0:T(8,128)S(1)}, f32[128,256]{1,0:T(8,128)S(1)}, u32[]{:S(2)}, u32[]{:S(2)}) collective-permute-start(f32[128,256]{1,0:T(8,128)S(1)} %add.15.refs_1_), channel_id=1, source_target_pairs={{0,1},{1,0},{2,3},{3,2},{4,5},{5,4},{6,7},{7,6},{8,9},{9,8},{10,11... | collective-permute-start | bytes 393224 | tf_op jit(solution)/shard_map/ppermute | solution.py:305

commit v8 on v7

--- a/solution.py
+++ b/solution.py
@@ -333,10 +333,11 @@
                 pairs += [(below, above), (above, below)]
         first = [device_of(chip, 0) for chip in range(chips)]
         last = [(subs - 1) * fetched + device_of(chip, 1) for chip in range(chips)]
-        if shift == 0:
+        if shift > 0:
             pairs += [*zip(first, last), *zip(last, first)]
         ghosts.append(lax.ppermute(edge, ("sub", "inner"), pairs))
 
+    send_inner, held_outer = lax.optimization_barrier((send_inner, held_outer))
     held_inner, came_inner = chip_sum(keep_inner + other_core(send_inner))
 
     window = pl.pallas_call(

time: 20.8 us -> 20.7 us (level)
  starting transfers between devices: 9.53 us -> 8.94 us
  waiting for transfers between devices: 3.87 us -> 4.41 us
    ppermute x2, waiting for transfers between devices: 0.88 us -> 1.92 us  [chip_sum(): came = lax.ppermute(value, 'inner', pairs)]
    ppermute x5, starting transfers between devices: 2.39 us -> 1.52 us  [other_core(): return lax.ppermute(value, 'inner', swap_cores)]
    ppermute x2, waiting for transfers between devices: 2.77 us -> 2.29 us  [per_device(): ghosts.append(lax.ppermute(edge, ('sub', 'inner'), pairs))]
    ppermute x2, starting transfers between devices: 2.26 us -> 2.61 us  [chip_sum(): came = lax.ppermute(value, 'inner', pairs)]
where the time goes in v8:
time: 20.7 us; the launch traced here: 20.5 us
  starting transfers between devices  8.94 us (43%)
  Pallas kernels  6.95 us (34%)
  waiting for transfers between devices  4.41 us (21%)
    ppermute x2, starting transfers between devices, per_device(): ghosts.append(lax.ppermute(edge, ('sub', 'inner'), pairs))  4.81 us
    pallas_call x1, Pallas kernels, per_device(): pl.pallas_call(left_kernel, out_shape=[f32(width, fetched * size), f32(ro...  2.81 us
    pallas_call x3, Pallas kernels, store(): pl.pallas_call(functools.partial(store_kernel, places), out_shape=f32(CG,...  2.71 us
    ppermute x2, starting transfers between devices, chip_sum(): came = lax.ppermute(value, 'inner', pairs)  2.61 us
    ppermute x2, waiting for transfers between devices, per_device(): ghosts.append(lax.ppermute(edge, ('sub', 'inner'), pairs))  2.29 us
    ppermute x2, waiting for transfers between devices, chip_sum(): came = lax.ppermute(value, 'inner', pairs)  1.92 us
    ppermute x5, starting transfers between devices, other_core(): return lax.ppermute(value, 'inner', swap_cores)  1.52 us
    pallas_call x1, Pallas kernels, per_device(): pl.pallas_call(middle_kernel, out_shape=[f32(width, fetched * size), f32(...  0.88 us
  transfers between devices with their start and end apart: 9, of which 4 were waited for; matrix products, arithmetic and copies ran while one was open for 0% of the time, Pallas kernels for 16%

profile of v8, /device:TPU:3, one launch (start us, length us, event | category | flops | bytes accessed | tf_op | source)
XLA Modules:
  0.0 20.5 jit_solution(17112548469101652066)
XLA Ops:
  0.0 2.8 %left.1 = (f32[256,256]{1,0:T(8,128)S(1)}, f32[256,256]{1,0:T(8,128)S(1)}, f32[256,256]{1,0:T(8,128)S(1)}, f32[256,256]{1,0:T(8,128)S(1)}, f32[56,256]{1,0:T(8,128)S(1)}, /*index=5*/f32[56,256]{1,0:T(8,128)S(1)}) custom-call(s32[4,27]{1,0:T(4,128)} %cols_hbm.1, s32[4]{0:T(128)} %count_hbm.1, s32[4,3]{1,0:T(4,128)} %prolong_cols_hbm.1, s32[4]{0:T(128)} %prolong_count_hbm.1, ...), custom_call_target="tpu_custom_call" | custom-call | tf_op jit(solution)/shard_map/left/pallas_call | solution.py:252
  2.8 0.7 %collective-permute-start = (f32[256,256]{1,0:T(8,128)S(1)}, f32[256,256]{1,0:T(8,128)S(1)}, u32[]{:S(2)}, u32[]{:S(2)}) collective-permute-start(f32[256,256]{1,0:T(8,128)S(1)} %get-tuple-element.24), channel_id=1, source_target_pairs={{0,1},{1,0},{2,3},{3,2},{4,5},{5,4},{6,7},{7,6},{8,9},{9,8},{10,11... | collective-permute-start | bytes 786440 | tf_op jit(solution)/shard_map/ppermute | solution.py:305
  3.5 0.1 collective-permute-start.4
  3.6 0.9 %middle.1 = (f32[256,256]{1,0:T(8,128)S(1)}, f32[128,256]{1,0:T(8,128)S(1)}, f32[128,256]{1,0:T(8,128)S(1)}) custom-call(f32[256,256]{1,0:T(8,128)S(1)} %get-tuple-element.18.dense_ref, f32[256,256]{1,0:T(8,128)S(1)} %get-tuple-element.19.outer_ref, f32[256,256]{1,0:T(8,128)S(1)} %get-tuple-element.20.local_ref), custom_call_target="tpu_custom_call" | custom-call | tf_op jit(solution)/shard_map/middle/pallas_call | solution.py:292
  4.5 0.2 collective-permute-done
  4.7 1.6 %collective-permute-start.3 = (f32[256,256]{1,0:T(8,128)S(1)}, f32[256,256]{1,0:T(8,128)S(1)}, u32[]{:S(2)}, u32[]{:S(2)}) collective-permute-start(f32[256,256]{1,0:T(8,128)S(1)} %add.12.held_ref), channel_id=1, source_target_pairs={{0,3},{1,2},{3,0},{2,1},{4,7},{5,6},{7,4},{6,5},{8,11},{9,10},{11,... | collective-permute-start | bytes 786440 | tf_op jit(solution)/shard_map/ppermute | solution.py:315
  6.3 0.0 collective-permute-done.4
  6.3 0.2 collective-permute-start.1
  6.5 1.3 %collective-permute-start.6 = (f32[104,256]{1,0:T(8,128)S(1)}, f32[104,256]{1,0:T(8,128)S(1)}, u32[]{:S(2)}, u32[]{:S(2)}) collective-permute-start(f32[104,256]{1,0:T(8,128)S(1)} %pad_maximum_fusion), channel_id=1, source_target_pairs={{1,7},{7,1},{2,4},{4,2},{5,11},{11,5},{6,8},{8,6},{9,15},{15,9},{1... | collective-permute-start | bytes 319496 | tf_op jit(solution)/shard_map/ppermute | solution.py:338
  7.8 3.5 %collective-permute-start.5 = (f32[104,256]{1,0:T(8,128)S(1)}, f32[104,256]{1,0:T(8,128)S(1)}, u32[]{:S(2)}, u32[]{:S(2)}) collective-permute-start(f32[104,256]{1,0:T(8,128)S(1)} %pad_maximum_fusion), channel_id=1, source_target_pairs={{1,4},{4,1},{2,7},{7,2},{5,8},{8,5},{6,11},{11,6},{9,12},{12,9},{1... | collective-permute-start | bytes 319496 | tf_op jit(solution)/shard_map/ppermute | solution.py:338
  11.4 0.0 collective-permute-done.1
  11.4 1.0 %collective-permute-start.2 = (f32[128,256]{1,0:T(8,128)S(1)}, f32[128,256]{1,0:T(8,128)S(1)}, u32[]{:S(2)}, u32[]{:S(2)}) collective-permute-start(f32[128,256]{1,0:T(8,128)S(1)} %add.13), channel_id=1, source_target_pairs={{0,3},{1,2},{3,0},{2,1},{4,7},{5,6},{7,4},{6,5},{8,11},{9,10},{11,... | collective-permute-start | bytes 393224 | tf_op jit(solution)/shard_map/ppermute | solution.py:315
  12.4 0.0 collective-permute-done.6.refs_1_
  12.4 2.3 %collective-permute-done.5.refs_0_ = f32[104,256]{1,0:T(8,128)S(1)} collective-permute-done((f32[104,256]{1,0:T(8,128)S(1)}, f32[104,256]{1,0:T(8,128)S(1)}, u32[]{:S(2)}, u32[]{:S(2)}) %collective-permute-start.5) | collective-permute-done | bytes 106528 | tf_op jit(solution)/shard_map/ppermute | solution.py:338
  14.7 1.3 %collective-permute-done.3.came_ref = f32[256,256]{1,0:T(8,128)S(1)} collective-permute-done((f32[256,256]{1,0:T(8,128)S(1)}, f32[256,256]{1,0:T(8,128)S(1)}, u32[]{:S(2)}, u32[]{:S(2)}) %collective-permute-start.3) | collective-permute-done | bytes 262176 | tf_op jit(solution)/shard_map/ppermute | solution.py:315
  16.0 0.5 %window.1.refs_0_ = f32[256,256]{1,0:T(8,128)S(1)} custom-call(f32[256,256]{1,0:T(8,128)S(1)} %add.12.held_ref, f32[256,256]{1,0:T(8,128)S(1)} %collective-permute-done.3.came_ref, f32[104,256]{1,0:T(8,128)S(1)} %collective-permute-done.5.refs_0_, f32[104,256]{1,0:T(8,128)S(1)} %collective-permute-done.6.refs_1_), custom_call_target="tpu_custom_call" | custom-call | tf_op jit(solution)/shard_map/window/pallas_call | solution.py:343
  16.6 0.1 collective-permute-start.8
  16.6 0.9 %store_own.1.refs_2_ = f32[4,12,64,64]{3,2,1,0:T(8,128)} custom-call(f32[256,256]{1,0:T(8,128)S(1)} %window.1.refs_0_), custom_call_target="tpu_custom_call" | custom-call | tf_op jit(solution)/shard_map/store_own/pallas_call | solution.py:356
  17.5 0.7 %collective-permute-done.2 = f32[128,256]{1,0:T(8,128)S(1)} collective-permute-done((f32[128,256]{1,0:T(8,128)S(1)}, f32[128,256]{1,0:T(8,128)S(1)}, u32[]{:S(2)}, u32[]{:S(2)}) %collective-permute-start.2) | collective-permute-done | bytes 131104 | tf_op jit(solution)/shard_map/ppermute | solution.py:315
  18.2 0.4 %collective-permute-start.7 = (f32[128,256]{1,0:T(8,128)S(1)}, f32[128,256]{1,0:T(8,128)S(1)}, u32[]{:S(2)}, u32[]{:S(2)}) collective-permute-start(f32[128,256]{1,0:T(8,128)S(1)} %add.15.refs_1_), channel_id=1, source_target_pairs={{0,1},{1,0},{2,3},{3,2},{4,5},{5,4},{6,7},{7,6},{8,9},{9,8},{10,11... | collective-permute-start | bytes 393224 | tf_op jit(solution)/shard_map/ppermute | solution.py:305
  18.7 0.0 collective-permute-done.8.refs_0_
  18.7 1.0 %store_both.1.refs_1_ = f32[4,12,64,64]{3,2,1,0:T(8,128)} custom-call(f32[256,256]{1,0:T(8,128)S(1)} %collective-permute-done.8.refs_0_, f32[128,256]{1,0:T(8,128)S(1)} %add.15.refs_1_, f32[4,12,64,64]{3,2,1,0:T(8,128)} %store_own.1.refs_2_), custom_call_target="tpu_custom_call", output_to_operand_aliasing={{}: (2, {})} | custom-call | tf_op jit(solution)/shard_map/store_both/pallas_call | solution.py:356
  19.7 0.0 collective-permute-done.7.refs_0_
  19.7 0.8 %store_other.1 = f32[4,12,64,64]{3,2,1,0:T(8,128)} custom-call(f32[128,256]{1,0:T(8,128)S(1)} %collective-permute-done.7.refs_0_, f32[4,12,64,64]{3,2,1,0:T(8,128)} %store_both.1.refs_1_), custom_call_target="tpu_custom_call", output_to_operand_aliasing={{}: (1, {})} | custom-call | tf_op jit(solution)/shard_map/store_other/pallas_call | solution.py:356
  (7 shorter events, 0.1 us)
Async XLA Ops:
  2.8 1.9 %collective-permute-start = (f32[256,256]{1,0:T(8,128)S(1)}, f32[256,256]{1,0:T(8,128)S(1)}, u32[]{:S(2)}, u32[]{:S(2)}) collective-permute-start(f32[256,256]{1,0:T(8,128)S(1)} %get-tuple-element.24), channel_id=1, source_target_pairs={{0,1},{1,0},{2,3},{3,2},{4,5},{5,4},{6,7},{7,6},{8,9},{9,8},{10,11... | collective-permute-start | bytes 786440 | tf_op jit(solution)/shard_map/ppermute | solution.py:305
  3.5 2.8 %collective-permute-start.4 = (f32[56,256]{1,0:T(8,128)S(1)}, f32[56,256]{1,0:T(8,128)S(1)}, u32[]{:S(2)}, u32[]{:S(2)}) collective-permute-start(f32[56,256]{1,0:T(8,128)S(1)} %get-tuple-element.28), channel_id=1, source_target_pairs={{0,1},{1,0},{2,3},{3,2},{4,5},{5,4},{6,7},{7,6},{8,9},{9,8},{10,11... | collective-permute-start | bytes 172040 | tf_op jit(solution)/shard_map/ppermute | solution.py:305
  4.7 11.2 %collective-permute-start.3 = (f32[256,256]{1,0:T(8,128)S(1)}, f32[256,256]{1,0:T(8,128)S(1)}, u32[]{:S(2)}, u32[]{:S(2)}) collective-permute-start(f32[256,256]{1,0:T(8,128)S(1)} %add.12.held_ref), channel_id=1, source_target_pairs={{0,3},{1,2},{3,0},{2,1},{4,7},{5,6},{7,4},{6,5},{8,11},{9,10},{11,... | collective-permute-start | bytes 786440 | tf_op jit(solution)/shard_map/ppermute | solution.py:315
  6.3 5.0 %collective-permute-start.1 = (f32[128,256]{1,0:T(8,128)S(1)}, f32[128,256]{1,0:T(8,128)S(1)}, u32[]{:S(2)}, u32[]{:S(2)}) collective-permute-start(f32[128,256]{1,0:T(8,128)S(1)} %get-tuple-element.25), channel_id=1, source_target_pairs={{0,1},{1,0},{2,3},{3,2},{4,5},{5,4},{6,7},{7,6},{8,9},{9,8},{10,11... | collective-permute-start | bytes 393224 | tf_op jit(solution)/shard_map/ppermute | solution.py:305
  6.5 5.9 %collective-permute-start.6 = (f32[104,256]{1,0:T(8,128)S(1)}, f32[104,256]{1,0:T(8,128)S(1)}, u32[]{:S(2)}, u32[]{:S(2)}) collective-permute-start(f32[104,256]{1,0:T(8,128)S(1)} %pad_maximum_fusion), channel_id=1, source_target_pairs={{1,7},{7,1},{2,4},{4,2},{5,11},{11,5},{6,8},{8,6},{9,15},{15,9},{1... | collective-permute-start | bytes 319496 | tf_op jit(solution)/shard_map/ppermute | solution.py:338
  7.8 6.9 %collective-permute-start.5 = (f32[104,256]{1,0:T(8,128)S(1)}, f32[104,256]{1,0:T(8,128)S(1)}, u32[]{:S(2)}, u32[]{:S(2)}) collective-permute-start(f32[104,256]{1,0:T(8,128)S(1)} %pad_maximum_fusion), channel_id=1, source_target_pairs={{1,4},{4,1},{2,7},{7,2},{5,8},{8,5},{6,11},{11,6},{9,12},{12,9},{1... | collective-permute-start | bytes 319496 | tf_op jit(solution)/shard_map/ppermute | solution.py:338
  11.4 6.8 %collective-permute-start.2 = (f32[128,256]{1,0:T(8,128)S(1)}, f32[128,256]{1,0:T(8,128)S(1)}, u32[]{:S(2)}, u32[]{:S(2)}) collective-permute-start(f32[128,256]{1,0:T(8,128)S(1)} %add.13), channel_id=1, source_target_pairs={{0,3},{1,2},{3,0},{2,1},{4,7},{5,6},{7,4},{6,5},{8,11},{9,10},{11,... | collective-permute-start | bytes 393224 | tf_op jit(solution)/shard_map/ppermute | solution.py:315
  16.6 2.1 %collective-permute-start.8 = (f32[256,256]{1,0:T(8,128)S(1)}, f32[256,256]{1,0:T(8,128)S(1)}, u32[]{:S(2)}, u32[]{:S(2)}) collective-permute-start(f32[256,256]{1,0:T(8,128)S(1)} %window.1.refs_0_), channel_id=1, source_target_pairs={{0,1},{1,0},{2,3},{3,2},{4,5},{5,4},{6,7},{7,6},{8,9},{9,8},{10,11... | collective-permute-start | bytes 786440 | tf_op jit(solution)/shard_map/ppermute | solution.py:305
  18.2 1.5 %collective-permute-start.7 = (f32[128,256]{1,0:T(8,128)S(1)}, f32[128,256]{1,0:T(8,128)S(1)}, u32[]{:S(2)}, u32[]{:S(2)}) collective-permute-start(f32[128,256]{1,0:T(8,128)S(1)} %add.15.refs_1_), channel_id=1, source_target_pairs={{0,1},{1,0},{2,3},{3,2},{4,5},{5,4},{6,7},{7,6},{8,9},{9,8},{10,11... | collective-permute-start | bytes 393224 | tf_op jit(solution)/shard_map/ppermute | solution.py:305
